TPU v7x, 32 devices: a whole 2x2x4 slice. The times are simulated.
32 devices in a mesh: gz: 4 (over y, core), gy: 8 (over z, x).
Axes of the slice: x: 2, y: 2, z: 4, core: 2. Of those that a mesh axis runs over, the one named last changes fastest.
Arguments:
- right_side: float32 [32, 64, 1024], P('gz', 'gy'), may hold values from -5 to 5
- coefficient: float32 [32, 64, 1024], P('gz', 'gy'), may hold values from 0.5 to 4
Outputs:
- correction: float32 [32, 64, 1024], P('gz', 'gy')
- residual: float32 [32, 64, 1024], P('gz', 'gy')
All inputs are finite; a program needn't handle non-finite values.
Results may differ from a plain program's by a relative error of at most 0.0003.
Values sent between devices are 32-bit elements; how exact they have to be, the bound alone decides.
No kernel may reach another device: no remote copies, remote signals or barrier semaphores. Data moves between devices by JAX's collectives and lax.ppermute only.
A program may use at most 64 MiB of HBM per device.

v0:
```python
import jax
import jax.numpy as jnp
from jax import lax
from jax.sharding import PartitionSpec as P

LEVELS = 4


def extended(array, sides, width):
    for axis, dim in sides:
        size, length = (lax.axis_size(axis), array.shape[dim])
        up = [(i, (i + 1) % size) for i in range(size - 1)]
        down = [(j, i) for i, j in up]
        last = lax.slice_in_dim(array, length - width, length, axis=dim)
        initial = lax.slice_in_dim(array, 0, width, axis=dim)
        before = lax.ppermute(last, axis, up)
        after = lax.ppermute(initial, axis, down)
        array = jnp.concatenate([before, array, after], axis=dim)
    return array


def coarsen(field):
    total = field[0::2, 0::2, 0::2] + field[0::2, 0::2, 1::2]
    total = total + field[0::2, 1::2, 0::2] + field[0::2, 1::2, 1::2]
    total = total + field[1::2, 0::2, 0::2] + field[1::2, 0::2, 1::2]
    total = total + field[1::2, 1::2, 0::2] + field[1::2, 1::2, 1::2]
    return total * 0.125


def prolong(field):
    return jnp.repeat(jnp.repeat(jnp.repeat(field, 2, axis=0), 2, axis=1), 2, axis=2)


def face_terms(kpad):
    center = kpad[1:-1, 1:-1, 1:-1]
    z_minus = 0.5 * (center + kpad[:-2, 1:-1, 1:-1])
    z_plus = 0.5 * (center + kpad[2:, 1:-1, 1:-1])
    y_minus = 0.5 * (center + kpad[1:-1, :-2, 1:-1])
    y_plus = 0.5 * (center + kpad[1:-1, 2:, 1:-1])
    x_minus = 0.5 * (center + kpad[1:-1, 1:-1, :-2])
    x_plus = 0.5 * (center + kpad[1:-1, 1:-1, 2:])
    total = z_minus + z_plus + y_minus + y_plus + x_minus + x_plus
    return ((z_minus, z_plus, y_minus, y_plus, x_minus, x_plus), total)


def neighbour_sum(weights, upad):
    z_minus, z_plus, y_minus, y_plus, x_minus, x_plus = weights
    acc = z_minus * upad[:-2, 1:-1, 1:-1] + z_plus * upad[2:, 1:-1, 1:-1]
    acc = acc + y_minus * upad[1:-1, :-2, 1:-1] + y_plus * upad[1:-1, 2:, 1:-1]
    acc = acc + x_minus * upad[1:-1, 1:-1, :-2] + x_plus * upad[1:-1, 1:-1, 2:]
    return acc


def extend(field, layout):
    if layout == "column":
        wider = extended(field, (("gy", 1),), 1)
        wider = jnp.pad(wider, ((1, 1), (0, 0), (0, 0)))
    else:
        wider = extended(field, (("gz", 0), ("gy", 1)), 1)
    return jnp.pad(wider, ((0, 0), (0, 0), (1, 1)))


def region_masks(shape, z_start, y_start):
    zpos = lax.broadcasted_iota(jnp.int32, shape, 0) + z_start
    ypos = lax.broadcasted_iota(jnp.int32, shape, 1) + y_start
    xpos = lax.broadcasted_iota(jnp.int32, shape, 2)
    return (zpos + ypos + xpos + 4) % 2


def cycle(rhs, conduct, level, layout, z_start, y_start, z_total, y_total):
    scale = 4.0**level
    weights, total = face_terms(extend(conduct, layout))
    parity = region_masks(rhs.shape, z_start, y_start)
    first = parity == 0
    second = parity == 1

    def relax(field, colour):
        fresh = (scale * rhs + neighbour_sum(weights, extend(field, layout))) / total
        return jnp.where(colour, fresh, field)

    def smooth(field, sweeps):
        for sweep in range(sweeps):
            for colour in (first, second):
                field = relax(field, colour)
        return field

    def remainder(field):
        return rhs - (total * field - neighbour_sum(weights, extend(field, layout))) / scale

    field = jnp.zeros(rhs.shape, jnp.float32)
    if level == LEVELS - 1:
        return (smooth(field, 12), None)
    field = smooth(field, 2)
    rhs_next = coarsen(remainder(field))
    conduct_next = coarsen(conduct)
    joined = layout == "split" and level == 1
    if joined:
        local_depth = rhs_next.shape[0]
        rhs_next, conduct_next = (
            lax.all_gather(rhs_next, "gz", axis=0, tiled=True),
            lax.all_gather(conduct_next, "gz", axis=0, tiled=True),
        )
        error, unused = cycle(
            rhs_next, conduct_next, level + 1, "column", 0, y_start // 2, z_total // 2, y_total // 2
        )
        error = lax.dynamic_slice_in_dim(error, lax.axis_index("gz") * local_depth, local_depth, 0)
    else:
        error, unused = cycle(
            rhs_next,
            conduct_next,
            level + 1,
            layout,
            z_start // 2,
            y_start // 2,
            z_total // 2,
            y_total // 2,
        )
    field = field + prolong(error)
    field = smooth(field, 2)
    return (field, remainder(field))


def on_device(right_side, coefficient):
    depth, rows, width = right_side.shape
    z_start = lax.axis_index("gz") * depth
    y_start = lax.axis_index("gy") * rows
    z_total = depth * lax.axis_size("gz")
    y_total = rows * lax.axis_size("gy")
    correction, residual = cycle(
        right_side, coefficient, 0, "split", z_start, y_start, z_total, y_total
    )
    return (correction, residual)


def solution(mesh):
    placed = (P("gz", "gy", None), P("gz", "gy", None))
    return jax.shard_map(
        on_device,
        mesh=mesh,
        in_specs=placed,
        out_specs=(P("gz", "gy", None), P("gz", "gy", None)),
        check_vma=False,
    )
```

profile of v0, /device:TPU:0, one launch (start us, length us, event | category | flops | bytes accessed | tf_op | source)
XLA Modules:
  0.0 686.8 jit_solution(16813393005840216807)
XLA Ops:
  37.9 6.9 %collective-permute-start.25 = (f32[1,4,512]{2,1,0:T(4,128)S(1)}, f32[1,4,512]{2,1,0:T(4,128)S(1)}, u32[]{:S(2)}, u32[]{:S(2)}) collective-permute-start(f32[1,4,512]{2,1,0:T(4,128)S(1)} %broadcast.402), channel_id=1, source_target_pairs={{0,8},{8,16},{16,24},{1,9},{9,17},{17,25},{2,10},{10,18},{18,26},{... | collective-permute-start | bytes 24584 | tf_op jit(solution)/shard_map/ppermute | solution.py:16
  164.9 5.8 all_gather.7
  178.5 6.1 collective-permute-start.48
  237.1 6.4 all_gather.6
  252.8 6.1 collective-permute-start.54
  288.7 5.7 collective-permute-start.64
  297.1 5.7 collective-permute-start.66
  305.5 5.7 collective-permute-start.68
  313.9 5.7 collective-permute-start.70
  322.3 5.7 collective-permute-start.72
  330.8 5.7 collective-permute-start.74
  339.2 5.7 collective-permute-start.76
  347.6 5.7 collective-permute-start.78
  356.0 5.7 collective-permute-start.80
  364.4 5.7 collective-permute-start.82
  372.8 5.7 collective-permute-start.84
  381.2 5.7 collective-permute-start.86
  389.6 5.7 collective-permute-start.88
  398.1 5.7 collective-permute-start.90
  406.5 5.7 collective-permute-start.92
  414.9 5.7 collective-permute-start.94
  423.3 5.7 collective-permute-start.96
  431.7 5.7 collective-permute-start.98
  440.1 5.7 collective-permute-start.100
  448.5 5.7 collective-permute-start.102
  457.0 5.7 collective-permute-start.104
  465.4 5.7 collective-permute-start.106
  473.8 5.7 collective-permute-start.108
  482.5 5.7 collective-permute-start.110
  491.1 5.7 collective-permute-start.112
  499.7 5.7 collective-permute-start.114
  508.3 5.7 collective-permute-start.116
  (569 shorter events, 496.6 us)
Async XLA Ops:
  0.7 19.4 %collective-permute-start.3 = (f32[1,8,1024]{2,1,0:T(8,128)S(1)}, f32[1,8,1024]{2,1,0:T(8,128)S(1)}, u32[]{:S(2)}, u32[]{:S(2)}) collective-permute-start(f32[1,8,1024]{2,1,0:T(8,128)S(1)} %broadcast.399), channel_id=1, source_target_pairs={{8,0},{16,8},{24,16},{9,1},{17,9},{25,17},{10,2},{18,10},{26,18},{... | collective-permute-start | bytes 98312 | tf_op jit(solution)/shard_map/ppermute | solution.py:17
  2.1 18.0 %collective-permute-start.1 = (f32[1,8,1024]{2,1,0:T(8,128)S(1)}, f32[1,8,1024]{2,1,0:T(8,128)S(1)}, u32[]{:S(2)}, u32[]{:S(2)}) collective-permute-start(f32[1,8,1024]{2,1,0:T(8,128)S(1)} %broadcast.399), channel_id=1, source_target_pairs={{0,8},{8,16},{16,24},{1,9},{9,17},{17,25},{2,10},{10,18},{18,26},{... | collective-permute-start | bytes 98312 | tf_op jit(solution)/shard_map/ppermute | solution.py:16
  14.2 11.7 %collective-permute-start.6 = (f32[10,1,1024]{2,1,0:T(1,128)S(1)}, f32[10,1,1024]{2,1,0:T(1,128)S(1)}, u32[]{:S(2)}, u32[]{:S(2)}) collective-permute-start(f32[10,1,1024]{2,1,0:T(1,128)S(1)} %get-tuple-element.57), channel_id=1, source_target_pairs={{1,0},{2,1},{3,2},{4,3},{5,4},{6,5},{7,6},{9,8},{10,9},{11,10},{12... | collective-permute-start | bytes 122888 | tf_op jit(solution)/shard_map/ppermute | solution.py:17
  15.5 10.4 %collective-permute-start.4 = (f32[10,1,1024]{2,1,0:T(1,128)S(1)}, f32[10,1,1024]{2,1,0:T(1,128)S(1)}, u32[]{:S(2)}, u32[]{:S(2)}) collective-permute-start(f32[10,1,1024]{2,1,0:T(1,128)S(1)} %get-tuple-element.58), channel_id=1, source_target_pairs={{0,1},{1,2},{2,3},{3,4},{4,5},{5,6},{6,7},{8,9},{9,10},{10,11},{11... | collective-permute-start | bytes 122888 | tf_op jit(solution)/shard_map/ppermute | solution.py:16
  33.3 23.4 %collective-permute-start.8 = (f32[1,8,1024]{2,1,0:T(8,128)S(1)}, f32[1,8,1024]{2,1,0:T(8,128)S(1)}, u32[]{:S(2)}, u32[]{:S(2)}) collective-permute-start(f32[1,8,1024]{2,1,0:T(8,128)S(1)} %get-tuple-element.77), channel_id=1, source_target_pairs={{0,8},{8,16},{16,24},{1,9},{9,17},{17,25},{2,10},{10,18},{18,26},{... | collective-permute-start | bytes 98312 | tf_op jit(solution)/shard_map/ppermute | solution.py:16
  35.3 21.4 %collective-permute-start.9 = (f32[1,8,1024]{2,1,0:T(8,128)S(1)}, f32[1,8,1024]{2,1,0:T(8,128)S(1)}, u32[]{:S(2)}, u32[]{:S(2)}) collective-permute-start(f32[1,8,1024]{2,1,0:T(8,128)S(1)} %get-tuple-element.78), channel_id=1, source_target_pairs={{8,0},{16,8},{24,16},{9,1},{17,9},{25,17},{10,2},{18,10},{26,18},{... | collective-permute-start | bytes 98312 | tf_op jit(solution)/shard_map/ppermute | solution.py:17
  36.6 51.6 %collective-permute-start.27 = (f32[1,4,512]{2,1,0:T(4,128)S(1)}, f32[1,4,512]{2,1,0:T(4,128)S(1)}, u32[]{:S(2)}, u32[]{:S(2)}) collective-permute-start(f32[1,4,512]{2,1,0:T(4,128)S(1)} %broadcast.402), channel_id=1, source_target_pairs={{8,0},{16,8},{24,16},{9,1},{17,9},{25,17},{10,2},{18,10},{26,18},{... | collective-permute-start | bytes 24584 | tf_op jit(solution)/shard_map/ppermute | solution.py:17
  37.9 51.6 %collective-permute-start.25 = (f32[1,4,512]{2,1,0:T(4,128)S(1)}, f32[1,4,512]{2,1,0:T(4,128)S(1)}, u32[]{:S(2)}, u32[]{:S(2)}) collective-permute-start(f32[1,4,512]{2,1,0:T(4,128)S(1)} %broadcast.402), channel_id=1, source_target_pairs={{0,8},{8,16},{16,24},{1,9},{9,17},{17,25},{2,10},{10,18},{18,26},{... | collective-permute-start | bytes 24584 | tf_op jit(solution)/shard_map/ppermute | solution.py:16
  70.6 28.6 %collective-permute-start.26 = (f32[1,4,512]{2,1,0:T(4,128)S(1)}, f32[1,4,512]{2,1,0:T(4,128)S(1)}, u32[]{:S(2)}, u32[]{:S(2)}) collective-permute-start(f32[1,4,512]{2,1,0:T(4,128)S(1)} %get-tuple-element.120), channel_id=1, source_target_pairs={{8,0},{16,8},{24,16},{9,1},{17,9},{25,17},{10,2},{18,10},{26,18},{... | collective-permute-start | bytes 24584 | tf_op jit(solution)/shard_map/ppermute | solution.py:17
  79.9 20.7 %collective-permute-start.24 = (f32[1,4,512]{2,1,0:T(4,128)S(1)}, f32[1,4,512]{2,1,0:T(4,128)S(1)}, u32[]{:S(2)}, u32[]{:S(2)}) collective-permute-start(f32[1,4,512]{2,1,0:T(4,128)S(1)} %get-tuple-element.121), channel_id=1, source_target_pairs={{0,8},{8,16},{16,24},{1,9},{9,17},{17,25},{2,10},{10,18},{18,26},{... | collective-permute-start | bytes 24584 | tf_op jit(solution)/shard_map/ppermute | solution.py:16
  85.1 8.2 %collective-permute-start.16 = (f32[1,8,1024]{2,1,0:T(8,128)S(1)}, f32[1,8,1024]{2,1,0:T(8,128)S(1)}, u32[]{:S(2)}, u32[]{:S(2)}) collective-permute-start(f32[1,8,1024]{2,1,0:T(8,128)S(1)} %get-tuple-element.73), channel_id=1, source_target_pairs={{0,8},{8,16},{16,24},{1,9},{9,17},{17,25},{2,10},{10,18},{18,26},{... | collective-permute-start | bytes 98312 | tf_op jit(solution)/shard_map/ppermute | solution.py:16
  89.6 33.7 %collective-permute-start.29 = (f32[6,1,512]{2,1,0:T(1,128)S(1)}, f32[6,1,512]{2,1,0:T(1,128)S(1)}, u32[]{:S(2)}, u32[]{:S(2)}) collective-permute-start(f32[6,1,512]{2,1,0:T(1,128)S(1)} %get-tuple-element.99), channel_id=1, source_target_pairs={{0,1},{1,2},{2,3},{3,4},{4,5},{5,6},{6,7},{8,9},{9,10},{10,11},{11... | collective-permute-start | bytes 36872 | tf_op jit(solution)/shard_map/ppermute | solution.py:16
  93.3 29.9 %collective-permute-start.31 = (f32[6,1,512]{2,1,0:T(1,128)S(1)}, f32[6,1,512]{2,1,0:T(1,128)S(1)}, u32[]{:S(2)}, u32[]{:S(2)}) collective-permute-start(f32[6,1,512]{2,1,0:T(1,128)S(1)} %get-tuple-element.100), channel_id=1, source_target_pairs={{1,0},{2,1},{3,2},{4,3},{5,4},{6,5},{7,6},{9,8},{10,9},{11,10},{12... | collective-permute-start | bytes 36872 | tf_op jit(solution)/shard_map/ppermute | solution.py:17
  99.3 8.3 %collective-permute-start.19 = (f32[10,1,1024]{2,1,0:T(1,128)S(1)}, f32[10,1,1024]{2,1,0:T(1,128)S(1)}, u32[]{:S(2)}, u32[]{:S(2)}) collective-permute-start(f32[10,1,1024]{2,1,0:T(1,128)S(1)} %get-tuple-element.52), channel_id=1, source_target_pairs={{1,0},{2,1},{3,2},{4,3},{5,4},{6,5},{7,6},{9,8},{10,9},{11,10},{12... | collective-permute-start | bytes 122888 | tf_op jit(solution)/shard_map/ppermute | solution.py:17
  100.6 10.8 %collective-permute-start.30 = (f32[6,1,512]{2,1,0:T(1,128)S(1)}, f32[6,1,512]{2,1,0:T(1,128)S(1)}, u32[]{:S(2)}, u32[]{:S(2)}) collective-permute-start(f32[6,1,512]{2,1,0:T(1,128)S(1)} %get-tuple-element.97), channel_id=1, source_target_pairs={{1,0},{2,1},{3,2},{4,3},{5,4},{6,5},{7,6},{9,8},{10,9},{11,10},{12... | collective-permute-start | bytes 36872 | tf_op jit(solution)/shard_map/ppermute | solution.py:17
  101.9 10.8 %collective-permute-start.28 = (f32[6,1,512]{2,1,0:T(1,128)S(1)}, f32[6,1,512]{2,1,0:T(1,128)S(1)}, u32[]{:S(2)}, u32[]{:S(2)}) collective-permute-start(f32[6,1,512]{2,1,0:T(1,128)S(1)} %get-tuple-element.98), channel_id=1, source_target_pairs={{0,1},{1,2},{2,3},{3,4},{4,5},{5,6},{6,7},{8,9},{9,10},{10,11},{11... | collective-permute-start | bytes 36872 | tf_op jit(solution)/shard_map/ppermute | solution.py:16
  147.7 11.4 %collective-permute-start.34 = (f32[6,1,512]{2,1,0:T(1,128)S(1)}, f32[6,1,512]{2,1,0:T(1,128)S(1)}, u32[]{:S(2)}, u32[]{:S(2)}) collective-permute-start(f32[6,1,512]{2,1,0:T(1,128)S(1)} %get-tuple-element.95), channel_id=1, source_target_pairs={{0,1},{1,2},{2,3},{3,4},{4,5},{5,6},{6,7},{8,9},{9,10},{10,11},{11... | collective-permute-start | bytes 36872 | tf_op jit(solution)/shard_map/ppermute | solution.py:16
  153.9 63.9 %collective-permute-start.51 = (f32[8,1,256]{2,0,1:T(8,128)S(1)}, f32[8,1,256]{2,0,1:T(8,128)S(1)}, u32[]{:S(2)}, u32[]{:S(2)}) collective-permute-start(f32[8,1,256]{2,0,1:T(8,128)S(1)} %broadcast.408), channel_id=1, source_target_pairs={{1,0},{2,1},{3,2},{4,3},{5,4},{6,5},{7,6},{9,8},{10,9},{11,10},{12... | collective-permute-start | bytes 24584 | tf_op jit(solution)/shard_map/ppermute | solution.py:17
  159.5 11.2 %collective-permute-start.36 = (f32[1,4,512]{2,1,0:T(4,128)S(1)}, f32[1,4,512]{2,1,0:T(4,128)S(1)}, u32[]{:S(2)}, u32[]{:S(2)}) collective-permute-start(f32[1,4,512]{2,1,0:T(4,128)S(1)} %get-tuple-element.116), channel_id=1, source_target_pairs={{0,8},{8,16},{16,24},{1,9},{9,17},{17,25},{2,10},{10,18},{18,26},{... | collective-permute-start | bytes 24584 | tf_op jit(solution)/shard_map/ppermute | solution.py:16
  170.7 13.9 %collective-permute-start.38 = (f32[6,1,512]{2,1,0:T(1,128)S(1)}, f32[6,1,512]{2,1,0:T(1,128)S(1)}, u32[]{:S(2)}, u32[]{:S(2)}) collective-permute-start(f32[6,1,512]{2,1,0:T(1,128)S(1)} %get-tuple-element.93), channel_id=1, source_target_pairs={{0,1},{1,2},{2,3},{3,4},{4,5},{5,6},{6,7},{8,9},{9,10},{10,11},{11... | collective-permute-start | bytes 36872 | tf_op jit(solution)/shard_map/ppermute | solution.py:16
  175.9 8.8 %collective-permute-start.39 = (f32[6,1,512]{2,1,0:T(1,128)S(1)}, f32[6,1,512]{2,1,0:T(1,128)S(1)}, u32[]{:S(2)}, u32[]{:S(2)}) collective-permute-start(f32[6,1,512]{2,1,0:T(1,128)S(1)} %get-tuple-element.94), channel_id=1, source_target_pairs={{1,0},{2,1},{3,2},{4,3},{5,4},{6,5},{7,6},{9,8},{10,9},{11,10},{12... | collective-permute-start | bytes 36872 | tf_op jit(solution)/shard_map/ppermute | solution.py:17
  177.2 18.3 %collective-permute-start.49 = (f32[8,1,256]{2,0,1:T(8,128)S(1)}, f32[8,1,256]{2,0,1:T(8,128)S(1)}, u32[]{:S(2)}, u32[]{:S(2)}) collective-permute-start(f32[8,1,256]{2,0,1:T(8,128)S(1)} %copy.1640), channel_id=1, source_target_pairs={{1,0},{2,1},{3,2},{4,3},{5,4},{6,5},{7,6},{9,8},{10,9},{11,10},{12... | collective-permute-start | bytes 24584 | tf_op jit(solution)/shard_map/ppermute | solution.py:17
  178.5 21.6 %collective-permute-start.48 = (f32[8,1,256]{2,0,1:T(8,128)S(1)}, f32[8,1,256]{2,0,1:T(8,128)S(1)}, u32[]{:S(2)}, u32[]{:S(2)}) collective-permute-start(f32[8,1,256]{2,0,1:T(8,128)S(1)} %copy.1639), channel_id=1, source_target_pairs={{0,1},{1,2},{2,3},{3,4},{4,5},{5,6},{6,7},{8,9},{9,10},{10,11},{11... | collective-permute-start | bytes 24584 | tf_op jit(solution)/shard_map/ppermute | solution.py:16
  185.0 16.5 %collective-permute-start.40 = (f32[1,4,512]{2,1,0:T(4,128)S(1)}, f32[1,4,512]{2,1,0:T(4,128)S(1)}, u32[]{:S(2)}, u32[]{:S(2)}) collective-permute-start(f32[1,4,512]{2,1,0:T(4,128)S(1)} %get-tuple-element.114), channel_id=1, source_target_pairs={{0,8},{8,16},{16,24},{1,9},{9,17},{17,25},{2,10},{10,18},{18,26},{... | collective-permute-start | bytes 24584 | tf_op jit(solution)/shard_map/ppermute | solution.py:16
  186.7 14.8 %collective-permute-start.41 = (f32[1,4,512]{2,1,0:T(4,128)S(1)}, f32[1,4,512]{2,1,0:T(4,128)S(1)}, u32[]{:S(2)}, u32[]{:S(2)}) collective-permute-start(f32[1,4,512]{2,1,0:T(4,128)S(1)} %get-tuple-element.115), channel_id=1, source_target_pairs={{8,0},{16,8},{24,16},{9,1},{17,9},{25,17},{10,2},{18,10},{26,18},{... | collective-permute-start | bytes 24584 | tf_op jit(solution)/shard_map/ppermute | solution.py:17
  195.6 26.8 %collective-permute-start.50 = (f32[8,1,256]{2,0,1:T(8,128)S(1)}, f32[8,1,256]{2,0,1:T(8,128)S(1)}, u32[]{:S(2)}, u32[]{:S(2)}) collective-permute-start(f32[8,1,256]{2,0,1:T(8,128)S(1)} %broadcast.408), channel_id=1, source_target_pairs={{0,1},{1,2},{2,3},{3,4},{4,5},{5,6},{6,7},{8,9},{9,10},{10,11},{11... | collective-permute-start | bytes 24584 | tf_op jit(solution)/shard_map/ppermute | solution.py:16
  200.1 65.1 %collective-permute-start.63 = (f32[4,1,128]{2,1,0:T(1,128)S(1)}, f32[4,1,128]{2,1,0:T(1,128)S(1)}, u32[]{:S(2)}, u32[]{:S(2)}) collective-permute-start(f32[4,1,128]{2,1,0:T(1,128)S(1)} %broadcast_in_dim.46), channel_id=1, source_target_pairs={{1,0},{2,1},{3,2},{4,3},{5,4},{6,5},{7,6},{9,8},{10,9},{11,10},{12... | collective-permute-start | bytes 6152 | tf_op jit(solution)/shard_map/ppermute | solution.py:17
  212.8 9.5 %collective-permute-start.44 = (f32[1,4,512]{2,1,0:T(4,128)S(1)}, f32[1,4,512]{2,1,0:T(4,128)S(1)}, u32[]{:S(2)}, u32[]{:S(2)}) collective-permute-start(f32[1,4,512]{2,1,0:T(4,128)S(1)} %get-tuple-element.112), channel_id=1, source_target_pairs={{0,8},{8,16},{16,24},{1,9},{9,17},{17,25},{2,10},{10,18},{18,26},{... | collective-permute-start | bytes 24584 | tf_op jit(solution)/shard_map/ppermute | solution.py:16
  217.7 52.3 %collective-permute-start.62 = (f32[4,1,128]{2,1,0:T(1,128)S(1)}, f32[4,1,128]{2,1,0:T(1,128)S(1)}, u32[]{:S(2)}, u32[]{:S(2)}) collective-permute-start(f32[4,1,128]{2,1,0:T(1,128)S(1)} %broadcast_in_dim.46), channel_id=1, source_target_pairs={{0,1},{1,2},{2,3},{3,4},{4,5},{5,6},{6,7},{8,9},{9,10},{10,11},{11... | collective-permute-start | bytes 6152 | tf_op jit(solution)/shard_map/ppermute | solution.py:16
  249.9 28.3 %collective-permute-start.61 = (f32[4,1,128]{2,1,0:T(1,128)S(1)}, f32[4,1,128]{2,1,0:T(1,128)S(1)}, u32[]{:S(2)}, u32[]{:S(2)}) collective-permute-start(f32[4,1,128]{2,1,0:T(1,128)S(1)} %add_multiply_fusion.5), channel_id=1, source_target_pairs={{1,0},{2,1},{3,2},{4,3},{5,4},{6,5},{7,6},{9,8},{10,9},{11,10},{12... | collective-permute-start | bytes 6152 | tf_op jit(solution)/shard_map/ppermute | solution.py:17
  252.8 11.0 %collective-permute-start.54 = (f32[8,1,256]{2,0,1:T(8,128)S(1)}, f32[8,1,256]{2,0,1:T(8,128)S(1)}, u32[]{:S(2)}, u32[]{:S(2)}) collective-permute-start(f32[8,1,256]{2,0,1:T(8,128)S(1)} %copy.1655), channel_id=1, source_target_pairs={{0,1},{1,2},{2,3},{3,4},{4,5},{5,6},{6,7},{8,9},{9,10},{10,11},{11... | collective-permute-start | bytes 24584 | tf_op jit(solution)/shard_map/ppermute | solution.py:16
  258.9 19.3 %collective-permute-start.60 = (f32[4,1,128]{2,1,0:T(1,128)S(1)}, f32[4,1,128]{2,1,0:T(1,128)S(1)}, u32[]{:S(2)}, u32[]{:S(2)}) collective-permute-start(f32[4,1,128]{2,1,0:T(1,128)S(1)} %add_multiply_fusion.5), channel_id=1, source_target_pairs={{0,1},{1,2},{2,3},{3,4},{4,5},{5,6},{6,7},{8,9},{9,10},{10,11},{11... | collective-permute-start | bytes 6152 | tf_op jit(solution)/shard_map/ppermute | solution.py:16
  (125 other events, 855.1 us)
where the time goes:
time: 699 us; the launch traced here: 687 us
  starting transfers between devices  454 us (65%)
  waiting for transfers between devices  135 us (19%)
  local copies, waits for them, and re-layouts  60.5 us (9%)
  other arithmetic  19.6 us (3%)
  blocking collectives  12.2 us (2%)
    ppermute x77, starting transfers between devices, extended(): before = lax.ppermute(last, axis, up)  354 us
    ppermute x77, starting transfers between devices, extended(): after = lax.ppermute(initial, axis, down)  100 us
    ppermute x77, waiting for transfers between devices, extended(): after = lax.ppermute(initial, axis, down)  94.8 us
    ppermute x77, waiting for transfers between devices, extended(): before = lax.ppermute(last, axis, up)  40.7 us
  transfers between devices with their start and end apart: 154, of which 68 were waited for; matrix products, arithmetic and copies ran while one was open for 5% of the time, Pallas kernels for 0%

commit v1 on v0

--- a/solution.py
+++ b/solution.py
@@ -1,9 +1,646 @@
 import jax
 import jax.numpy as jnp
 from jax import lax
+from jax.experimental import pallas as pl
+from jax.experimental.pallas import tpu as pltpu
 from jax.sharding import PartitionSpec as P
 
+LANES = 128
+LINES = 18
 LEVELS = 4
+PAD = 5
+F32 = jnp.float32
+WHOLE_COARSE_CELLS = 1 << 19
+
+
+def call(body, micros, outs, scratch, *args, specs=None):
+    vmem = pl.BlockSpec(memory_space=pltpu.VMEM)
+    return pl.pallas_call(
+        body,
+        out_shape=[jax.ShapeDtypeStruct(s, F32) for s in outs],
+        in_specs=specs or [vmem] * len(args),
+        out_specs=[vmem] * len(outs),
+        scratch_shapes=[pltpu.VMEM(s, F32) for s in scratch],
+        cost_estimate=pl.CostEstimate(flops=0, transcendentals=0, bytes_accessed=micros * 3_000_000),
+        compiler_params=pltpu.CompilerParams(vmem_limit_bytes=56 << 20),
+    )(*args)
+
+
+def iota(axis, rows=8):
+    return lax.broadcasted_iota(jnp.int32, (rows, LANES), axis)
+
+
+def barrel(arrays, block):
+    for bit in (1, 2, 4):
+        high = (block & bit) != 0
+        arrays = [jnp.where(high, arrays[(j + bit) % 8], arrays[j]) for j in range(8)]
+    return arrays
+
+
+def lane_gather(array, index):
+    return jnp.take_along_axis(array, index, axis=1, mode="promise_in_bounds")
+
+
+def split_lanes(tiles):
+    lane = iota(1)
+    block = lane // 16
+    parts = [lane_gather(tiles[t], 8 * (lane % 16) + (block - t) % 8) for t in range(8)]
+    mixed = barrel(parts, block)
+    return [pltpu.roll(mixed[-s % 8], (-16 * s) % LANES, axis=1) for s in range(8)]
+
+
+def join_lanes(arrays):
+    lane = iota(1)
+    block = lane // 16
+    moved = [pltpu.roll(arrays[s], (16 * s) % LANES, axis=1) for s in range(8)]
+    mixed = barrel(moved, block)
+    return [lane_gather(mixed[-t % 8], 16 * ((lane % 8 + t) % 8) + lane // 8) for t in range(8)]
+
+
+def put_coarse(message, row, s, value):
+    for z in range(4):
+        e, c = z % 2, (s + z + row) % 2
+        message[(c * 2 + e) * 2 + s // 2, 2 * row + z // 2, :] = value[z]
+
+
+REACH = ((0, 0, 4), (0, 1, 3), (1, 0, 4), (1, 1, 5))
+YFACE = [(a, c, y, n) for a, c, n in REACH for y in range(n)]
+ZFACE = sorted(((a, c, d) for a, c, n in REACH for d in range(1, n + 1)), key=lambda r: r[2] - REACH[2 * r[0] + r[1]][2])
+CORNER = {1: (12, 0, 12), 2: (8, 16, 8), 3: (4, 12, 4), 4: (1, 24, 4)}
+CORNER_ROWS = 28
+
+
+def own_sides():
+    return [lax.rem(lax.axis_index(axis), 2) == 0 for axis in ("gz", "gy")]
+
+
+def halo_cell(side, distance):
+    z = 7 + distance if side == 0 else -distance
+    return z % 2, (z // 2) % 8
+
+
+def pick(flag, a, b):
+    return jnp.where(flag, a, b), jnp.where(flag, b, a)
+
+
+def pack_kernel(f_ref, k_ref, local, ya, yb, za, zb, coarse, natural):
+    zup, yup = own_sides()
+    for a, ref in enumerate((f_ref, k_ref)):
+        for z in range(8):
+            arrays = split_lanes([ref[z, :, t * LANES : (t + 1) * LANES] for t in range(8)])
+            for s in range(8):
+                natural[a, s, 8 * z : 8 * z + 8, :] = arrays[s]
+    for a in range(2):
+        for c in range(2):
+            for y in range(8):
+                for e in range(2):
+                    q = (e + y + c) % 2
+                    for s in range(4):
+                        local[a, c, y, e, s] = natural[a, 2 * s + q, pl.ds(y + 8 * e, 4, stride=16), :]
+    for i, (a, c, y, n) in enumerate(YFACE):
+        first, second = pick(yup, y + 8 - n, y)
+        ya[i] = local[a, c, first]
+        yb[i] = local[a, c, second]
+
+    def faces(y, carry):
+        for i, (a, c, d) in enumerate(ZFACE):
+            high, low = 8 - d, d - 1
+            for s in range(4):
+                up = local[a, c, y, high % 2, s, high // 2 : high // 2 + 1]
+                down = local[a, c, y, low % 2, s, low // 2 : low // 2 + 1]
+                za[y, s, i : i + 1], zb[y, s, i : i + 1] = pick(zup, up, down)
+        return carry
+
+    lax.fori_loop(0, 8, faces, 0)
+    for row in range(4):
+        for s in range(4):
+            total = None
+            for c in range(2):
+                for y in (2 * row, 2 * row + 1):
+                    pair = local[1, c, y, 0, s] + local[1, c, y, 1, s]
+                    total = pair if total is None else total + pair
+            put_coarse(coarse, row, s, total * 0.125)
+
+
+def relay_kernel(za, zb, ca, cb):
+    zabove, yup = own_sides()
+    for target, up in ((ca, yup), (cb, jnp.logical_not(yup))):
+        for d, (_, at, rows) in CORNER.items():
+            y = jnp.where(up, 8 - d, d - 1)
+            for s in range(4):
+                parts = pick(zabove, za[y, s, 0:rows], zb[y, s, 0:rows])
+                for side in range(2):
+                    base = (4 * side + s) * CORNER_ROWS + at
+                    target[base : base + rows, :] = parts[side]
+
+
+def neighbours(ref, line, e, s, q, groups, edge=None, first=None, last=None):
+    rows = ref.shape[-2]
+    lane = iota(1, rows)
+    same = ref[line, e, s]
+    if q == 0 and s == 0:
+        other = jnp.where(lane == 0, 0.0, pltpu.roll(ref[line, e, groups - 1], 1, axis=1))
+    elif q == 1 and s == groups - 1:
+        other = jnp.where(lane == LANES - 1, 0.0, pltpu.roll(ref[line, e, 0], LANES - 1, axis=1))
+    else:
+        other = ref[line, e, s + (1 if q else -1)]
+    zsame = ref[line, 1 - e, s]
+    zother = pltpu.roll(zsame, 1 if e == 0 else rows - 1, axis=0)
+    if edge is not None:
+        zother = edge(zother, line, e, s)
+    return (same + other) + (zsame + zother) + (ref[line - 1, e, s] + ref[line + 1, e, s])
+
+
+def closed(zother, line, e, s):
+    rows = zother.shape[0]
+    return jnp.where(iota(0, rows) == (0 if e == 0 else rows - 1), 0.0, zother)
+
+
+def over_lines(low, high, offset, visit, lines=4):
+    steps, rest = divmod(high - low + 1, lines)
+
+    def step(i, carry):
+        for j in range(lines):
+            visit(low + offset + j + lines * i, (low + j) % 2)
+        return carry
+
+    lax.fori_loop(0, steps, step, 0)
+    for y in range(high + 1 - rest, high + 1):
+        visit(y + offset, y % 2)
+
+
+def diagonal(k, kother, line, e, s, q, groups, edge=None):
+    centre = k[line, e, s]
+    return centre, 6.0 * centre + neighbours(kother, line, e, s, q, groups, edge)
+
+
+def down_kernel(
+    local, ya, yb, za, zb, ca, cb,
+    k, g, fs, half, ub, kx, zc, zd, coarse,
+    f, ur, vr, vb,
+):
+    zabove, yabove = own_sides()
+    zup = zabove
+    blank = jnp.zeros((8, LANES), F32)
+    for c in range(2):
+        for line in (*range(PAD), *range(PAD + 8, LINES)):
+            for e in range(2):
+                for s in range(4):
+                    k[c, line, e, s] = blank
+                    f[c, line, e, s] = blank
+    both = (f, k)
+
+    def assemble(y, carry):
+        for e in range(2):
+            for s in range(4):
+                f[1, PAD + y, e, s] = blank
+                for a in range(2):
+                    for c in range(2):
+                        both[a][c, PAD + y, e, s, 0:4] = local[a, c, y, e, s]
+        for s in range(4):
+            for side, part in enumerate(pick(zabove, za[y, s], zb[y, s])):
+                for i, (a, c, d) in enumerate(ZFACE):
+                    e, row = halo_cell(side, d)
+                    if d == 5:
+                        kx[side, y, s : s + 1] = part[i : i + 1]
+                    else:
+                        both[a][c, PAD + y, e, s, row : row + 1] = part[i : i + 1]
+        return carry
+
+    lax.fori_loop(0, 8, assemble, 0)
+    for i, (a, c, y, n) in enumerate(YFACE):
+        first, second = pick(yabove, PAD + y + 8, PAD + y - n)
+        for e in range(2):
+            for s in range(4):
+                both[a][c, first, e, s, 0:4] = ya[i, e, s]
+                both[a][c, second, e, s, 0:4] = yb[i, e, s]
+    for d, (count, at, _) in CORNER.items():
+        for message, line in zip((ca, cb), pick(yabove, PAD + 7 + d, PAD - d)):
+            for side in range(2):
+                for i, (a, c, dz) in enumerate(ZFACE[:count]):
+                    e, row = halo_cell(side, dz)
+                    for s in range(4):
+                        base = (4 * side + s) * CORNER_ROWS + at + i
+                        both[a][c, line, e, s, row : row + 1] = message[base : base + 1, :]
+
+    rows = iota(0)
+
+    def far(zother, line, e, s):
+        beyond = kx[1 - e, line - PAD, s : s + 1]
+        return jnp.where(rows == (6 if e == 0 else 5), jnp.broadcast_to(beyond, (8, LANES)), zother)
+
+    def prepare(c, line, parity, edge, keep):
+        for e in range(2):
+            q = (e + parity + c) % 2
+            for s in range(4):
+                centre, total = diagonal(k.at[c], k.at[1 - c], line, e, s, q, 4, edge)
+                inside = centre != 0.0
+                scale = jnp.where(inside, 1.0 / jnp.where(inside, total, 1.0), 0.0)
+                start = 2.0 * f[c, line, e, s] * scale
+                g[c, line, e, s] = scale
+                fs[c, line, e, s] = start
+                if keep:
+                    half[line - PAD, e, s] = 0.5 * total
+                if c == 0:
+                    ur[line, e, s] = start
+                    vr[line, e, s] = centre * start
+
+    over_lines(-4, -1, PAD, lambda line, parity: prepare(0, line, parity, None, False))
+    over_lines(8, 11, PAD, lambda line, parity: prepare(0, line, parity, None, False))
+    over_lines(0, 7, PAD, lambda line, parity: prepare(0, line, parity, far, True))
+    over_lines(-3, 10, PAD, lambda line, parity: prepare(1, line, parity, None, False))
+
+    def relax(c, low, high):
+        sweep(c, low, high, k, g, fs, (ur, ub), (vr, vb))
+
+    relax(1, -3, 10)
+    relax(0, -2, 9)
+    relax(1, -1, 8)
+
+    for row in range(4):
+        for s in range(4):
+            total = None
+            for y in (2 * row, 2 * row + 1):
+                for e in range(2):
+                    line = PAD + y
+                    value = red_residual(line, y % 2, e, s, k, g, fs, half, ur, ub, vb)
+                    total = value if total is None else total + value
+            put_coarse(coarse, row, s, total * 0.125)
+
+    for y in range(8):
+        for s in range(4):
+            for d in range(1, 6):
+                at, high, low = (4 * y + s) * 5 + d - 1, 8 - d, d - 1
+                up = ub[PAD + y, high % 2, s, high // 2 : high // 2 + 1]
+                down = ub[PAD + y, low % 2, s, low // 2 : low // 2 + 1]
+                zc[at : at + 1, :], zd[at : at + 1, :] = pick(zup, up, down)
+
+
+def widen_kernel(ub, zc, zd, wide, yc, yd):
+    zabove, yup = own_sides()
+    for y in range(8):
+        for s in range(4):
+            at = (4 * y + s) * 5
+            for e in range(2):
+                wide[y, e, s, 0:4] = ub[PAD + y, e, s, 0:4]
+            for side, part in enumerate(pick(zabove, zc[at : at + 4, :], zd[at : at + 4, :])):
+                for d in range(1, 5):
+                    e, row = halo_cell(side, d)
+                    wide[y, e, s, row : row + 1] = part[d - 1 : d]
+    first, second = pick(yup, 3, 0)
+    for i in range(5):
+        yc[i] = wide[first + i]
+        yd[i] = wide[second + i]
+
+
+def sweep(c, low, high, k, g, fs, u, v, edges=(None, None)):
+    def visit(line, parity):
+        for e in range(2):
+            q = (e + parity + c) % 2
+            for s in range(4):
+                near = neighbours(u[1 - c], line, e, s, q, 4, edges[0])
+                flow = neighbours(v[1 - c], line, e, s, q, 4, edges[1])
+                centre = k[c, line, e, s]
+                value = fs[c, line, e, s] + g[c, line, e, s] * (centre * near + flow)
+                u[c][line, e, s] = value
+                v[c][line, e, s] = centre * value
+
+    over_lines(low, high, PAD, visit)
+
+
+def red_residual(line, parity, e, s, k, g, fs, half, ur, ub, vb):
+    q = (e + parity) % 2
+    near = neighbours(ub, line, e, s, q, 4)
+    flow = neighbours(vb, line, e, s, q, 4)
+    fresh = fs[0, line, e, s] + g[0, line, e, s] * (k[0, line, e, s] * near + flow)
+    return half[line - PAD, e, s] * (fresh - ur[line, e, s])
+
+
+def up_kernel(
+    k, g, fs, half, wide, kx, yc, yd, zc, zd, error, errorx,
+    correction, residual,
+    ub, ur, vb, vr, ux, vx, natural,
+):
+    zabove, yabove = own_sides()
+    ub[PAD : PAD + 8] = wide[...]
+    first, second = pick(yabove, PAD + 8, 0)
+    for i in range(5):
+        ub[first + i] = yc[i]
+        ub[second + i] = yd[i]
+    for y in range(8):
+        for s in range(4):
+            at = (4 * y + s) * 5 + 4
+            for side, part in enumerate(pick(zabove, zc[at : at + 1, :], zd[at : at + 1, :])):
+                beyond = kx[side, y, s : s + 1]
+                value = part + errorx[side, y // 2, s : s + 1]
+                value = jnp.where(beyond != 0.0, value, 0.0)
+                ux[side, y, s : s + 1] = value
+                vx[side, y, s : s + 1] = beyond * value
+
+    def add(line, parity):
+        for e in range(2):
+            for s in range(4):
+                centre = k[1, line, e, s]
+                value = ub[line, e, s] + error[(line + 1) // 2, s]
+                value = jnp.where(centre != 0.0, value, 0.0)
+                ub[line, e, s] = value
+                vb[line, e, s] = centre * value
+
+    over_lines(-5, 12, PAD, add)
+
+    rows = iota(0)
+
+    def far(ref):
+        def edge(zother, line, e, s):
+            beyond = ref[1 - e, line - PAD, s : s + 1]
+            return jnp.where(rows == (6 if e == 0 else 5), jnp.broadcast_to(beyond, (8, LANES)), zother)
+
+        return edge
+
+    u, v = (ur, ub), (vr, vb)
+    sweep(0, -4, -1, k, g, fs, u, v)
+    sweep(0, 8, 11, k, g, fs, u, v)
+    sweep(0, 0, 7, k, g, fs, u, v, (far(ux), far(vx)))
+    sweep(1, -3, 10, k, g, fs, u, v)
+    sweep(0, -2, 9, k, g, fs, u, v)
+    sweep(1, -1, 8, k, g, fs, u, v)
+
+    quiet = jnp.zeros((4, LANES), F32)
+    for y in range(8):
+        for e in range(2):
+            at = pl.ds(y + 8 * e, 4, stride=16)
+            q = (e + y) % 2
+            for s in range(4):
+                value = red_residual(PAD + y, y % 2, e, s, k, g, fs, half, ur, ub, vb)
+                natural[1, 2 * s + q, at, :] = value[0:4]
+                natural[1, 2 * s + 1 - q, at, :] = quiet
+                natural[0, 2 * s + q, at, :] = ur[PAD + y, e, s, 0:4]
+                natural[0, 2 * s + 1 - q, at, :] = ub[PAD + y, e, s, 0:4]
+    for a, out in enumerate((correction, residual)):
+        for z in range(8):
+            tiles = join_lanes([natural[a, s, 8 * z : 8 * z + 8, :] for s in range(8)])
+            for t in range(8):
+                out[z, :, t * LANES : (t + 1) * LANES] = tiles[t]
+
+
+def shifted(value, step, axis):
+    size = value.shape[axis]
+    where = iota(axis, value.shape[0])
+    moved = pltpu.roll(value, -step % size, axis=axis)
+    return jnp.where((where >= size - step) if step > 0 else (where < -step), 0.0, moved)
+
+
+def coarse_kernel(nz, ny):
+    height, depth = 4 * ny, 2 * nz
+    height2, height3 = height // 2, height // 4
+
+    def body(
+        fmine, ftheirs, kmine, ktheirs, error, errorx,
+        f, k, g, fs, half, ur, ub, vr, vb, f2, k2, fc, kc, gc, sc, uc, vc, hc, w3, f3,
+    ):
+        u, v = (ur, ub), (vr, vb)
+        zplace, yplace = lax.axis_index("gz"), lax.axis_index("gy")
+        swaps = swap_steps(nz, ny)[:-1]
+
+        def slot(i, j):
+            apart = (zplace * ny + yplace) ^ (i * ny + j)
+            return sum(((apart >> step) & 1) << bit for bit, step in enumerate(swaps))
+
+        def spread(odd):
+            def visit(j, carry):
+                order = [slot(i, j) for i in range(nz)]
+                for sources, target in (((fmine, ftheirs), f), ((kmine, ktheirs), k)):
+                    for m in range(8):
+                        pieces = [sources[(i + odd) % 2][order[i], m] for i in range(nz)]
+                        for row in range(4):
+                            whole = jnp.concatenate([p[2 * row : 2 * row + 2] for p in pieces], axis=0)
+                            target[m // 4, 1 + 4 * j + row, m // 2 % 2, m % 2] = whole
+                return carry
+
+            lax.fori_loop(0, ny, visit, 0)
+
+        for odd in range(2):
+            pl.when(lax.rem(zplace, 2) == odd)(lambda odd=odd: spread(odd))
+        blank = jnp.zeros((depth, LANES), F32)
+        for line in (0, height + 1):
+            for e in range(2):
+                for s in range(2):
+                    for c in range(2):
+                        k[c, line, e, s] = blank
+                        u[c][line, e, s] = blank
+                        v[c][line, e, s] = blank
+
+        def prepare(c):
+            def visit(line, parity):
+                for e in range(2):
+                    for s in range(2):
+                        centre, total = diagonal(k.at[c], k.at[1 - c], line, e, s, (e + parity + c) % 2, 2, closed)
+                        scale = 1.0 / total
+                        start = 8.0 * f[c, line, e, s] * scale
+                        g[c, line, e, s] = scale
+                        fs[c, line, e, s] = start
+                        if c == 0:
+                            half[line, e, s] = 0.125 * total
+                            ur[line, e, s] = start
+                            vr[line, e, s] = centre * start
+
+            over_lines(0, height - 1, 1, visit, 8)
+
+        def fresh(c, line, parity, e, s):
+            q = (e + parity + c) % 2
+            near = neighbours(u[1 - c], line, e, s, q, 2, closed)
+            flow = neighbours(v[1 - c], line, e, s, q, 2, closed)
+            return fs[c, line, e, s] + g[c, line, e, s] * (k[c, line, e, s] * near + flow)
+
+        def relax(c):
+            def visit(line, parity):
+                for e in range(2):
+                    for s in range(2):
+                        value = fresh(c, line, parity, e, s)
+                        u[c][line, e, s] = value
+                        v[c][line, e, s] = k[c, line, e, s] * value
+
+            over_lines(0, height - 1, 1, visit, 8)
+
+        prepare(0)
+        prepare(1)
+        relax(1)
+        relax(0)
+        relax(1)
+
+        def restrict(i, carry):
+            for s in range(2):
+                value, conduct = None, None
+                for j in range(2):
+                    line = 1 + 2 * i + j
+                    for e in range(2):
+                        part = half[line, e, s] * (fresh(0, line, j, e, s) - ur[line, e, s])
+                        value = part if value is None else value + part
+                        part = k[0, line, e, s] + k[1, line, e, s]
+                        conduct = part if conduct is None else conduct + part
+                f2[s, i] = value * 0.125
+                k2[s, i] = conduct * 0.125
+            return carry
+
+        lax.fori_loop(0, height2, restrict, 0)
+
+        even = iota(0, depth) % 2 == 0
+
+        def q_is_zero(c, y):
+            return even if (y + c) % 2 == 0 else jnp.logical_not(even)
+
+        def coloured(pair, c, y):
+            return jnp.where(q_is_zero(c, y), pair[0], pair[1])
+
+        def around(ref, c, y):
+            mid = ref[1 + y]
+            other = jnp.where(q_is_zero(c, y), shifted(mid, -1, 1), shifted(mid, 1, 1))
+            return (mid + other) + (shifted(mid, -1, 0) + shifted(mid, 1, 0)) + (ref[y] + ref[y + 2])
+
+        for c in range(2):
+            for line in (0, height2 + 1):
+                kc[c, line] = blank
+                uc[c, line] = blank
+                vc[c, line] = blank
+            for y in range(height2):
+                kc[c, 1 + y] = coloured((k2[0, y], k2[1, y]), c, y)
+                fc[c, y] = coloured((f2[0, y], f2[1, y]), c, y)
+        for c in range(2):
+            for y in range(height2):
+                centre = kc[c, 1 + y]
+                total = 6.0 * centre + around(kc.at[1 - c], c, y)
+                scale = 1.0 / total
+                start = 32.0 * fc[c, y] * scale
+                gc[c, y] = scale
+                sc[c, y] = start
+                if c == 0:
+                    hc[y] = total * (0.5 / 16.0)
+                    uc[0, 1 + y] = start
+                    vc[0, 1 + y] = centre * start
+
+        def fresh2(c, y):
+            flow = kc[c, 1 + y] * around(uc.at[1 - c], c, y) + around(vc.at[1 - c], c, y)
+            return sc[c, y] + gc[c, y] * flow
+
+        def relax2(c):
+            for y in range(height2):
+                value = fresh2(c, y)
+                uc[c, 1 + y] = value
+                vc[c, 1 + y] = kc[c, 1 + y] * value
+
+        relax2(1)
+        relax2(0)
+        relax2(1)
+
+        def paired(a, b):
+            total = (a + b) * 0.125
+            return jnp.where(even, total + pltpu.roll(total, depth - 1, axis=0), 0.0)
+
+        conduct = []
+        right = []
+        for y in range(height3):
+            parts = [hc[2 * y + j] * (fresh2(0, 2 * y + j) - uc[0, 1 + 2 * y + j]) for j in range(2)]
+            right.append(paired(*parts))
+            parts = [kc[0, 1 + 2 * y + j] + kc[1, 1 + 2 * y + j] for j in range(2)]
+            conduct.append(paired(*parts))
+        moves = ((-2, 0), (2, 0), (-1, 1), (1, 1))
+        for y in range(height3):
+            centre = conduct[y]
+            beside = [shifted(centre, step, axis) for step, axis in moves]
+            beside.append(conduct[y - 1] if y else jnp.zeros_like(centre))
+            beside.append(conduct[y + 1] if y + 1 < height3 else jnp.zeros_like(centre))
+            total = 6.0 * centre
+            for part in beside:
+                total = total + part
+            scale = jnp.where(even, 1.0 / jnp.where(even, total, 1.0), 0.0)
+            f3[y] = 128.0 * right[y] * scale
+            lane, row = iota(1, depth), iota(0, depth)
+            open_faces = (row >= 2, row < depth - 2, lane >= 1, lane < LANES - 1)
+            for i in range(6):
+                weight = (centre + beside[i]) * scale
+                w3[y, i] = jnp.where(open_faces[i], weight, 0.0) if i < 4 else weight
+        mixed = (iota(0, depth) // 2 + iota(1, depth)) % 2
+
+        def relax3(c, field):
+            result = []
+            for y in range(height3):
+                mid = field[y]
+                value = f3[y]
+                for i, (step, axis) in enumerate(moves):
+                    value = value + w3[y, i] * pltpu.roll(mid, -step % mid.shape[axis], axis=axis)
+                if y:
+                    value = value + w3[y, 4] * field[y - 1]
+                if y + 1 < height3:
+                    value = value + w3[y, 5] * field[y + 1]
+                result.append(jnp.where(mixed == (y + c) % 2, value, mid))
+            return result
+
+        def two_colours(_, field):
+            return tuple(relax3(1, relax3(0, list(field))))
+
+        field = lax.fori_loop(0, 12, two_colours, (blank,) * height3)
+
+        for y in range(height2):
+            coarse = field[y // 2]
+            value = uc[1, 1 + y] + (coarse + pltpu.roll(coarse, 1, axis=0))
+            uc[1, 1 + y] = value
+            vc[1, 1 + y] = kc[1, 1 + y] * value
+        for c in (0, 1, 0, 1):
+            relax2(c)
+
+        for y in range(height2):
+            zero = q_is_zero(0, y)
+            red, black = uc[0, 1 + y], uc[1, 1 + y]
+            f2[0, y] = jnp.where(zero, red, black)
+            f2[1, y] = jnp.where(zero, black, red)
+
+        def add(line, parity):
+            for e in range(2):
+                for s in range(2):
+                    value = ub[line, e, s] + f2[s, (line - 1) // 2]
+                    ub[line, e, s] = value
+                    vb[line, e, s] = k[1, line, e, s] * value
+
+        over_lines(0, height - 1, 1, add, 8)
+        for c in (0, 1, 0, 1):
+            relax(c)
+
+        for j in range(-3, 7):
+            line = 1 + jnp.clip(4 * yplace + j, 0, height - 1)
+            for t in range(-3, 7):
+                e = t % 2
+                at = pl.ds(jnp.clip(2 * zplace + t // 2, 0, depth - 1), 1)
+                for s in range(4):
+                    row = u[(s + e + j) % 2][line, e, s // 2, at, :]
+                    if -2 <= t <= 5:
+                        error[j + 3, s, t % 8 : t % 8 + 1, :] = row
+                    elif 0 <= j < 8 // 2:
+                        errorx[1 if t < 0 else 0, j, s : s + 1, :] = row
+
+    lines, lines2 = (height + 2, 2, 2, depth, LANES), (height2 + 2, depth, LANES)
+    flat2 = (2, height2, depth, LANES)
+    scratch = [(2, *lines)] * 4 + [lines] * 5 + [flat2, flat2, flat2, (2, *lines2), flat2, flat2]
+    scratch += [(2, *lines2), (2, *lines2), flat2[1:], (height3, 6, depth, LANES), (height3, depth, LANES)]
+    return body, scratch
+
+
+def swap_steps(nz, ny):
+    ybits, zbits = ny.bit_length() - 1, nz.bit_length() - 1
+    return [*range(ybits - 1, -1, -1), *range(ybits + zbits - 1, ybits - 1, -1)]
+
+
+def swap(block, step, nz, ny):
+    return lax.ppermute(block, ("gz", "gy"), [(i, i ^ (1 << step)) for i in range(nz * ny)])
+
+
+def swapped(block, step, nz, ny):
+    return jnp.concatenate([block, swap(block, step, nz, ny)])
+
+
+def solve_coarse(fmine, ftheirs, kmine, ktheirs, nz, ny):
+    body, scratch = coarse_kernel(nz, ny)
+    outs = ((10, 4, 8, LANES), (2, 4, 4, LANES))
+    return call(body, 11, outs, scratch, fmine, ftheirs, kmine, ktheirs)
 
 
 def extended(array, sides, width):
@@ -120,24 +757,89 @@
     return (field, remainder(field))
 
 
+def natural_coarse(message):
+    packed = message.reshape(2, 2, 2, 4, 2, LANES)
+    parity = (jnp.arange(2)[:, None, None, None, None] + jnp.arange(4)[None, None, :, None, None]) % 2 == 0
+    even = jnp.where(parity, packed[0], packed[1])
+    odd = jnp.where(parity, packed[1], packed[0])
+    both = jnp.stack([even, odd])
+    return both.transpose(4, 1, 3, 5, 2, 0).reshape(4, 4, 4 * LANES)
+
+
+def solve_coarse_spread(message, kmessage, nz, ny):
+    z_start, y_start = 4 * lax.axis_index("gz"), 4 * lax.axis_index("gy")
+    field, unused = cycle(
+        natural_coarse(message), natural_coarse(kmessage), 1, "split", z_start, y_start, 4 * nz, 4 * ny
+    )
+    wide = extended(field, (("gz", 0), ("gy", 1)), 3).reshape(10, 10, LANES, 4).transpose(1, 3, 0, 2)
+    error = jnp.concatenate([wide[:, :, 3:9], wide[:, :, 1:3]], axis=2)
+    return error, jnp.stack([wide[3:7, :, 9], wide[3:7, :, 0]])
+
+
+def exchange(first, second, axis):
+    size = lax.axis_size(axis)
+    results = []
+    for message, start in ((first, 0), (second, 1)):
+        pairs = [(i, i + 1) for i in range(start, size - 1, 2)]
+        results.append(lax.ppermute(message, axis, pairs + [(j, i) for i, j in pairs]))
+    return results
+
+
 def on_device(right_side, coefficient):
-    depth, rows, width = right_side.shape
-    z_start = lax.axis_index("gz") * depth
-    y_start = lax.axis_index("gy") * rows
-    z_total = depth * lax.axis_size("gz")
-    y_total = rows * lax.axis_size("gy")
-    correction, residual = cycle(
-        right_side, coefficient, 0, "split", z_start, y_start, z_total, y_total
+    nz, ny = lax.axis_size("gz"), lax.axis_size("gy")
+    assert right_side.shape == (8, 8, 8 * LANES)
+    cells = (2, 2, 8, 2, 4, 4, LANES)
+    yface, zface = (16, 2, 4, 4, LANES), (8, 4, 16, LANES)
+    coarse = (8, 8, LANES)
+    outs = (cells, yface, yface, zface, zface, coarse)
+    packed = call(pack_kernel, 3, outs, [(2, 8, 64, LANES)], right_side, coefficient)
+    local, ya, yb, za, zb, kmessage = packed
+    coarse_cells = 8 * 8 * LANES
+    whole = nz * ny * coarse_cells <= WHOLE_COARSE_CELLS and nz & (nz - 1) == 0 and ny & (ny - 1) == 0
+    swaps = swap_steps(nz, ny)
+    kall = kmessage[None]
+    ya, yb = exchange(ya, yb, "gy")
+    za, zb = exchange(za, zb, "gz")
+    relayed = (8 * CORNER_ROWS, LANES)
+    ca, cb = exchange(*call(relay_kernel, 2, (relayed, relayed), [], za, zb), "gy")
+    if whole:
+        kall = swapped(kall, swaps[0], nz, ny)
+        kall = swapped(kall, swaps[1], nz, ny)
+        ca, cb, kall = lax.optimization_barrier((ca, cb, kall))
+        for step in swaps[2:-1]:
+            kall = swapped(kall, step, nz, ny)
+        ktheirs = swap(kall, swaps[-1], nz, ny)
+    lines, zface = (LINES, 2, 4, 8, LANES), (160, LANES)
+    outs = ((2, *lines), (2, *lines), (2, *lines), (8, *lines[1:]), lines, (2, 8, 4, LANES), zface, zface, coarse)
+    scratch = [(2, *lines), lines, lines, lines]
+    k, g, fs, half, ub, kx, zc, zd, message = call(down_kernel, 6, outs, scratch, local, ya, yb, za, zb, ca, cb)
+    fall, half_way = message[None], len(swaps) // 2
+    zc, zd = exchange(zc, zd, "gz")
+    if whole:
+        for step in swaps[:half_way]:
+            fall = swapped(fall, step, nz, ny)
+        fall, zc, zd = lax.optimization_barrier((fall, zc, zd))
+    yface = (5, *lines[1:])
+    wide, yc, yd = call(widen_kernel, 2, ((8, *lines[1:]), yface, yface), [], ub, zc, zd)
+    if whole:
+        fall = swapped(fall, swaps[half_way], nz, ny)
+        fall, yc, yd = lax.optimization_barrier((fall, yc, yd))
+    yc, yd = exchange(yc, yd, "gy")
+    if whole:
+        for step in swaps[half_way + 1 : -1]:
+            fall = swapped(fall, step, nz, ny)
+        fall, yc, yd = lax.optimization_barrier((fall, yc, yd))
+        ftheirs = swap(fall, swaps[-1], nz, ny)
+        error, errorx = solve_coarse(fall, ftheirs, kall, ktheirs, nz, ny)
+    else:
+        error, errorx = solve_coarse_spread(message, kmessage, nz, ny)
+    block = (8, 8, 8 * LANES)
+    scratch = [lines] * 4 + [(2, 8, 4, LANES)] * 2 + [(2, 8, 64, LANES)]
+    return call(up_kernel, 6, (block, block), scratch, k, g, fs, half, wide, kx, yc, yd, zc, zd, error, errorx)
+
+
+def solution(mesh):
+    spec = P("gz", "gy", None)
+    return jax.shard_map(
+        on_device, mesh=mesh, in_specs=(spec, spec), out_specs=(spec, spec), check_vma=False
     )
-    return (correction, residual)
-
-
-def solution(mesh):
-    placed = (P("gz", "gy", None), P("gz", "gy", None))
-    return jax.shard_map(
-        on_device,
-        mesh=mesh,
-        in_specs=placed,
-        out_specs=(P("gz", "gy", None), P("gz", "gy", None)),
-        check_vma=False,
-    )

time: 699 us -> 88.4 us (0.13); the launches traced: 687 us -> 87.8 us
  starting transfers between devices: 454 us -> 32.5 us
  waiting for transfers between devices: 135 us -> 17.4 us
  local copies, waits for them, and re-layouts: 60.5 us -> 3.08 us
  Pallas kernels: 0 us -> 30.8 us
  other arithmetic: 19.6 us -> 3.13 us
  blocking collectives: 12.2 us -> 0 us
    ppermute x154 -> x20, starting transfers between devices: 454 us -> 32.5 us  [the longest x10 24.3 us: swap(): lax.ppermute(block, ('gz', 'gy'), [(i, i ^ 1 << step) for i in range(nz *...]
    ppermute x154 -> x20, waiting for transfers between devices: 135 us -> 17.4 us  [the longest x10 16 us: swap(): lax.ppermute(block, ('gz', 'gy'), [(i, i ^ 1 << step) for i in range(nz *...]
    slice x95 -> x0, local copies, waits for them, and re-layouts: 47.5 us -> none  [the longest x12 11.9 us: coarsen(): total = total + field[1::2, 1::2, 0::2] + field[1::2, 1::2, 1::2]]
    pallas_call x0 -> x6, Pallas kernels: none -> 30.8 us  [call(): pl.pallas_call(body, out_shape=[jax.ShapeDtypeStruct(s, F32) for s in out...]
    all_gather x2 -> x0, blocking collectives: 12.2 us -> none  [the longest x1 6.35 us: cycle(): lax.all_gather(rhs_next, 'gz', axis=0, tiled=True)]
    select_n x47 -> x0, other arithmetic: 9.42 us -> none  [relax(): return jnp.where(colour, fresh, field)]
  transfers between devices with their start and end apart: 154 -> 20, of which waited for: 68 -> 7; matrix products, arithmetic and copies ran while one was open for 5% -> 3% of each run, Pallas kernels for 0% -> 4%
where the time goes in v1:
time: 88.4 us; the launch traced here: 87.8 us
  starting transfers between devices  32.5 us (37%)
  Pallas kernels  30.8 us (35%)
  waiting for transfers between devices  17.4 us (20%)
  other arithmetic  3.13 us (4%)
  local copies, waits for them, and re-layouts  3.08 us (3%)
  between operations  0.91 us (1%)
    pallas_call x6, Pallas kernels, call(): pl.pallas_call(body, out_shape=[jax.ShapeDtypeStruct(s, F32) for s in out...  30.8 us
    ppermute x10, starting transfers between devices, swap(): lax.ppermute(block, ('gz', 'gy'), [(i, i ^ 1 << step) for i in range(nz *...  24.3 us
    ppermute x10, waiting for transfers between devices, swap(): lax.ppermute(block, ('gz', 'gy'), [(i, i ^ 1 << step) for i in range(nz *...  16 us
    ppermute x10, starting transfers between devices, exchange(): lax.ppermute(message, axis, pairs + [(j, i) for i, j in pairs])  8.19 us
    concatenate x7, other arithmetic, swapped(): return jnp.concatenate([block, swap(block, step, nz, ny)])  3.13 us
    unnamed x34, local copies, waits for them, and re-layouts  3.07 us
  transfers between devices with their start and end apart: 20, of which 7 were waited for; matrix products, arithmetic and copies ran while one was open for 3% of the time, Pallas kernels for 4%

profile of v1, /device:TPU:0, one launch (start us, length us, event | category | flops | bytes accessed | tf_op | source)
XLA Modules:
  0.0 87.8 jit_solution(17789894697948194620)
XLA Ops:
  0.6 4.0 %shard_map.41 = (f32[2,2,8,2,4,4,128]{6,5,4,3,2,1,0:T(4,128)}, f32[16,2,4,4,128]{4,3,2,1,0:T(4,128)}, f32[16,2,4,4,128]{4,3,2,1,0:T(4,128)}, f32[8,4,16,128]{3,2...) custom-call(f32[8,8,1024]{2,1,0:T(8,128)} %f_ref.1, f32[8,8,1024]{2,1,0:T(8,128)} %k_ref.1), custom_call_target="tpu_custom_call" | custom-call | bytes 9000000 | tf_op jit(solution)/shard_map/pallas_call | solution.py:18
  5.0 0.7 collective-permute-start.3
  5.7 3.7 %collective-permute-start.6 = (f32[1,8,8,128]{3,2,1,0:T(8,128)}, f32[1,8,8,128]{3,2,1,0:T(8,128)S(1)}, u32[]{:S(2)}, u32[]{:S(2)}) collective-permute-start(f32[1,8,8,128]{3,2,1,0:T(8,128)} %bitcast.2), channel_id=1, source_target_pairs={{0,4},{1,5},{2,6},{3,7},{4,0},{5,1},{6,2},{7,3},{8,12},{9,13},{10,... | collective-permute-start | bytes 98312 | tf_op jit(solution)/shard_map/ppermute | solution.py:633
  9.4 1.5 %collective-permute-start = (f32[16,2,4,4,128]{4,3,2,1,0:T(4,128)}, f32[16,2,4,4,128]{4,3,2,1,0:T(4,128)S(1)}, u32[]{:S(2)}, u32[]{:S(2)}) collective-permute-start(f32[16,2,4,4,128]{4,3,2,1,0:T(4,128)} %get-tuple-element.37), channel_id=1, source_target_pairs={{0,1},{2,3},{4,5},{6,7},{1,0},{3,2},{5,4},{7,6},{8,9},{10,11},{12,... | collective-permute-start | bytes 786440 | tf_op jit(solution)/shard_map/ppermute | solution.py:784
  10.9 0.7 collective-permute-start.1
  11.5 0.8 pad_maximum_fusion.5
  12.3 3.2 %collective-permute-start.7 = (f32[2,8,8,128]{3,2,1,0:T(8,128)S(1)}, f32[2,8,8,128]{3,2,1,0:T(8,128)S(1)}, u32[]{:S(2)}, u32[]{:S(2)}) collective-permute-start(f32[2,8,8,128]{3,2,1,0:T(8,128)S(1)} %pad_maximum_fusion.5), channel_id=1, source_target_pairs={{0,2},{1,3},{2,0},{3,1},{4,6},{5,7},{6,4},{7,5},{8,10},{9,11},{10,... | collective-permute-start | bytes 196616 | tf_op jit(solution)/shard_map/ppermute | solution.py:633
  15.5 0.7 copy-done.1
  16.2 0.7 copy-done.2
  16.9 1.8 %shard_map.42 = (f32[224,128]{1,0:T(8,128)}, f32[224,128]{1,0:T(8,128)}) custom-call(f32[8,4,16,128]{3,2,1,0:T(8,128)} %copy-done.1, f32[8,4,16,128]{3,2,1,0:T(8,128)} %copy-done.2), custom_call_target="tpu_custom_call" | custom-call | bytes 6000000 | tf_op jit(solution)/shard_map/pallas_call | solution.py:18
  18.7 1.0 %collective-permute-start.4 = (f32[224,128]{1,0:T(8,128)}, f32[224,128]{1,0:T(8,128)S(1)}, u32[]{:S(2)}, u32[]{:S(2)}) collective-permute-start(f32[224,128]{1,0:T(8,128)} %get-tuple-element.41), channel_id=1, source_target_pairs={{0,1},{2,3},{4,5},{6,7},{1,0},{3,2},{5,4},{7,6},{8,9},{10,11},{12,... | collective-permute-start | bytes 344072 | tf_op jit(solution)/shard_map/ppermute | solution.py:784
  20.4 1.8 %collective-permute-done.7 = f32[2,8,8,128]{3,2,1,0:T(8,128)S(1)} collective-permute-done((f32[2,8,8,128]{3,2,1,0:T(8,128)S(1)}, f32[2,8,8,128]{3,2,1,0:T(8,128)S(1)}, u32[]{:S(2)}, u32[]{:S(2)}) %collective-permute-start.7) | collective-permute-done | bytes 65568 | tf_op jit(solution)/shard_map/ppermute | solution.py:633
  22.2 0.8 pad_maximum_fusion.3
  23.0 1.4 %collective-permute-done.4.ca = f32[224,128]{1,0:T(8,128)S(1)} collective-permute-done((f32[224,128]{1,0:T(8,128)}, f32[224,128]{1,0:T(8,128)S(1)}, u32[]{:S(2)}, u32[]{:S(2)}) %collective-permute-start.4) | collective-permute-done | bytes 114720 | tf_op jit(solution)/shard_map/ppermute | solution.py:784
  25.2 5.7 %shard_map.43 = (f32[2,18,2,4,8,128]{5,4,3,2,1,0:T(8,128)}, f32[2,18,2,4,8,128]{5,4,3,2,1,0:T(8,128)}, f32[2,18,2,4,8,128]{5,4,3,2,1,0:T(8,128)}, f32[8,2,4,8,12...) custom-call(f32[2,2,8,2,4,4,128]{6,5,4,3,2,1,0:T(4,128)} %get-tuple-, ...), custom_call_target="tpu_custom_call" | custom-call | bytes 18000000 | tf_op jit(solution)/shard_map/pallas_call | solution.py:18
  31.0 6.0 %collective-permute-start.8 = (f32[1,8,8,128]{3,2,1,0:T(8,128)}, f32[1,8,8,128]{3,2,1,0:T(8,128)S(1)}, u32[]{:S(2)}, u32[]{:S(2)}) collective-permute-start(f32[1,8,8,128]{3,2,1,0:T(8,128)} %bitcast.5), channel_id=1, source_target_pairs={{0,4},{1,5},{2,6},{3,7},{4,0},{5,1},{6,2},{7,3},{8,12},{9,13},{10,... | collective-permute-start | bytes 98312 | tf_op jit(solution)/shard_map/ppermute | solution.py:633
  37.0 2.4 %collective-permute-done.8 = f32[1,8,8,128]{3,2,1,0:T(8,128)S(1)} collective-permute-done((f32[1,8,8,128]{3,2,1,0:T(8,128)}, f32[1,8,8,128]{3,2,1,0:T(8,128)S(1)}, u32[]{:S(2)}, u32[]{:S(2)}) %collective-permute-start.8) | collective-permute-done | bytes 32800 | tf_op jit(solution)/shard_map/ppermute | solution.py:633
  39.4 0.8 pad_maximum_fusion.6
  40.1 2.6 %collective-permute-start.9 = (f32[2,8,8,128]{3,2,1,0:T(8,128)S(1)}, f32[2,8,8,128]{3,2,1,0:T(8,128)S(1)}, u32[]{:S(2)}, u32[]{:S(2)}) collective-permute-start(f32[2,8,8,128]{3,2,1,0:T(8,128)S(1)} %pad_maximum_fusion.6), channel_id=1, source_target_pairs={{0,2},{1,3},{2,0},{3,1},{4,6},{5,7},{6,4},{7,5},{8,10},{9,11},{10,... | collective-permute-start | bytes 196616 | tf_op jit(solution)/shard_map/ppermute | solution.py:633
  43.5 1.5 %collective-permute-done.9 = f32[2,8,8,128]{3,2,1,0:T(8,128)S(1)} collective-permute-done((f32[2,8,8,128]{3,2,1,0:T(8,128)S(1)}, f32[2,8,8,128]{3,2,1,0:T(8,128)S(1)}, u32[]{:S(2)}, u32[]{:S(2)}) %collective-permute-start.9) | collective-permute-done | bytes 65568 | tf_op jit(solution)/shard_map/ppermute | solution.py:633
  45.0 0.8 pad_maximum_fusion.4
  45.8 1.5 %collective-permute-start.12 = (f32[4,8,8,128]{3,2,1,0:T(8,128)S(1)}, f32[4,8,8,128]{3,2,1,0:T(8,128)S(1)}, u32[]{:S(2)}, u32[]{:S(2)}) collective-permute-start(f32[4,8,8,128]{3,2,1,0:T(8,128)S(1)} %pad_maximum_fusion.4), channel_id=1, source_target_pairs={{0,1},{1,0},{2,3},{3,2},{4,5},{5,4},{6,7},{7,6},{8,9},{9,8},{10,11... | collective-permute-start | bytes 393224 | tf_op jit(solution)/shard_map/ppermute | solution.py:633
  47.3 2.0 %shard_map.44 = (f32[8,2,4,8,128]{4,3,2,1,0:T(8,128)}, f32[5,2,4,8,128]{4,3,2,1,0:T(8,128)}, f32[5,2,4,8,128]{4,3,2,1,0:T(8,128)}) custom-call(f32[18,2,4,8,128]{4,3,2,1,0:T(8,128)} %get-tuple-element.50.ub, f32[160,128]{1,0:T(8,128)} %copy-done.6, f32[160,128]{1,0:T(8,128)} %copy-done.7), custom_call_target="tpu_custom_call" | custom-call | bytes 6000000 | tf_op jit(solution)/shard_map/pallas_call | solution.py:18
  49.4 6.0 %collective-permute-start.18 = (f32[8,8,8,128]{3,2,1,0:T(8,128)S(1)}, f32[8,8,8,128]{3,2,1,0:T(8,128)S(1)}, u32[]{:S(2)}, u32[]{:S(2)}) collective-permute-start(f32[8,8,8,128]{3,2,1,0:T(8,128)S(1)} %pad_maximum_fusion.2), channel_id=1, source_target_pairs={{0,16},{1,17},{2,18},{3,19},{4,20},{5,21},{6,22},{7,23},{8,24},{9,... | collective-permute-start | bytes 786440 | tf_op jit(solution)/shard_map/ppermute | solution.py:633
  55.4 1.1 %collective-permute-start.13 = (f32[8,8,8,128]{3,2,1,0:T(8,128)S(1)}, f32[8,8,8,128]{3,2,1,0:T(8,128)S(1)}, u32[]{:S(2)}, u32[]{:S(2)}) collective-permute-start(f32[8,8,8,128]{3,2,1,0:T(8,128)S(1)} %pad_maximum_fusion.1), channel_id=1, source_target_pairs={{0,16},{1,17},{2,18},{3,19},{4,20},{5,21},{6,22},{7,23},{8,24},{9,... | collective-permute-start | bytes 786440 | tf_op jit(solution)/shard_map/ppermute | solution.py:633
  56.6 1.8 %collective-permute-start.14 = (f32[5,2,4,8,128]{4,3,2,1,0:T(8,128)S(1)}, f32[5,2,4,8,128]{4,3,2,1,0:T(8,128)S(1)}, u32[]{:S(2)}, u32[]{:S(2)}) collective-permute-start(f32[5,2,4,8,128]{4,3,2,1,0:T(8,128)S(1)} %copy-done.15), channel_id=1, source_target_pairs={{0,1},{2,3},{4,5},{6,7},{1,0},{3,2},{5,4},{7,6},{8,9},{10,11},{12,... | collective-permute-start | bytes 491528 | tf_op jit(solution)/shard_map/ppermute | solution.py:784
  59.1 3.4 %collective-permute-done.18 = f32[8,8,8,128]{3,2,1,0:T(8,128)S(1)} collective-permute-done((f32[8,8,8,128]{3,2,1,0:T(8,128)S(1)}, f32[8,8,8,128]{3,2,1,0:T(8,128)S(1)}, u32[]{:S(2)}, u32[]{:S(2)}) %collective-permute-start.18) | collective-permute-done | bytes 262176 | tf_op jit(solution)/shard_map/ppermute | solution.py:633
  62.6 5.0 %collective-permute-done.13 = f32[8,8,8,128]{3,2,1,0:T(8,128)S(1)} collective-permute-done((f32[8,8,8,128]{3,2,1,0:T(8,128)S(1)}, f32[8,8,8,128]{3,2,1,0:T(8,128)S(1)}, u32[]{:S(2)}, u32[]{:S(2)}) %collective-permute-start.13) | collective-permute-done | bytes 262176 | tf_op jit(solution)/shard_map/ppermute | solution.py:633
  67.8 1.9 %collective-permute-done.16.ftheirs = f32[16,8,8,128]{3,2,1,0:T(8,128)S(1)} collective-permute-done((f32[16,8,8,128]{3,2,1,0:T(8,128)S(1)}, f32[16,8,8,128]{3,2,1,0:T(8,128)S(1)}, u32[]{:S(2)}, u32[]{:S(2)}) %collective-permute-start.16) | collective-permute-done | bytes 524320 | tf_op jit(solution)/shard_map/ppermute | solution.py:633
  69.7 0.8 copy-done.5
  70.5 11.5 %shard_map.45 = (f32[10,4,8,128]{3,2,1,0:T(8,128)}, f32[2,4,4,128]{3,2,1,0:T(4,128)}) custom-call(f32[16,8,8,128]{3,2,1,0:T(8,128)} %copy-done, f32[16,8,8,128]{3,2,1,0:T(8,128)} %copy-done.5, f32[16,8,8,128]{3,2,1,0:T(8,128)} %copy-done.3, f32[16,8,8,128]{3,2,1,0:T(8,128)} %copy-done.4), custom_call_target="tpu_custom_call" | custom-call | bytes 33000000 | tf_op jit(solution)/shard_map/pallas_call | solution.py:18
  82.0 5.8 %shard_map.46 = (f32[8,8,1024]{2,1,0:T(8,128)}, f32[8,8,1024]{2,1,0:T(8,128)}) custom-call(f32[2,18,2,4,8,128]{5,4,3,2,1,0:T(8,128)} %get-tuple-element.46.k, f32[2,18,2,4,8,128]{5,4,3,2,1,0:T(8,128)} %get-tuple-element.47.g, f32[2,18,2,4,8,128]{5,4,3,2,1,0:T(8,128)} %get-tuple-element.48.fs, f32[8,2,4,8,128]{4,3,2,1,0:T(8,128)} %get-tuple-element.49.half, ...), custom_call_target="tpu_custom_call" | custom-call | bytes 18000000 | tf_op jit(solution)/shard_map/pallas_call | solution.py:18
  (56 shorter events, 3.6 us)
Async XLA Ops:
  4.6 11.0 %collective-permute-start.2 = (f32[8,4,16,128]{3,2,1,0:T(8,128)}, f32[8,4,16,128]{3,2,1,0:T(8,128)S(1)}, u32[]{:S(2)}, u32[]{:S(2)}) collective-permute-start(f32[8,4,16,128]{3,2,1,0:T(8,128)} %get-tuple-element.39), channel_id=1, source_target_pairs={{0,8},{16,24},{8,0},{24,16},{1,9},{17,25},{9,1},{25,17},{2,10},{18... | collective-permute-start | bytes 786440 | tf_op jit(solution)/shard_map/ppermute | solution.py:784
  5.0 10.5 %collective-permute-start.3 = (f32[8,4,16,128]{3,2,1,0:T(8,128)}, f32[8,4,16,128]{3,2,1,0:T(8,128)S(1)}, u32[]{:S(2)}, u32[]{:S(2)}) collective-permute-start(f32[8,4,16,128]{3,2,1,0:T(8,128)} %get-tuple-element.40), channel_id=1, source_target_pairs={{8,16},{16,8},{9,17},{17,9},{10,18},{18,10},{11,19},{19,11},{12,20... | collective-permute-start | bytes 786440 | tf_op jit(solution)/shard_map/ppermute | solution.py:784
  5.7 5.8 %collective-permute-start.6 = (f32[1,8,8,128]{3,2,1,0:T(8,128)}, f32[1,8,8,128]{3,2,1,0:T(8,128)S(1)}, u32[]{:S(2)}, u32[]{:S(2)}) collective-permute-start(f32[1,8,8,128]{3,2,1,0:T(8,128)} %bitcast.2), channel_id=1, source_target_pairs={{0,4},{1,5},{2,6},{3,7},{4,0},{5,1},{6,2},{7,3},{8,12},{9,13},{10,... | collective-permute-start | bytes 98312 | tf_op jit(solution)/shard_map/ppermute | solution.py:633
  9.4 15.0 %collective-permute-start = (f32[16,2,4,4,128]{4,3,2,1,0:T(4,128)}, f32[16,2,4,4,128]{4,3,2,1,0:T(4,128)S(1)}, u32[]{:S(2)}, u32[]{:S(2)}) collective-permute-start(f32[16,2,4,4,128]{4,3,2,1,0:T(4,128)} %get-tuple-element.37), channel_id=1, source_target_pairs={{0,1},{2,3},{4,5},{6,7},{1,0},{3,2},{5,4},{7,6},{8,9},{10,11},{12,... | collective-permute-start | bytes 786440 | tf_op jit(solution)/shard_map/ppermute | solution.py:784
  10.9 13.5 %collective-permute-start.1 = (f32[16,2,4,4,128]{4,3,2,1,0:T(4,128)}, f32[16,2,4,4,128]{4,3,2,1,0:T(4,128)S(1)}, u32[]{:S(2)}, u32[]{:S(2)}) collective-permute-start(f32[16,2,4,4,128]{4,3,2,1,0:T(4,128)} %get-tuple-element.38), channel_id=1, source_target_pairs={{1,2},{3,4},{5,6},{2,1},{4,3},{6,5},{9,10},{11,12},{13,14},{10,9},... | collective-permute-start | bytes 786440 | tf_op jit(solution)/shard_map/ppermute | solution.py:784
  12.3 9.9 %collective-permute-start.7 = (f32[2,8,8,128]{3,2,1,0:T(8,128)S(1)}, f32[2,8,8,128]{3,2,1,0:T(8,128)S(1)}, u32[]{:S(2)}, u32[]{:S(2)}) collective-permute-start(f32[2,8,8,128]{3,2,1,0:T(8,128)S(1)} %pad_maximum_fusion.5), channel_id=1, source_target_pairs={{0,2},{1,3},{2,0},{3,1},{4,6},{5,7},{6,4},{7,5},{8,10},{9,11},{10,... | collective-permute-start | bytes 196616 | tf_op jit(solution)/shard_map/ppermute | solution.py:633
  18.7 5.7 %collective-permute-start.4 = (f32[224,128]{1,0:T(8,128)}, f32[224,128]{1,0:T(8,128)S(1)}, u32[]{:S(2)}, u32[]{:S(2)}) collective-permute-start(f32[224,128]{1,0:T(8,128)} %get-tuple-element.41), channel_id=1, source_target_pairs={{0,1},{2,3},{4,5},{6,7},{1,0},{3,2},{5,4},{7,6},{8,9},{10,11},{12,... | collective-permute-start | bytes 344072 | tf_op jit(solution)/shard_map/ppermute | solution.py:784
  19.7 4.6 %collective-permute-start.5 = (f32[224,128]{1,0:T(8,128)}, f32[224,128]{1,0:T(8,128)S(1)}, u32[]{:S(2)}, u32[]{:S(2)}) collective-permute-start(f32[224,128]{1,0:T(8,128)} %get-tuple-element.42), channel_id=1, source_target_pairs={{1,2},{3,4},{5,6},{2,1},{4,3},{6,5},{9,10},{11,12},{13,14},{10,9},... | collective-permute-start | bytes 344072 | tf_op jit(solution)/shard_map/ppermute | solution.py:784
  24.4 0.8 copy-start.8
  24.4 0.8 copy-start.9
  31.0 8.4 %collective-permute-start.8 = (f32[1,8,8,128]{3,2,1,0:T(8,128)}, f32[1,8,8,128]{3,2,1,0:T(8,128)S(1)}, u32[]{:S(2)}, u32[]{:S(2)}) collective-permute-start(f32[1,8,8,128]{3,2,1,0:T(8,128)} %bitcast.5), channel_id=1, source_target_pairs={{0,4},{1,5},{2,6},{3,7},{4,0},{5,1},{6,2},{7,3},{8,12},{9,13},{10,... | collective-permute-start | bytes 98312 | tf_op jit(solution)/shard_map/ppermute | solution.py:633
  40.1 4.9 %collective-permute-start.9 = (f32[2,8,8,128]{3,2,1,0:T(8,128)S(1)}, f32[2,8,8,128]{3,2,1,0:T(8,128)S(1)}, u32[]{:S(2)}, u32[]{:S(2)}) collective-permute-start(f32[2,8,8,128]{3,2,1,0:T(8,128)S(1)} %pad_maximum_fusion.6), channel_id=1, source_target_pairs={{0,2},{1,3},{2,0},{3,1},{4,6},{5,7},{6,4},{7,5},{8,10},{9,11},{10,... | collective-permute-start | bytes 196616 | tf_op jit(solution)/shard_map/ppermute | solution.py:633
  42.8 6.6 %collective-permute-start.17 = (f32[4,8,8,128]{3,2,1,0:T(8,128)S(1)}, f32[4,8,8,128]{3,2,1,0:T(8,128)S(1)}, u32[]{:S(2)}, u32[]{:S(2)}) collective-permute-start(f32[4,8,8,128]{3,2,1,0:T(8,128)S(1)} %pad_maximum_fusion.3), channel_id=1, source_target_pairs={{0,1},{1,0},{2,3},{3,2},{4,5},{5,4},{6,7},{7,6},{8,9},{9,8},{10,11... | collective-permute-start | bytes 393224 | tf_op jit(solution)/shard_map/ppermute | solution.py:633
  42.8 3.0 %collective-permute-start.10 = (f32[160,128]{1,0:T(8,128)}, f32[160,128]{1,0:T(8,128)S(1)}, u32[]{:S(2)}, u32[]{:S(2)}) collective-permute-start(f32[160,128]{1,0:T(8,128)} %get-tuple-element.52), channel_id=1, source_target_pairs={{0,8},{16,24},{8,0},{24,16},{1,9},{17,25},{9,1},{25,17},{2,10},{18... | collective-permute-start | bytes 245768 | tf_op jit(solution)/shard_map/ppermute | solution.py:784
  42.8 3.0 %collective-permute-start.11 = (f32[160,128]{1,0:T(8,128)}, f32[160,128]{1,0:T(8,128)S(1)}, u32[]{:S(2)}, u32[]{:S(2)}) collective-permute-start(f32[160,128]{1,0:T(8,128)} %get-tuple-element.53), channel_id=1, source_target_pairs={{8,16},{16,8},{9,17},{17,9},{10,18},{18,10},{11,19},{19,11},{12,20... | collective-permute-start | bytes 245768 | tf_op jit(solution)/shard_map/ppermute | solution.py:784
  45.8 1.5 %copy-start.6 = (f32[160,128]{1,0:T(8,128)}, f32[160,128]{1,0:T(8,128)S(1)}, u32[]{:S(2)}) copy-start(f32[160,128]{1,0:T(8,128)S(1)} %collective-permute-done.10.zc) | copy-start | bytes 245764
  45.8 1.5 %copy-start.7 = (f32[160,128]{1,0:T(8,128)}, f32[160,128]{1,0:T(8,128)S(1)}, u32[]{:S(2)}) copy-start(f32[160,128]{1,0:T(8,128)S(1)} %collective-permute-done.11.zd) | copy-start | bytes 245764
  45.8 9.5 %collective-permute-start.12 = (f32[4,8,8,128]{3,2,1,0:T(8,128)S(1)}, f32[4,8,8,128]{3,2,1,0:T(8,128)S(1)}, u32[]{:S(2)}, u32[]{:S(2)}) collective-permute-start(f32[4,8,8,128]{3,2,1,0:T(8,128)S(1)} %pad_maximum_fusion.4), channel_id=1, source_target_pairs={{0,1},{1,0},{2,3},{3,2},{4,5},{5,4},{6,7},{7,6},{8,9},{9,8},{10,11... | collective-permute-start | bytes 393224 | tf_op jit(solution)/shard_map/ppermute | solution.py:633
  49.4 7.2 %copy-start.15 = (f32[5,2,4,8,128]{4,3,2,1,0:T(8,128)S(1)}, f32[5,2,4,8,128]{4,3,2,1,0:T(8,128)}, u32[]{:S(2)}) copy-start(f32[5,2,4,8,128]{4,3,2,1,0:T(8,128)} %get-tuple-element.62) | copy-start | bytes 491524
  49.4 9.0 %copy-start.14 = (f32[5,2,4,8,128]{4,3,2,1,0:T(8,128)S(1)}, f32[5,2,4,8,128]{4,3,2,1,0:T(8,128)}, u32[]{:S(2)}) copy-start(f32[5,2,4,8,128]{4,3,2,1,0:T(8,128)} %get-tuple-element.63) | copy-start | bytes 491524
  49.4 13.1 %collective-permute-start.18 = (f32[8,8,8,128]{3,2,1,0:T(8,128)S(1)}, f32[8,8,8,128]{3,2,1,0:T(8,128)S(1)}, u32[]{:S(2)}, u32[]{:S(2)}) collective-permute-start(f32[8,8,8,128]{3,2,1,0:T(8,128)S(1)} %pad_maximum_fusion.2), channel_id=1, source_target_pairs={{0,16},{1,17},{2,18},{3,19},{4,20},{5,21},{6,22},{7,23},{8,24},{9,... | collective-permute-start | bytes 786440 | tf_op jit(solution)/shard_map/ppermute | solution.py:633
  55.4 12.2 %collective-permute-start.13 = (f32[8,8,8,128]{3,2,1,0:T(8,128)S(1)}, f32[8,8,8,128]{3,2,1,0:T(8,128)S(1)}, u32[]{:S(2)}, u32[]{:S(2)}) collective-permute-start(f32[8,8,8,128]{3,2,1,0:T(8,128)S(1)} %pad_maximum_fusion.1), channel_id=1, source_target_pairs={{0,16},{1,17},{2,18},{3,19},{4,20},{5,21},{6,22},{7,23},{8,24},{9,... | collective-permute-start | bytes 786440 | tf_op jit(solution)/shard_map/ppermute | solution.py:633
  56.6 11.1 %collective-permute-start.14 = (f32[5,2,4,8,128]{4,3,2,1,0:T(8,128)S(1)}, f32[5,2,4,8,128]{4,3,2,1,0:T(8,128)S(1)}, u32[]{:S(2)}, u32[]{:S(2)}) collective-permute-start(f32[5,2,4,8,128]{4,3,2,1,0:T(8,128)S(1)} %copy-done.15), channel_id=1, source_target_pairs={{0,1},{2,3},{4,5},{6,7},{1,0},{3,2},{5,4},{7,6},{8,9},{10,11},{12,... | collective-permute-start | bytes 491528 | tf_op jit(solution)/shard_map/ppermute | solution.py:784
  58.4 9.3 %collective-permute-start.15 = (f32[5,2,4,8,128]{4,3,2,1,0:T(8,128)S(1)}, f32[5,2,4,8,128]{4,3,2,1,0:T(8,128)S(1)}, u32[]{:S(2)}, u32[]{:S(2)}) collective-permute-start(f32[5,2,4,8,128]{4,3,2,1,0:T(8,128)S(1)} %copy-done.14), channel_id=1, source_target_pairs={{1,2},{3,4},{5,6},{2,1},{4,3},{6,5},{9,10},{11,12},{13,14},{10,9},... | collective-permute-start | bytes 491528 | tf_op jit(solution)/shard_map/ppermute | solution.py:784
  62.5 7.2 %copy-start.3 = (f32[16,8,8,128]{3,2,1,0:T(8,128)}, f32[16,8,8,128]{3,2,1,0:T(8,128)S(1)}, u32[]{:S(2)}) copy-start(f32[16,8,8,128]{3,2,1,0:T(8,128)S(1)} %constant_dynamic-update-slice_fusion.kmine) | copy-start | bytes 1572868
  62.5 5.3 %collective-permute-start.19 = (f32[16,8,8,128]{3,2,1,0:T(8,128)S(1)}, f32[16,8,8,128]{3,2,1,0:T(8,128)S(1)}, u32[]{:S(2)}, u32[]{:S(2)}) collective-permute-start(f32[16,8,8,128]{3,2,1,0:T(8,128)S(1)} %constant_dynamic-update-slice_fusion.kmine), channel_id=1, source_target_pairs={{0,8},{1,9},{2,10},{3,11},{4,12},{5,13},{6,14},{7,15},{8,0},{9,1},... | collective-permute-start | bytes 1572872 | tf_op jit(solution)/shard_map/ppermute | solution.py:633
  67.6 2.0 %copy-start = (f32[16,8,8,128]{3,2,1,0:T(8,128)}, f32[16,8,8,128]{3,2,1,0:T(8,128)S(1)}, u32[]{:S(2)}) copy-start(f32[16,8,8,128]{3,2,1,0:T(8,128)S(1)} %pad_maximum_fusion.fmine) | copy-start | bytes 1572868
  67.7 14.3 %copy-start.10 = (f32[5,2,4,8,128]{4,3,2,1,0:T(8,128)}, f32[5,2,4,8,128]{4,3,2,1,0:T(8,128)S(1)}, u32[]{:S(2)}) copy-start(f32[5,2,4,8,128]{4,3,2,1,0:T(8,128)S(1)} %collective-permute-done.14.yc) | copy-start | bytes 491524
  67.7 14.3 %copy-start.11 = (f32[5,2,4,8,128]{4,3,2,1,0:T(8,128)}, f32[5,2,4,8,128]{4,3,2,1,0:T(8,128)S(1)}, u32[]{:S(2)}) copy-start(f32[5,2,4,8,128]{4,3,2,1,0:T(8,128)S(1)} %collective-permute-done.15.yd) | copy-start | bytes 491524
  67.7 2.0 %collective-permute-start.16 = (f32[16,8,8,128]{3,2,1,0:T(8,128)S(1)}, f32[16,8,8,128]{3,2,1,0:T(8,128)S(1)}, u32[]{:S(2)}, u32[]{:S(2)}) collective-permute-start(f32[16,8,8,128]{3,2,1,0:T(8,128)S(1)} %pad_maximum_fusion.fmine), channel_id=1, source_target_pairs={{0,8},{1,9},{2,10},{3,11},{4,12},{5,13},{6,14},{7,15},{8,0},{9,1},... | collective-permute-start | bytes 1572872 | tf_op jit(solution)/shard_map/ppermute | solution.py:633
  67.8 1.9 %copy-start.4 = (f32[16,8,8,128]{3,2,1,0:T(8,128)}, f32[16,8,8,128]{3,2,1,0:T(8,128)S(1)}, u32[]{:S(2)}) copy-start(f32[16,8,8,128]{3,2,1,0:T(8,128)S(1)} %collective-permute-done.19.ktheirs) | copy-start | bytes 1572868
  69.7 0.8 copy-start.5
  (4 other events, 2.7 us)

commit v2 on v1

--- a/solution.py
+++ b/solution.py
@@ -20,7 +20,7 @@
         out_shape=[jax.ShapeDtypeStruct(s, F32) for s in outs],
         in_specs=specs or [vmem] * len(args),
         out_specs=[vmem] * len(outs),
-        scratch_shapes=[pltpu.VMEM(s, F32) for s in scratch],
+        scratch_shapes=[pltpu.VMEM(s, F32) if isinstance(s, tuple) else s for s in scratch],
         cost_estimate=pl.CostEstimate(flops=0, transcendentals=0, bytes_accessed=micros * 3_000_000),
         compiler_params=pltpu.CompilerParams(vmem_limit_bytes=56 << 20),
     )(*args)
@@ -83,8 +83,8 @@
     return jnp.where(flag, a, b), jnp.where(flag, b, a)
 
 
-def pack_kernel(f_ref, k_ref, local, ya, yb, za, zb, coarse, natural):
-    zup, yup = own_sides()
+def pack_kernel(f_ref, k_ref, local, ya, yb, natural):
+    _, yup = own_sides()
     for a, ref in enumerate((f_ref, k_ref)):
         for z in range(8):
             arrays = split_lanes([ref[z, :, t * LANES : (t + 1) * LANES] for t in range(8)])
@@ -102,6 +102,10 @@
         ya[i] = local[a, c, first]
         yb[i] = local[a, c, second]
 
+
+def zpack_kernel(local, za, zb, coarse):
+    zup, _ = own_sides()
+
     def faces(y, carry):
         for i, (a, c, d) in enumerate(ZFACE):
             high, low = 8 - d, d - 1
@@ -122,8 +126,13 @@
             put_coarse(coarse, row, s, total * 0.125)
 
 
-def relay_kernel(za, zb, ca, cb):
+def relay_kernel(za_far, zb_far, ca, cb, za, zb, sem):
     zabove, yup = own_sides()
+    copies = [pltpu.make_async_copy(*pair, sem.at[i]) for i, pair in enumerate(((za_far, za), (zb_far, zb)))]
+    for copy in copies:
+        copy.start()
+    for copy in copies:
+        copy.wait()
     for target, up in ((ca, yup), (cb, jnp.logical_not(yup))):
         for d, (_, at, rows) in CORNER.items():
             y = jnp.where(up, 8 - d, d - 1)
@@ -400,16 +409,18 @@
     ):
         u, v = (ur, ub), (vr, vb)
         zplace, yplace = lax.axis_index("gz"), lax.axis_index("gy")
-        swaps = swap_steps(nz, ny)[:-1]
-
-        def slot(i, j):
+
+        def slot(i, j, swaps):
             apart = (zplace * ny + yplace) ^ (i * ny + j)
-            return sum(((apart >> step) & 1) << bit for bit, step in enumerate(swaps))
+            return sum(((apart >> step) & 1) << bit for bit, step in enumerate(swaps[:-1]))
 
         def spread(odd):
             def visit(j, carry):
-                order = [slot(i, j) for i in range(nz)]
-                for sources, target in (((fmine, ftheirs), f), ((kmine, ktheirs), k)):
+                for sources, target, swaps in (
+                    ((fmine, ftheirs), f, swap_steps(nz, ny)),
+                    ((kmine, ktheirs), k, swap_steps(nz, ny, 0)),
+                ):
+                    order = [slot(i, j, swaps) for i in range(nz)]
                     for m in range(8):
                         pieces = [sources[(i + odd) % 2][order[i], m] for i in range(nz)]
                         for row in range(4):
@@ -624,9 +635,12 @@
     return body, scratch
 
 
-def swap_steps(nz, ny):
+def swap_steps(nz, ny, first=None):
     ybits, zbits = ny.bit_length() - 1, nz.bit_length() - 1
-    return [*range(ybits - 1, -1, -1), *range(ybits + zbits - 1, ybits - 1, -1)]
+    along_y = list(range(ybits - 1, -1, -1))
+    if first is not None:
+        along_y = [first, *(bit for bit in along_y if bit != first)]
+    return [*along_y, *range(ybits + zbits - 1, ybits - 1, -1)]
 
 
 def swap(block, step, nz, ny):
@@ -791,24 +805,28 @@
     cells = (2, 2, 8, 2, 4, 4, LANES)
     yface, zface = (16, 2, 4, 4, LANES), (8, 4, 16, LANES)
     coarse = (8, 8, LANES)
-    outs = (cells, yface, yface, zface, zface, coarse)
-    packed = call(pack_kernel, 3, outs, [(2, 8, 64, LANES)], right_side, coefficient)
-    local, ya, yb, za, zb, kmessage = packed
+    packed = call(pack_kernel, 3, (cells, yface, yface), [(2, 8, 64, LANES)], right_side, coefficient)
+    local, ya, yb = packed
+    ya, yb = exchange(ya, yb, "gy")
+    za, zb, kmessage = call(zpack_kernel, 2, (zface, zface, coarse), [], local)
+    za, zb = exchange(za, zb, "gz")
     coarse_cells = 8 * 8 * LANES
     whole = nz * ny * coarse_cells <= WHOLE_COARSE_CELLS and nz & (nz - 1) == 0 and ny & (ny - 1) == 0
-    swaps = swap_steps(nz, ny)
+    swaps, kswaps = swap_steps(nz, ny), swap_steps(nz, ny, 0)
     kall = kmessage[None]
-    ya, yb = exchange(ya, yb, "gy")
-    za, zb = exchange(za, zb, "gz")
+    if whole:
+        kall = swapped(kall, kswaps[0], nz, ny)
+        ya, za, zb, kall = lax.optimization_barrier((ya, za, zb, kall))
     relayed = (8 * CORNER_ROWS, LANES)
-    ca, cb = exchange(*call(relay_kernel, 2, (relayed, relayed), [], za, zb), "gy")
+    scratch = [zface, zface, pltpu.SemaphoreType.DMA((2,))]
+    far = [pl.BlockSpec(memory_space=pl.ANY)] * 2
+    ca, cb = exchange(*call(relay_kernel, 2, (relayed, relayed), scratch, za, zb, specs=far), "gy")
     if whole:
-        kall = swapped(kall, swaps[0], nz, ny)
-        kall = swapped(kall, swaps[1], nz, ny)
+        for step in kswaps[1:-2]:
+            kall = swapped(kall, step, nz, ny)
         ca, cb, kall = lax.optimization_barrier((ca, cb, kall))
-        for step in swaps[2:-1]:
-            kall = swapped(kall, step, nz, ny)
-        ktheirs = swap(kall, swaps[-1], nz, ny)
+        kall = swapped(kall, kswaps[-2], nz, ny)
+        ktheirs = swap(kall, kswaps[-1], nz, ny)
     lines, zface = (LINES, 2, 4, 8, LANES), (160, LANES)
     outs = ((2, *lines), (2, *lines), (2, *lines), (8, *lines[1:]), lines, (2, 8, 4, LANES), zface, zface, coarse)
     scratch = [(2, *lines), lines, lines, lines]

time: 88.4 us -> 91.2 us (1.032)
  waiting for transfers between devices: 17.4 us -> 24.4 us
  starting transfers between devices: 32.5 us -> 28.3 us
  Pallas kernels: 30.8 us -> 32.3 us
    ppermute x10, waiting for transfers between devices: 16 us -> 24.4 us  [swap(): lax.ppermute(block, ('gz', 'gy'), [(i, i ^ 1 << step) for i in range(nz *...]
    ppermute x10, starting transfers between devices: 24.3 us -> 19.1 us  [swap(): lax.ppermute(block, ('gz', 'gy'), [(i, i ^ 1 << step) for i in range(nz *...]
    pallas_call x6 -> x7, Pallas kernels: 30.8 us -> 32.3 us  [call(): pl.pallas_call(body, out_shape=[jax.ShapeDtypeStruct(s, F32) for s in out...]
    ppermute x10, waiting for transfers between devices: 1.41 us -> 0.03 us  [exchange(): lax.ppermute(message, axis, pairs + [(j, i) for i, j in pairs])]
    ppermute x10, starting transfers between devices: 8.19 us -> 9.27 us  [exchange(): lax.ppermute(message, axis, pairs + [(j, i) for i, j in pairs])]
    unnamed x34 -> x29, local copies, waits for them, and re-layouts: 3.07 us -> 2.22 us
  transfers between devices with their start and end apart: 20 -> 20, of which waited for: 7 -> 8; matrix products, arithmetic and copies ran while one was open for 3% -> 2% of each run, Pallas kernels for 4% -> 7%
where the time goes in v2:
time: 91.2 us; the launch traced here: 90.6 us
  Pallas kernels  32.3 us (35%)
  starting transfers between devices  28.3 us (31%)
  waiting for transfers between devices  24.4 us (27%)
  other arithmetic  2.38 us (3%)
  local copies, waits for them, and re-layouts  2.24 us (2%)
  between operations  0.92 us (1%)
    pallas_call x7, Pallas kernels, call(): pl.pallas_call(body, out_shape=[jax.ShapeDtypeStruct(s, F32) for s in out...  32.3 us
    ppermute x10, waiting for transfers between devices, swap(): lax.ppermute(block, ('gz', 'gy'), [(i, i ^ 1 << step) for i in range(nz *...  24.4 us
    ppermute x10, starting transfers between devices, swap(): lax.ppermute(block, ('gz', 'gy'), [(i, i ^ 1 << step) for i in range(nz *...  19.1 us
    ppermute x10, starting transfers between devices, exchange(): lax.ppermute(message, axis, pairs + [(j, i) for i, j in pairs])  9.27 us
    concatenate x7, other arithmetic, swapped(): return jnp.concatenate([block, swap(block, step, nz, ny)])  2.38 us
    unnamed x29, local copies, waits for them, and re-layouts  2.22 us
  transfers between devices with their start and end apart: 20, of which 8 were waited for; matrix products, arithmetic and copies ran while one was open for 2% of the time, Pallas kernels for 7%

profile of v2, /device:TPU:0, one launch (start us, length us, event | category | flops | bytes accessed | tf_op | source)
XLA Modules:
  0.0 90.6 jit_solution(14084292873843657863)
XLA Ops:
  0.6 3.3 %shard_map.41 = (f32[2,2,8,2,4,4,128]{6,5,4,3,2,1,0:T(4,128)}, f32[16,2,4,4,128]{4,3,2,1,0:T(4,128)}, f32[16,2,4,4,128]{4,3,2,1,0:T(4,128)}) custom-call(f32[8,8,1024]{2,1,0:T(8,128)} %f_ref.1, f32[8,8,1024]{2,1,0:T(8,128)} %k_ref.1), custom_call_target="tpu_custom_call" | custom-call | bytes 9000000 | tf_op jit(solution)/shard_map/pallas_call | solution.py:18
  3.9 2.9 %collective-permute-start = (f32[16,2,4,4,128]{4,3,2,1,0:T(4,128)}, f32[16,2,4,4,128]{4,3,2,1,0:T(4,128)S(1)}, u32[]{:S(2)}, u32[]{:S(2)}) collective-permute-start(f32[16,2,4,4,128]{4,3,2,1,0:T(4,128)} %get-tuple-element.41), channel_id=1, source_target_pairs={{0,1},{2,3},{4,5},{6,7},{1,0},{3,2},{5,4},{7,6},{8,9},{10,11},{12,... | collective-permute-start | bytes 786440 | tf_op jit(solution)/shard_map/ppermute | solution.py:798
  6.9 2.3 %shard_map.42 = (f32[8,4,16,128]{3,2,1,0:T(8,128)}, f32[8,4,16,128]{3,2,1,0:T(8,128)}, f32[8,8,128]{2,1,0:T(8,128)}) custom-call(f32[2,2,8,2,4,4,128]{6,5,4,3,2,1,0:T(4,128)} %get-tuple-element.40.local), custom_call_target="tpu_custom_call" | custom-call | bytes 6000000 | tf_op jit(solution)/shard_map/pallas_call | solution.py:18
  9.1 0.7 collective-permute-start.2
  9.9 4.1 %collective-permute-done.3 = f32[1,8,8,128]{3,2,1,0:T(8,128)S(1)} collective-permute-done((f32[1,8,8,128]{3,2,1,0:T(8,128)}, f32[1,8,8,128]{3,2,1,0:T(8,128)S(1)}, u32[]{:S(2)}, u32[]{:S(2)}) %collective-permute-start.3) | collective-permute-done | bytes 32800 | tf_op jit(solution)/shard_map/ppermute | solution.py:647
  14.0 0.8 pad_maximum_fusion.5
  14.8 2.7 %collective-permute-start.7 = (f32[2,8,8,128]{3,2,1,0:T(8,128)S(1)}, f32[2,8,8,128]{3,2,1,0:T(8,128)S(1)}, u32[]{:S(2)}, u32[]{:S(2)}) collective-permute-start(f32[2,8,8,128]{3,2,1,0:T(8,128)S(1)} %pad_maximum_fusion.5), channel_id=1, source_target_pairs={{0,4},{1,5},{2,6},{3,7},{4,0},{5,1},{6,2},{7,3},{8,12},{9,13},{10,... | collective-permute-start | bytes 196616 | tf_op jit(solution)/shard_map/ppermute | solution.py:647
  17.4 0.7 collective-permute-start.4
  18.1 1.9 %collective-permute-done.7 = f32[2,8,8,128]{3,2,1,0:T(8,128)S(1)} collective-permute-done((f32[2,8,8,128]{3,2,1,0:T(8,128)S(1)}, f32[2,8,8,128]{3,2,1,0:T(8,128)S(1)}, u32[]{:S(2)}, u32[]{:S(2)}) %collective-permute-start.7) | collective-permute-done | bytes 65568 | tf_op jit(solution)/shard_map/ppermute | solution.py:647
  20.0 2.4 %collective-permute-start.8 = (f32[4,8,8,128]{3,2,1,0:T(8,128)S(1)}, f32[4,8,8,128]{3,2,1,0:T(8,128)S(1)}, u32[]{:S(2)}, u32[]{:S(2)}) collective-permute-start(f32[4,8,8,128]{3,2,1,0:T(8,128)S(1)} %pad_maximum_fusion.3), channel_id=1, source_target_pairs={{0,2},{1,3},{2,0},{3,1},{4,6},{5,7},{6,4},{7,5},{8,10},{9,11},{10,... | collective-permute-start | bytes 393224 | tf_op jit(solution)/shard_map/ppermute | solution.py:647
  22.4 1.8 %shard_map.43 = (f32[224,128]{1,0:T(8,128)}, f32[224,128]{1,0:T(8,128)}) custom-call(f32[8,4,16,128]{3,2,1,0:T(8,128)} %copy-done.2, f32[8,4,16,128]{3,2,1,0:T(8,128)} %copy-done.3), custom_call_target="tpu_custom_call" | custom-call | bytes 6000000 | tf_op jit(solution)/shard_map/pallas_call | solution.py:18
  24.2 2.0 %collective-permute-start.5 = (f32[224,128]{1,0:T(8,128)}, f32[224,128]{1,0:T(8,128)S(1)}, u32[]{:S(2)}, u32[]{:S(2)}) collective-permute-start(f32[224,128]{1,0:T(8,128)} %get-tuple-element.49), channel_id=1, source_target_pairs={{0,1},{2,3},{4,5},{6,7},{1,0},{3,2},{5,4},{7,6},{8,9},{10,11},{12,... | collective-permute-start | bytes 344072 | tf_op jit(solution)/shard_map/ppermute | solution.py:798
  26.8 5.3 %collective-permute-done.8 = f32[4,8,8,128]{3,2,1,0:T(8,128)S(1)} collective-permute-done((f32[4,8,8,128]{3,2,1,0:T(8,128)S(1)}, f32[4,8,8,128]{3,2,1,0:T(8,128)S(1)}, u32[]{:S(2)}, u32[]{:S(2)}) %collective-permute-start.8) | collective-permute-done | bytes 131104 | tf_op jit(solution)/shard_map/ppermute | solution.py:647
  32.8 0.7 copy-done.9
  33.5 5.7 %shard_map.44 = (f32[2,18,2,4,8,128]{5,4,3,2,1,0:T(8,128)}, f32[2,18,2,4,8,128]{5,4,3,2,1,0:T(8,128)}, f32[2,18,2,4,8,128]{5,4,3,2,1,0:T(8,128)}, f32[8,2,4,8,12...) custom-call(f32[2,2,8,2,4,4,128]{6,5,4,3,2,1,0:T(4,128)} %get-tuple-, ...), custom_call_target="tpu_custom_call" | custom-call | bytes 18000000 | tf_op jit(solution)/shard_map/pallas_call | solution.py:18
  39.2 5.2 %collective-permute-start.9 = (f32[1,8,8,128]{3,2,1,0:T(8,128)}, f32[1,8,8,128]{3,2,1,0:T(8,128)S(1)}, u32[]{:S(2)}, u32[]{:S(2)}) collective-permute-start(f32[1,8,8,128]{3,2,1,0:T(8,128)} %bitcast.2), channel_id=1, source_target_pairs={{0,4},{1,5},{2,6},{3,7},{4,0},{5,1},{6,2},{7,3},{8,12},{9,13},{10,... | collective-permute-start | bytes 98312 | tf_op jit(solution)/shard_map/ppermute | solution.py:647
  44.4 2.1 %collective-permute-done.9 = f32[1,8,8,128]{3,2,1,0:T(8,128)S(1)} collective-permute-done((f32[1,8,8,128]{3,2,1,0:T(8,128)}, f32[1,8,8,128]{3,2,1,0:T(8,128)S(1)}, u32[]{:S(2)}, u32[]{:S(2)}) %collective-permute-start.9) | collective-permute-done | bytes 32800 | tf_op jit(solution)/shard_map/ppermute | solution.py:647
  46.6 0.8 pad_maximum_fusion.6
  47.3 1.3 %collective-permute-start.10 = (f32[2,8,8,128]{3,2,1,0:T(8,128)S(1)}, f32[2,8,8,128]{3,2,1,0:T(8,128)S(1)}, u32[]{:S(2)}, u32[]{:S(2)}) collective-permute-start(f32[2,8,8,128]{3,2,1,0:T(8,128)S(1)} %pad_maximum_fusion.6), channel_id=1, source_target_pairs={{0,2},{1,3},{2,0},{3,1},{4,6},{5,7},{6,4},{7,5},{8,10},{9,11},{10,... | collective-permute-start | bytes 196616 | tf_op jit(solution)/shard_map/ppermute | solution.py:647
  49.2 2.3 %collective-permute-done.10 = f32[2,8,8,128]{3,2,1,0:T(8,128)S(1)} collective-permute-done((f32[2,8,8,128]{3,2,1,0:T(8,128)S(1)}, f32[2,8,8,128]{3,2,1,0:T(8,128)S(1)}, u32[]{:S(2)}, u32[]{:S(2)}) %collective-permute-start.10) | collective-permute-done | bytes 65568 | tf_op jit(solution)/shard_map/ppermute | solution.py:647
  51.6 0.8 pad_maximum_fusion.4
  52.4 1.9 %collective-permute-start.13 = (f32[4,8,8,128]{3,2,1,0:T(8,128)S(1)}, f32[4,8,8,128]{3,2,1,0:T(8,128)S(1)}, u32[]{:S(2)}, u32[]{:S(2)}) collective-permute-start(f32[4,8,8,128]{3,2,1,0:T(8,128)S(1)} %pad_maximum_fusion.4), channel_id=1, source_target_pairs={{0,1},{1,0},{2,3},{3,2},{4,5},{5,4},{6,7},{7,6},{8,9},{9,8},{10,11... | collective-permute-start | bytes 393224 | tf_op jit(solution)/shard_map/ppermute | solution.py:647
  54.3 3.4 %collective-permute-start.18 = (f32[8,8,8,128]{3,2,1,0:T(8,128)S(1)}, f32[8,8,8,128]{3,2,1,0:T(8,128)S(1)}, u32[]{:S(2)}, u32[]{:S(2)}) collective-permute-start(f32[8,8,8,128]{3,2,1,0:T(8,128)S(1)} %pad_maximum_fusion.1), channel_id=1, source_target_pairs={{0,16},{1,17},{2,18},{3,19},{4,20},{5,21},{6,22},{7,23},{8,24},{9,... | collective-permute-start | bytes 786440 | tf_op jit(solution)/shard_map/ppermute | solution.py:647
  57.7 2.0 %shard_map.45 = (f32[8,2,4,8,128]{4,3,2,1,0:T(8,128)}, f32[5,2,4,8,128]{4,3,2,1,0:T(8,128)}, f32[5,2,4,8,128]{4,3,2,1,0:T(8,128)}) custom-call(f32[18,2,4,8,128]{4,3,2,1,0:T(8,128)} %get-tuple-element.58.ub, f32[160,128]{1,0:T(8,128)} %copy-done.6, f32[160,128]{1,0:T(8,128)} %copy-done.7), custom_call_target="tpu_custom_call" | custom-call | bytes 6000000 | tf_op jit(solution)/shard_map/pallas_call | solution.py:18
  59.8 2.0 %collective-permute-start.14 = (f32[8,8,8,128]{3,2,1,0:T(8,128)S(1)}, f32[8,8,8,128]{3,2,1,0:T(8,128)S(1)}, u32[]{:S(2)}, u32[]{:S(2)}) collective-permute-start(f32[8,8,8,128]{3,2,1,0:T(8,128)S(1)} %pad_maximum_fusion.2), channel_id=1, source_target_pairs={{0,16},{1,17},{2,18},{3,19},{4,20},{5,21},{6,22},{7,23},{8,24},{9,... | collective-permute-start | bytes 786440 | tf_op jit(solution)/shard_map/ppermute | solution.py:647
  61.8 1.1 %collective-permute-start.15 = (f32[5,2,4,8,128]{4,3,2,1,0:T(8,128)}, f32[5,2,4,8,128]{4,3,2,1,0:T(8,128)S(1)}, u32[]{:S(2)}, u32[]{:S(2)}) collective-permute-start(f32[5,2,4,8,128]{4,3,2,1,0:T(8,128)} %get-tuple-element.70), channel_id=1, source_target_pairs={{0,1},{2,3},{4,5},{6,7},{1,0},{3,2},{5,4},{7,6},{8,9},{10,11},{12,... | collective-permute-start | bytes 491528 | tf_op jit(solution)/shard_map/ppermute | solution.py:798
  63.5 1.3 %collective-permute-done.18 = f32[8,8,8,128]{3,2,1,0:T(8,128)S(1)} collective-permute-done((f32[8,8,8,128]{3,2,1,0:T(8,128)S(1)}, f32[8,8,8,128]{3,2,1,0:T(8,128)S(1)}, u32[]{:S(2)}, u32[]{:S(2)}) %collective-permute-start.18) | collective-permute-done | bytes 262176 | tf_op jit(solution)/shard_map/ppermute | solution.py:647
  65.0 5.5 %collective-permute-done.14 = f32[8,8,8,128]{3,2,1,0:T(8,128)S(1)} collective-permute-done((f32[8,8,8,128]{3,2,1,0:T(8,128)S(1)}, f32[8,8,8,128]{3,2,1,0:T(8,128)S(1)}, u32[]{:S(2)}, u32[]{:S(2)}) %collective-permute-start.14) | collective-permute-done | bytes 262176 | tf_op jit(solution)/shard_map/ppermute | solution.py:647
  70.6 1.9 %collective-permute-done.17.ftheirs = f32[16,8,8,128]{3,2,1,0:T(8,128)S(1)} collective-permute-done((f32[16,8,8,128]{3,2,1,0:T(8,128)S(1)}, f32[16,8,8,128]{3,2,1,0:T(8,128)S(1)}, u32[]{:S(2)}, u32[]{:S(2)}) %collective-permute-start.17) | collective-permute-done | bytes 524320 | tf_op jit(solution)/shard_map/ppermute | solution.py:647
  72.5 0.8 copy-done.5
  73.3 11.5 %shard_map.46 = (f32[10,4,8,128]{3,2,1,0:T(8,128)}, f32[2,4,4,128]{3,2,1,0:T(4,128)}) custom-call(f32[16,8,8,128]{3,2,1,0:T(8,128)} %copy-done, f32[16,8,8,128]{3,2,1,0:T(8,128)} %copy-done.5, f32[16,8,8,128]{3,2,1,0:T(8,128)} %copy-done.1, f32[16,8,8,128]{3,2,1,0:T(8,128)} %copy-done.4), custom_call_target="tpu_custom_call" | custom-call | bytes 33000000 | tf_op jit(solution)/shard_map/pallas_call | solution.py:18
  84.8 5.8 %shard_map.47 = (f32[8,8,1024]{2,1,0:T(8,128)}, f32[8,8,1024]{2,1,0:T(8,128)}) custom-call(f32[2,18,2,4,8,128]{5,4,3,2,1,0:T(8,128)} %get-tuple-element.54.k, f32[2,18,2,4,8,128]{5,4,3,2,1,0:T(8,128)} %get-tuple-element.55.g, f32[2,18,2,4,8,128]{5,4,3,2,1,0:T(8,128)} %get-tuple-element.56.fs, f32[8,2,4,8,128]{4,3,2,1,0:T(8,128)} %get-tuple-element.57.half, ...), custom_call_target="tpu_custom_call" | custom-call | bytes 18000000 | tf_op jit(solution)/shard_map/pallas_call | solution.py:18
  (52 shorter events, 3.1 us)
Async XLA Ops:
  3.9 10.8 %collective-permute-start = (f32[16,2,4,4,128]{4,3,2,1,0:T(4,128)}, f32[16,2,4,4,128]{4,3,2,1,0:T(4,128)S(1)}, u32[]{:S(2)}, u32[]{:S(2)}) collective-permute-start(f32[16,2,4,4,128]{4,3,2,1,0:T(4,128)} %get-tuple-element.41), channel_id=1, source_target_pairs={{0,1},{2,3},{4,5},{6,7},{1,0},{3,2},{5,4},{7,6},{8,9},{10,11},{12,... | collective-permute-start | bytes 786440 | tf_op jit(solution)/shard_map/ppermute | solution.py:798
  9.1 5.6 %collective-permute-start.1 = (f32[8,4,16,128]{3,2,1,0:T(8,128)}, f32[8,4,16,128]{3,2,1,0:T(8,128)S(1)}, u32[]{:S(2)}, u32[]{:S(2)}) collective-permute-start(f32[8,4,16,128]{3,2,1,0:T(8,128)} %get-tuple-element.42), channel_id=1, source_target_pairs={{0,8},{16,24},{8,0},{24,16},{1,9},{17,25},{9,1},{25,17},{2,10},{18... | collective-permute-start | bytes 786440 | tf_op jit(solution)/shard_map/ppermute | solution.py:798
  9.1 5.7 %collective-permute-start.2 = (f32[8,4,16,128]{3,2,1,0:T(8,128)}, f32[8,4,16,128]{3,2,1,0:T(8,128)S(1)}, u32[]{:S(2)}, u32[]{:S(2)}) collective-permute-start(f32[8,4,16,128]{3,2,1,0:T(8,128)} %get-tuple-element.43), channel_id=1, source_target_pairs={{8,16},{16,8},{9,17},{17,9},{10,18},{18,10},{11,19},{19,11},{12,20... | collective-permute-start | bytes 786440 | tf_op jit(solution)/shard_map/ppermute | solution.py:798
  9.8 4.2 %collective-permute-start.3 = (f32[1,8,8,128]{3,2,1,0:T(8,128)}, f32[1,8,8,128]{3,2,1,0:T(8,128)S(1)}, u32[]{:S(2)}, u32[]{:S(2)}) collective-permute-start(f32[1,8,8,128]{3,2,1,0:T(8,128)} %bitcast.5), channel_id=1, source_target_pairs={{0,1},{1,0},{2,3},{3,2},{4,5},{5,4},{6,7},{7,6},{8,9},{9,8},{10,11... | collective-permute-start | bytes 98312 | tf_op jit(solution)/shard_map/ppermute | solution.py:647
  14.7 17.4 %copy-start.8 = (f32[16,2,4,4,128]{4,3,2,1,0:T(4,128)}, f32[16,2,4,4,128]{4,3,2,1,0:T(4,128)S(1)}, u32[]{:S(2)}) copy-start(f32[16,2,4,4,128]{4,3,2,1,0:T(4,128)S(1)} %collective-permute-done.ya) | copy-start | bytes 786436
  14.8 7.6 %copy-start.2 = (f32[8,4,16,128]{3,2,1,0:T(8,128)}, f32[8,4,16,128]{3,2,1,0:T(8,128)S(1)}, u32[]{:S(2)}) copy-start(f32[8,4,16,128]{3,2,1,0:T(8,128)S(1)} %collective-permute-done.1.za_far.za) | copy-start | bytes 786436
  14.8 7.6 %copy-start.3 = (f32[8,4,16,128]{3,2,1,0:T(8,128)}, f32[8,4,16,128]{3,2,1,0:T(8,128)S(1)}, u32[]{:S(2)}) copy-start(f32[8,4,16,128]{3,2,1,0:T(8,128)S(1)} %collective-permute-done.2.zb_far.zb) | copy-start | bytes 786436
  14.8 5.2 %collective-permute-start.7 = (f32[2,8,8,128]{3,2,1,0:T(8,128)S(1)}, f32[2,8,8,128]{3,2,1,0:T(8,128)S(1)}, u32[]{:S(2)}, u32[]{:S(2)}) collective-permute-start(f32[2,8,8,128]{3,2,1,0:T(8,128)S(1)} %pad_maximum_fusion.5), channel_id=1, source_target_pairs={{0,4},{1,5},{2,6},{3,7},{4,0},{5,1},{6,2},{7,3},{8,12},{9,13},{10,... | collective-permute-start | bytes 196616 | tf_op jit(solution)/shard_map/ppermute | solution.py:647
  17.4 14.7 %collective-permute-start.4 = (f32[16,2,4,4,128]{4,3,2,1,0:T(4,128)}, f32[16,2,4,4,128]{4,3,2,1,0:T(4,128)S(1)}, u32[]{:S(2)}, u32[]{:S(2)}) collective-permute-start(f32[16,2,4,4,128]{4,3,2,1,0:T(4,128)} %get-tuple-element.46), channel_id=1, source_target_pairs={{1,2},{3,4},{5,6},{2,1},{4,3},{6,5},{9,10},{11,12},{13,14},{10,9},... | collective-permute-start | bytes 786440 | tf_op jit(solution)/shard_map/ppermute | solution.py:798
  20.0 12.0 %collective-permute-start.8 = (f32[4,8,8,128]{3,2,1,0:T(8,128)S(1)}, f32[4,8,8,128]{3,2,1,0:T(8,128)S(1)}, u32[]{:S(2)}, u32[]{:S(2)}) collective-permute-start(f32[4,8,8,128]{3,2,1,0:T(8,128)S(1)} %pad_maximum_fusion.3), channel_id=1, source_target_pairs={{0,2},{1,3},{2,0},{3,1},{4,6},{5,7},{6,4},{7,5},{8,10},{9,11},{10,... | collective-permute-start | bytes 393224 | tf_op jit(solution)/shard_map/ppermute | solution.py:647
  24.2 7.9 %collective-permute-start.5 = (f32[224,128]{1,0:T(8,128)}, f32[224,128]{1,0:T(8,128)S(1)}, u32[]{:S(2)}, u32[]{:S(2)}) collective-permute-start(f32[224,128]{1,0:T(8,128)} %get-tuple-element.49), channel_id=1, source_target_pairs={{0,1},{2,3},{4,5},{6,7},{1,0},{3,2},{5,4},{7,6},{8,9},{10,11},{12,... | collective-permute-start | bytes 344072 | tf_op jit(solution)/shard_map/ppermute | solution.py:798
  26.1 6.0 %collective-permute-start.6 = (f32[224,128]{1,0:T(8,128)}, f32[224,128]{1,0:T(8,128)S(1)}, u32[]{:S(2)}, u32[]{:S(2)}) collective-permute-start(f32[224,128]{1,0:T(8,128)} %get-tuple-element.50), channel_id=1, source_target_pairs={{1,2},{3,4},{5,6},{2,1},{4,3},{6,5},{9,10},{11,12},{13,14},{10,9},... | collective-permute-start | bytes 344072 | tf_op jit(solution)/shard_map/ppermute | solution.py:798
  32.8 0.7 copy-start.9
  39.2 7.4 %collective-permute-start.9 = (f32[1,8,8,128]{3,2,1,0:T(8,128)}, f32[1,8,8,128]{3,2,1,0:T(8,128)S(1)}, u32[]{:S(2)}, u32[]{:S(2)}) collective-permute-start(f32[1,8,8,128]{3,2,1,0:T(8,128)} %bitcast.2), channel_id=1, source_target_pairs={{0,4},{1,5},{2,6},{3,7},{4,0},{5,1},{6,2},{7,3},{8,12},{9,13},{10,... | collective-permute-start | bytes 98312 | tf_op jit(solution)/shard_map/ppermute | solution.py:647
  47.3 4.3 %collective-permute-start.10 = (f32[2,8,8,128]{3,2,1,0:T(8,128)S(1)}, f32[2,8,8,128]{3,2,1,0:T(8,128)S(1)}, u32[]{:S(2)}, u32[]{:S(2)}) collective-permute-start(f32[2,8,8,128]{3,2,1,0:T(8,128)S(1)} %pad_maximum_fusion.6), channel_id=1, source_target_pairs={{0,2},{1,3},{2,0},{3,1},{4,6},{5,7},{6,4},{7,5},{8,10},{9,11},{10,... | collective-permute-start | bytes 196616 | tf_op jit(solution)/shard_map/ppermute | solution.py:647
  48.6 3.8 %collective-permute-start.11 = (f32[160,128]{1,0:T(8,128)}, f32[160,128]{1,0:T(8,128)S(1)}, u32[]{:S(2)}, u32[]{:S(2)}) collective-permute-start(f32[160,128]{1,0:T(8,128)} %get-tuple-element.60), channel_id=1, source_target_pairs={{0,8},{16,24},{8,0},{24,16},{1,9},{17,25},{9,1},{25,17},{2,10},{18... | collective-permute-start | bytes 245768 | tf_op jit(solution)/shard_map/ppermute | solution.py:798
  48.6 3.8 %collective-permute-start.12 = (f32[160,128]{1,0:T(8,128)}, f32[160,128]{1,0:T(8,128)S(1)}, u32[]{:S(2)}, u32[]{:S(2)}) collective-permute-start(f32[160,128]{1,0:T(8,128)} %get-tuple-element.61), channel_id=1, source_target_pairs={{8,16},{16,8},{9,17},{17,9},{10,18},{18,10},{11,19},{19,11},{12,20... | collective-permute-start | bytes 245768 | tf_op jit(solution)/shard_map/ppermute | solution.py:798
  52.4 5.3 %copy-start.6 = (f32[160,128]{1,0:T(8,128)}, f32[160,128]{1,0:T(8,128)S(1)}, u32[]{:S(2)}) copy-start(f32[160,128]{1,0:T(8,128)S(1)} %collective-permute-done.11.zc) | copy-start | bytes 245764
  52.4 5.3 %copy-start.7 = (f32[160,128]{1,0:T(8,128)}, f32[160,128]{1,0:T(8,128)S(1)}, u32[]{:S(2)}) copy-start(f32[160,128]{1,0:T(8,128)S(1)} %collective-permute-done.12.zd) | copy-start | bytes 245764
  52.4 7.3 %collective-permute-start.13 = (f32[4,8,8,128]{3,2,1,0:T(8,128)S(1)}, f32[4,8,8,128]{3,2,1,0:T(8,128)S(1)}, u32[]{:S(2)}, u32[]{:S(2)}) collective-permute-start(f32[4,8,8,128]{3,2,1,0:T(8,128)S(1)} %pad_maximum_fusion.4), channel_id=1, source_target_pairs={{0,1},{1,0},{2,3},{3,2},{4,5},{5,4},{6,7},{7,6},{8,9},{9,8},{10,11... | collective-permute-start | bytes 393224 | tf_op jit(solution)/shard_map/ppermute | solution.py:647
  54.3 10.5 %collective-permute-start.18 = (f32[8,8,8,128]{3,2,1,0:T(8,128)S(1)}, f32[8,8,8,128]{3,2,1,0:T(8,128)S(1)}, u32[]{:S(2)}, u32[]{:S(2)}) collective-permute-start(f32[8,8,8,128]{3,2,1,0:T(8,128)S(1)} %pad_maximum_fusion.1), channel_id=1, source_target_pairs={{0,16},{1,17},{2,18},{3,19},{4,20},{5,21},{6,22},{7,23},{8,24},{9,... | collective-permute-start | bytes 786440 | tf_op jit(solution)/shard_map/ppermute | solution.py:647
  59.8 10.7 %collective-permute-start.14 = (f32[8,8,8,128]{3,2,1,0:T(8,128)S(1)}, f32[8,8,8,128]{3,2,1,0:T(8,128)S(1)}, u32[]{:S(2)}, u32[]{:S(2)}) collective-permute-start(f32[8,8,8,128]{3,2,1,0:T(8,128)S(1)} %pad_maximum_fusion.2), channel_id=1, source_target_pairs={{0,16},{1,17},{2,18},{3,19},{4,20},{5,21},{6,22},{7,23},{8,24},{9,... | collective-permute-start | bytes 786440 | tf_op jit(solution)/shard_map/ppermute | solution.py:647
  61.8 8.7 %collective-permute-start.15 = (f32[5,2,4,8,128]{4,3,2,1,0:T(8,128)}, f32[5,2,4,8,128]{4,3,2,1,0:T(8,128)S(1)}, u32[]{:S(2)}, u32[]{:S(2)}) collective-permute-start(f32[5,2,4,8,128]{4,3,2,1,0:T(8,128)} %get-tuple-element.70), channel_id=1, source_target_pairs={{0,1},{2,3},{4,5},{6,7},{1,0},{3,2},{5,4},{7,6},{8,9},{10,11},{12,... | collective-permute-start | bytes 491528 | tf_op jit(solution)/shard_map/ppermute | solution.py:798
  62.8 7.7 %collective-permute-start.16 = (f32[5,2,4,8,128]{4,3,2,1,0:T(8,128)}, f32[5,2,4,8,128]{4,3,2,1,0:T(8,128)S(1)}, u32[]{:S(2)}, u32[]{:S(2)}) collective-permute-start(f32[5,2,4,8,128]{4,3,2,1,0:T(8,128)} %get-tuple-element.71), channel_id=1, source_target_pairs={{1,2},{3,4},{5,6},{2,1},{4,3},{6,5},{9,10},{11,12},{13,14},{10,9},... | collective-permute-start | bytes 491528 | tf_op jit(solution)/shard_map/ppermute | solution.py:798
  64.9 7.6 %copy-start.1 = (f32[16,8,8,128]{3,2,1,0:T(8,128)}, f32[16,8,8,128]{3,2,1,0:T(8,128)S(1)}, u32[]{:S(2)}) copy-start(f32[16,8,8,128]{3,2,1,0:T(8,128)S(1)} %constant_dynamic-update-slice_fusion.kmine) | copy-start | bytes 1572868
  64.9 5.7 %collective-permute-start.19 = (f32[16,8,8,128]{3,2,1,0:T(8,128)S(1)}, f32[16,8,8,128]{3,2,1,0:T(8,128)S(1)}, u32[]{:S(2)}, u32[]{:S(2)}) collective-permute-start(f32[16,8,8,128]{3,2,1,0:T(8,128)S(1)} %constant_dynamic-update-slice_fusion.kmine), channel_id=1, source_target_pairs={{0,8},{1,9},{2,10},{3,11},{4,12},{5,13},{6,14},{7,15},{8,0},{9,1},... | collective-permute-start | bytes 1572872 | tf_op jit(solution)/shard_map/ppermute | solution.py:647
  70.5 2.0 %copy-start = (f32[16,8,8,128]{3,2,1,0:T(8,128)}, f32[16,8,8,128]{3,2,1,0:T(8,128)S(1)}, u32[]{:S(2)}) copy-start(f32[16,8,8,128]{3,2,1,0:T(8,128)S(1)} %pad_maximum_fusion.fmine) | copy-start | bytes 1572868
  70.5 14.3 %copy-start.10 = (f32[5,2,4,8,128]{4,3,2,1,0:T(8,128)}, f32[5,2,4,8,128]{4,3,2,1,0:T(8,128)S(1)}, u32[]{:S(2)}) copy-start(f32[5,2,4,8,128]{4,3,2,1,0:T(8,128)S(1)} %collective-permute-done.15.yc) | copy-start | bytes 491524
  70.5 14.3 %copy-start.11 = (f32[5,2,4,8,128]{4,3,2,1,0:T(8,128)}, f32[5,2,4,8,128]{4,3,2,1,0:T(8,128)S(1)}, u32[]{:S(2)}) copy-start(f32[5,2,4,8,128]{4,3,2,1,0:T(8,128)S(1)} %collective-permute-done.16.yd) | copy-start | bytes 491524
  70.5 2.0 %collective-permute-start.17 = (f32[16,8,8,128]{3,2,1,0:T(8,128)S(1)}, f32[16,8,8,128]{3,2,1,0:T(8,128)S(1)}, u32[]{:S(2)}, u32[]{:S(2)}) collective-permute-start(f32[16,8,8,128]{3,2,1,0:T(8,128)S(1)} %pad_maximum_fusion.fmine), channel_id=1, source_target_pairs={{0,8},{1,9},{2,10},{3,11},{4,12},{5,13},{6,14},{7,15},{8,0},{9,1},... | collective-permute-start | bytes 1572872 | tf_op jit(solution)/shard_map/ppermute | solution.py:647
  70.6 1.9 %copy-start.4 = (f32[16,8,8,128]{3,2,1,0:T(8,128)}, f32[16,8,8,128]{3,2,1,0:T(8,128)S(1)}, u32[]{:S(2)}) copy-start(f32[16,8,8,128]{3,2,1,0:T(8,128)S(1)} %collective-permute-done.19.ktheirs) | copy-start | bytes 1572868
  72.5 0.8 copy-start.5
  (2 other events, 1.3 us)

commit v3 on v2

--- a/solution.py
+++ b/solution.py
@@ -126,21 +126,25 @@
             put_coarse(coarse, row, s, total * 0.125)
 
 
-def relay_kernel(za_far, zb_far, ca, cb, za, zb, sem):
-    zabove, yup = own_sides()
-    copies = [pltpu.make_async_copy(*pair, sem.at[i]) for i, pair in enumerate(((za_far, za), (zb_far, zb)))]
+def relay_kernel(ya_far, yb_far, ca, cb, faces, sem):
+    zup, yabove = own_sides()
+    slots = pick(yabove, 0, 1)
+    copies = [pltpu.make_async_copy(f, faces.at[t], sem.at[i]) for i, (f, t) in enumerate(zip((ya_far, yb_far), slots))]
     for copy in copies:
         copy.start()
     for copy in copies:
         copy.wait()
-    for target, up in ((ca, yup), (cb, jnp.logical_not(yup))):
-        for d, (_, at, rows) in CORNER.items():
-            y = jnp.where(up, 8 - d, d - 1)
-            for s in range(4):
-                parts = pick(zabove, za[y, s, 0:rows], zb[y, s, 0:rows])
+    for target, up in ((ca, zup), (cb, jnp.logical_not(zup))):
+        places = {d: jnp.where(up, 8 - d, d - 1) for d in range(1, 5)}
+        for d, (count, at, _) in CORNER.items():
+            for i, (a, c, dz) in enumerate(ZFACE[:count]):
+                e, t = lax.rem(places[dz], 2), places[dz] // 2
                 for side in range(2):
-                    base = (4 * side + s) * CORNER_ROWS + at
-                    target[base : base + rows, :] = parts[side]
+                    y = d - 1 if side == 0 else REACH[2 * a + c][2] - d
+                    line = YFACE.index((a, c, y, REACH[2 * a + c][2]))
+                    for s in range(4):
+                        base = (4 * side + s) * CORNER_ROWS + at + i
+                        target[base : base + 1, :] = faces[side, line, e, s, pl.ds(t, 1)]
 
 
 def neighbours(ref, line, e, s, q, groups, edge=None, first=None, last=None):
@@ -223,14 +227,14 @@
             for s in range(4):
                 both[a][c, first, e, s, 0:4] = ya[i, e, s]
                 both[a][c, second, e, s, 0:4] = yb[i, e, s]
-    for d, (count, at, _) in CORNER.items():
-        for message, line in zip((ca, cb), pick(yabove, PAD + 7 + d, PAD - d)):
-            for side in range(2):
-                for i, (a, c, dz) in enumerate(ZFACE[:count]):
-                    e, row = halo_cell(side, dz)
-                    for s in range(4):
-                        base = (4 * side + s) * CORNER_ROWS + at + i
-                        both[a][c, line, e, s, row : row + 1] = message[base : base + 1, :]
+    for yside in range(2):
+        for s in range(4):
+            for d, (count, at, _) in CORNER.items():
+                line, base = PAD + 7 + d if yside == 0 else PAD - d, (4 * yside + s) * CORNER_ROWS + at
+                for side, part in enumerate(pick(zabove, ca[base : base + count, :], cb[base : base + count, :])):
+                    for i, (a, c, dz) in enumerate(ZFACE[:count]):
+                        e, row = halo_cell(side, dz)
+                        both[a][c, line, e, s, row : row + 1] = part[i : i + 1]
 
     rows = iota(0)
 
@@ -816,22 +820,24 @@
     kall = kmessage[None]
     if whole:
         kall = swapped(kall, kswaps[0], nz, ny)
-        ya, za, zb, kall = lax.optimization_barrier((ya, za, zb, kall))
+        ya, yb, kall = lax.optimization_barrier((ya, yb, kall))
     relayed = (8 * CORNER_ROWS, LANES)
-    scratch = [zface, zface, pltpu.SemaphoreType.DMA((2,))]
+    scratch = [(2, *yface), pltpu.SemaphoreType.DMA((2,))]
     far = [pl.BlockSpec(memory_space=pl.ANY)] * 2
-    ca, cb = exchange(*call(relay_kernel, 2, (relayed, relayed), scratch, za, zb, specs=far), "gy")
+    ca, cb = exchange(*call(relay_kernel, 2, (relayed, relayed), scratch, ya, yb, specs=far), "gz")
     if whole:
         for step in kswaps[1:-2]:
             kall = swapped(kall, step, nz, ny)
-        ca, cb, kall = lax.optimization_barrier((ca, cb, kall))
+        ca, cb, za, zb, kall = lax.optimization_barrier((ca, cb, za, zb, kall))
         kall = swapped(kall, kswaps[-2], nz, ny)
-        ktheirs = swap(kall, kswaps[-1], nz, ny)
     lines, zface = (LINES, 2, 4, 8, LANES), (160, LANES)
     outs = ((2, *lines), (2, *lines), (2, *lines), (8, *lines[1:]), lines, (2, 8, 4, LANES), zface, zface, coarse)
     scratch = [(2, *lines), lines, lines, lines]
     k, g, fs, half, ub, kx, zc, zd, message = call(down_kernel, 6, outs, scratch, local, ya, yb, za, zb, ca, cb)
     fall, half_way = message[None], len(swaps) // 2
+    if whole:
+        fall, kall = lax.optimization_barrier((fall, kall))
+        ktheirs = swap(kall, kswaps[-1], nz, ny)
     zc, zd = exchange(zc, zd, "gz")
     if whole:
         for step in swaps[:half_way]:

time: 91.2 us -> 91.7 us (level)
  starting transfers between devices: 28.3 us -> 30.3 us
  local copies, waits for them, and re-layouts: 2.24 us -> 0.87 us
    ppermute x10, starting transfers between devices: 19.1 us -> 21.7 us  [swap(): lax.ppermute(block, ('gz', 'gy'), [(i, i ^ 1 << step) for i in range(nz *...]
    unnamed x29 -> x34, local copies, waits for them, and re-layouts: 2.22 us -> 0.87 us
    concatenate x7 -> x8, other arithmetic: 2.38 us -> 1.66 us  [swapped(): return jnp.concatenate([block, swap(block, step, nz, ny)])]
  transfers between devices with their start and end apart: 20 -> 20, of which waited for: 8 -> 10; matrix products, arithmetic and copies ran while one was open for 2% -> 1% of each run, Pallas kernels for 7% -> 13%
where the time goes in v3:
time: 91.7 us; the launch traced here: 90.7 us
  Pallas kernels  32.5 us (35%)
  starting transfers between devices  30.3 us (33%)
  waiting for transfers between devices  24.4 us (27%)
  other arithmetic  1.66 us (2%)
  between operations  0.93 us (1%)
    pallas_call x7, Pallas kernels, call(): pl.pallas_call(body, out_shape=[jax.ShapeDtypeStruct(s, F32) for s in out...  32.5 us
    ppermute x10, waiting for transfers between devices, swap(): lax.ppermute(block, ('gz', 'gy'), [(i, i ^ 1 << step) for i in range(nz *...  23.6 us
    ppermute x10, starting transfers between devices, swap(): lax.ppermute(block, ('gz', 'gy'), [(i, i ^ 1 << step) for i in range(nz *...  21.7 us
    ppermute x10, starting transfers between devices, exchange(): lax.ppermute(message, axis, pairs + [(j, i) for i, j in pairs])  8.65 us
  transfers between devices with their start and end apart: 20, of which 10 were waited for; matrix products, arithmetic and copies ran while one was open for 1% of the time, Pallas kernels for 13%

profile of v3, /device:TPU:0, one launch (start us, length us, event | category | flops | bytes accessed | tf_op | source)
XLA Modules:
  0.0 90.7 jit_solution(10264913604093938631)
XLA Ops:
  0.6 3.3 %shard_map.41 = (f32[2,2,8,2,4,4,128]{6,5,4,3,2,1,0:T(4,128)}, f32[16,2,4,4,128]{4,3,2,1,0:T(4,128)}, f32[16,2,4,4,128]{4,3,2,1,0:T(4,128)}) custom-call(f32[8,8,1024]{2,1,0:T(8,128)} %f_ref.1, f32[8,8,1024]{2,1,0:T(8,128)} %k_ref.1), custom_call_target="tpu_custom_call" | custom-call | bytes 9000000 | tf_op jit(solution)/shard_map/pallas_call | solution.py:18
  3.9 2.9 %collective-permute-start = (f32[16,2,4,4,128]{4,3,2,1,0:T(4,128)}, f32[16,2,4,4,128]{4,3,2,1,0:T(4,128)S(1)}, u32[]{:S(2)}, u32[]{:S(2)}) collective-permute-start(f32[16,2,4,4,128]{4,3,2,1,0:T(4,128)} %get-tuple-element.44), channel_id=1, source_target_pairs={{0,1},{2,3},{4,5},{6,7},{1,0},{3,2},{5,4},{7,6},{8,9},{10,11},{12,... | collective-permute-start | bytes 786440 | tf_op jit(solution)/shard_map/ppermute | solution.py:802
  7.5 2.3 %shard_map.42 = (f32[8,4,16,128]{3,2,1,0:T(8,128)}, f32[8,4,16,128]{3,2,1,0:T(8,128)}, f32[8,8,128]{2,1,0:T(8,128)}) custom-call(f32[2,2,8,2,4,4,128]{6,5,4,3,2,1,0:T(4,128)} %get-tuple-element.43.local), custom_call_target="tpu_custom_call" | custom-call | bytes 6000000 | tf_op jit(solution)/shard_map/pallas_call | solution.py:18
  9.8 4.3 %collective-permute-start.2 = (f32[1,8,8,128]{3,2,1,0:T(8,128)}, f32[1,8,8,128]{3,2,1,0:T(8,128)S(1)}, u32[]{:S(2)}, u32[]{:S(2)}) collective-permute-start(f32[1,8,8,128]{3,2,1,0:T(8,128)} %bitcast.5), channel_id=1, source_target_pairs={{0,1},{1,0},{2,3},{3,2},{4,5},{5,4},{6,7},{7,6},{8,9},{9,8},{10,11... | collective-permute-start | bytes 98312 | tf_op jit(solution)/shard_map/ppermute | solution.py:651
  14.1 5.0 %collective-permute-done.2 = f32[1,8,8,128]{3,2,1,0:T(8,128)S(1)} collective-permute-done((f32[1,8,8,128]{3,2,1,0:T(8,128)}, f32[1,8,8,128]{3,2,1,0:T(8,128)S(1)}, u32[]{:S(2)}, u32[]{:S(2)}) %collective-permute-start.2) | collective-permute-done | bytes 32800 | tf_op jit(solution)/shard_map/ppermute | solution.py:651
  19.1 0.8 pad_maximum_fusion.6
  19.9 3.5 %collective-permute-start.7 = (f32[2,8,8,128]{3,2,1,0:T(8,128)S(1)}, f32[2,8,8,128]{3,2,1,0:T(8,128)S(1)}, u32[]{:S(2)}, u32[]{:S(2)}) collective-permute-start(f32[2,8,8,128]{3,2,1,0:T(8,128)S(1)} %pad_maximum_fusion.6), channel_id=1, source_target_pairs={{0,4},{1,5},{2,6},{3,7},{4,0},{5,1},{6,2},{7,3},{8,12},{9,13},{10,... | collective-permute-start | bytes 196616 | tf_op jit(solution)/shard_map/ppermute | solution.py:651
  23.4 0.7 collective-permute-start.6
  24.1 1.6 %collective-permute-done.7 = f32[2,8,8,128]{3,2,1,0:T(8,128)S(1)} collective-permute-done((f32[2,8,8,128]{3,2,1,0:T(8,128)S(1)}, f32[2,8,8,128]{3,2,1,0:T(8,128)S(1)}, u32[]{:S(2)}, u32[]{:S(2)}) %collective-permute-start.7) | collective-permute-done | bytes 65568 | tf_op jit(solution)/shard_map/ppermute | solution.py:651
  25.7 1.9 %collective-permute-start.8 = (f32[4,8,8,128]{3,2,1,0:T(8,128)S(1)}, f32[4,8,8,128]{3,2,1,0:T(8,128)S(1)}, u32[]{:S(2)}, u32[]{:S(2)}) collective-permute-start(f32[4,8,8,128]{3,2,1,0:T(8,128)S(1)} %pad_maximum_fusion.4), channel_id=1, source_target_pairs={{0,2},{1,3},{2,0},{3,1},{4,6},{5,7},{6,4},{7,5},{8,10},{9,11},{10,... | collective-permute-start | bytes 393224 | tf_op jit(solution)/shard_map/ppermute | solution.py:651
  27.6 1.9 %shard_map.43 = (f32[224,128]{1,0:T(8,128)}, f32[224,128]{1,0:T(8,128)}) custom-call(f32[16,2,4,4,128]{4,3,2,1,0:T(4,128)} %copy-done.2, f32[16,2,4,4,128]{4,3,2,1,0:T(4,128)} %copy-done.3), custom_call_target="tpu_custom_call" | custom-call | bytes 6000000 | tf_op jit(solution)/shard_map/pallas_call | solution.py:18
  29.5 0.8 collective-permute-start.3
  31.0 0.9 collective-permute-done.8
  31.9 5.5 %collective-permute-start.9 = (f32[8,8,8,128]{3,2,1,0:T(8,128)S(1)}, f32[8,8,8,128]{3,2,1,0:T(8,128)S(1)}, u32[]{:S(2)}, u32[]{:S(2)}) collective-permute-start(f32[8,8,8,128]{3,2,1,0:T(8,128)S(1)} %pad_maximum_fusion.2), channel_id=1, source_target_pairs={{0,16},{1,17},{2,18},{3,19},{4,20},{5,21},{6,22},{7,23},{8,24},{9,... | collective-permute-start | bytes 786440 | tf_op jit(solution)/shard_map/ppermute | solution.py:651
  37.5 5.7 %shard_map.44 = (f32[2,18,2,4,8,128]{5,4,3,2,1,0:T(8,128)}, f32[2,18,2,4,8,128]{5,4,3,2,1,0:T(8,128)}, f32[2,18,2,4,8,128]{5,4,3,2,1,0:T(8,128)}, f32[8,2,4,8,12...) custom-call(f32[2,2,8,2,4,4,128]{6,5,4,3,2,1,0:T(4,128)} %get-tuple-, ...), custom_call_target="tpu_custom_call" | custom-call | bytes 18000000 | tf_op jit(solution)/shard_map/pallas_call | solution.py:18
  43.2 1.2 %collective-permute-done.9 = f32[8,8,8,128]{3,2,1,0:T(8,128)S(1)} collective-permute-done((f32[8,8,8,128]{3,2,1,0:T(8,128)S(1)}, f32[8,8,8,128]{3,2,1,0:T(8,128)S(1)}, u32[]{:S(2)}, u32[]{:S(2)}) %collective-permute-start.9) | collective-permute-done | bytes 262176 | tf_op jit(solution)/shard_map/ppermute | solution.py:651
  44.4 3.5 %collective-permute-start.10 = (f32[1,8,8,128]{3,2,1,0:T(8,128)}, f32[1,8,8,128]{3,2,1,0:T(8,128)S(1)}, u32[]{:S(2)}, u32[]{:S(2)}) collective-permute-start(f32[1,8,8,128]{3,2,1,0:T(8,128)} %bitcast.2), channel_id=1, source_target_pairs={{0,4},{1,5},{2,6},{3,7},{4,0},{5,1},{6,2},{7,3},{8,12},{9,13},{10,... | collective-permute-start | bytes 98312 | tf_op jit(solution)/shard_map/ppermute | solution.py:651
  47.9 2.2 %collective-permute-done.10 = f32[1,8,8,128]{3,2,1,0:T(8,128)S(1)} collective-permute-done((f32[1,8,8,128]{3,2,1,0:T(8,128)}, f32[1,8,8,128]{3,2,1,0:T(8,128)S(1)}, u32[]{:S(2)}, u32[]{:S(2)}) %collective-permute-start.10) | collective-permute-done | bytes 32800 | tf_op jit(solution)/shard_map/ppermute | solution.py:651
  50.1 0.8 pad_maximum_fusion.7
  51.0 0.7 collective-permute-start.13
  51.7 3.5 %collective-permute-done.11 = f32[2,8,8,128]{3,2,1,0:T(8,128)S(1)} collective-permute-done((f32[2,8,8,128]{3,2,1,0:T(8,128)S(1)}, f32[2,8,8,128]{3,2,1,0:T(8,128)S(1)}, u32[]{:S(2)}, u32[]{:S(2)}) %collective-permute-start.11) | collective-permute-done | bytes 65568 | tf_op jit(solution)/shard_map/ppermute | solution.py:651
  55.2 1.2 %collective-permute-start.14 = (f32[4,8,8,128]{3,2,1,0:T(8,128)S(1)}, f32[4,8,8,128]{3,2,1,0:T(8,128)S(1)}, u32[]{:S(2)}, u32[]{:S(2)}) collective-permute-start(f32[4,8,8,128]{3,2,1,0:T(8,128)S(1)} %pad_maximum_fusion.5), channel_id=1, source_target_pairs={{0,1},{1,0},{2,3},{3,2},{4,5},{5,4},{6,7},{7,6},{8,9},{9,8},{10,11... | collective-permute-start | bytes 393224 | tf_op jit(solution)/shard_map/ppermute | solution.py:651
  56.4 2.0 %shard_map.45 = (f32[8,2,4,8,128]{4,3,2,1,0:T(8,128)}, f32[5,2,4,8,128]{4,3,2,1,0:T(8,128)}, f32[5,2,4,8,128]{4,3,2,1,0:T(8,128)}) custom-call(f32[18,2,4,8,128]{4,3,2,1,0:T(8,128)} %get-tuple-element.62.ub, f32[160,128]{1,0:T(8,128)} %copy-done.6, f32[160,128]{1,0:T(8,128)} %copy-done.7), custom_call_target="tpu_custom_call" | custom-call | bytes 6000000 | tf_op jit(solution)/shard_map/pallas_call | solution.py:18
  58.4 2.2 %collective-permute-done.14 = f32[4,8,8,128]{3,2,1,0:T(8,128)S(1)} collective-permute-done((f32[4,8,8,128]{3,2,1,0:T(8,128)S(1)}, f32[4,8,8,128]{3,2,1,0:T(8,128)S(1)}, u32[]{:S(2)}, u32[]{:S(2)}) %collective-permute-start.14) | collective-permute-done | bytes 131104 | tf_op jit(solution)/shard_map/ppermute | solution.py:651
  60.7 1.6 %collective-permute-start.15 = (f32[8,8,8,128]{3,2,1,0:T(8,128)S(1)}, f32[8,8,8,128]{3,2,1,0:T(8,128)S(1)}, u32[]{:S(2)}, u32[]{:S(2)}) collective-permute-start(f32[8,8,8,128]{3,2,1,0:T(8,128)S(1)} %pad_maximum_fusion.3), channel_id=1, source_target_pairs={{0,16},{1,17},{2,18},{3,19},{4,20},{5,21},{6,22},{7,23},{8,24},{9,... | collective-permute-start | bytes 786440 | tf_op jit(solution)/shard_map/ppermute | solution.py:651
  62.3 1.6 %collective-permute-start.16 = (f32[5,2,4,8,128]{4,3,2,1,0:T(8,128)}, f32[5,2,4,8,128]{4,3,2,1,0:T(8,128)S(1)}, u32[]{:S(2)}, u32[]{:S(2)}) collective-permute-start(f32[5,2,4,8,128]{4,3,2,1,0:T(8,128)} %get-tuple-element.76), channel_id=1, source_target_pairs={{0,1},{2,3},{4,5},{6,7},{1,0},{3,2},{5,4},{7,6},{8,9},{10,11},{12,... | collective-permute-start | bytes 491528 | tf_op jit(solution)/shard_map/ppermute | solution.py:802
  64.7 5.1 %collective-permute-done.15 = f32[8,8,8,128]{3,2,1,0:T(8,128)S(1)} collective-permute-done((f32[8,8,8,128]{3,2,1,0:T(8,128)S(1)}, f32[8,8,8,128]{3,2,1,0:T(8,128)S(1)}, u32[]{:S(2)}, u32[]{:S(2)}) %collective-permute-start.15) | collective-permute-done | bytes 262176 | tf_op jit(solution)/shard_map/ppermute | solution.py:651
  69.8 0.8 collective-permute-done.16.yc
  70.6 1.9 %collective-permute-done.18.ftheirs = f32[16,8,8,128]{3,2,1,0:T(8,128)S(1)} collective-permute-done((f32[16,8,8,128]{3,2,1,0:T(8,128)S(1)}, f32[16,8,8,128]{3,2,1,0:T(8,128)S(1)}, u32[]{:S(2)}, u32[]{:S(2)}) %collective-permute-start.18) | collective-permute-done | bytes 524320 | tf_op jit(solution)/shard_map/ppermute | solution.py:651
  72.5 0.8 copy-done.5
  73.3 11.5 %shard_map.46 = (f32[10,4,8,128]{3,2,1,0:T(8,128)}, f32[2,4,4,128]{3,2,1,0:T(4,128)}) custom-call(f32[16,8,8,128]{3,2,1,0:T(8,128)} %copy-done.1, f32[16,8,8,128]{3,2,1,0:T(8,128)} %copy-done.5, f32[16,8,8,128]{3,2,1,0:T(8,128)} %copy-done, f32[16,8,8,128]{3,2,1,0:T(8,128)} %copy-done.4), custom_call_target="tpu_custom_call" | custom-call | bytes 33000000 | tf_op jit(solution)/shard_map/pallas_call | solution.py:18
  84.8 5.8 %shard_map.47 = (f32[8,8,1024]{2,1,0:T(8,128)}, f32[8,8,1024]{2,1,0:T(8,128)}) custom-call(f32[2,18,2,4,8,128]{5,4,3,2,1,0:T(8,128)} %get-tuple-element.58.k, f32[2,18,2,4,8,128]{5,4,3,2,1,0:T(8,128)} %get-tuple-element.59.g, f32[2,18,2,4,8,128]{5,4,3,2,1,0:T(8,128)} %get-tuple-element.60.fs, f32[8,2,4,8,128]{4,3,2,1,0:T(8,128)} %get-tuple-element.61.half, ...), custom_call_target="tpu_custom_call" | custom-call | bytes 18000000 | tf_op jit(solution)/shard_map/pallas_call | solution.py:18
  (57 shorter events, 2.4 us)
Async XLA Ops:
  3.9 15.9 %collective-permute-start = (f32[16,2,4,4,128]{4,3,2,1,0:T(4,128)}, f32[16,2,4,4,128]{4,3,2,1,0:T(4,128)S(1)}, u32[]{:S(2)}, u32[]{:S(2)}) collective-permute-start(f32[16,2,4,4,128]{4,3,2,1,0:T(4,128)} %get-tuple-element.44), channel_id=1, source_target_pairs={{0,1},{2,3},{4,5},{6,7},{1,0},{3,2},{5,4},{7,6},{8,9},{10,11},{12,... | collective-permute-start | bytes 786440 | tf_op jit(solution)/shard_map/ppermute | solution.py:802
  6.9 13.0 %collective-permute-start.1 = (f32[16,2,4,4,128]{4,3,2,1,0:T(4,128)}, f32[16,2,4,4,128]{4,3,2,1,0:T(4,128)S(1)}, u32[]{:S(2)}, u32[]{:S(2)}) collective-permute-start(f32[16,2,4,4,128]{4,3,2,1,0:T(4,128)} %get-tuple-element.45), channel_id=1, source_target_pairs={{1,2},{3,4},{5,6},{2,1},{4,3},{6,5},{9,10},{11,12},{13,14},{10,9},... | collective-permute-start | bytes 786440 | tf_op jit(solution)/shard_map/ppermute | solution.py:802
  9.8 9.3 %collective-permute-start.2 = (f32[1,8,8,128]{3,2,1,0:T(8,128)}, f32[1,8,8,128]{3,2,1,0:T(8,128)S(1)}, u32[]{:S(2)}, u32[]{:S(2)}) collective-permute-start(f32[1,8,8,128]{3,2,1,0:T(8,128)} %bitcast.5), channel_id=1, source_target_pairs={{0,1},{1,0},{2,3},{3,2},{4,5},{5,4},{6,7},{7,6},{8,9},{9,8},{10,11... | collective-permute-start | bytes 98312 | tf_op jit(solution)/shard_map/ppermute | solution.py:651
  19.8 7.8 %copy-start.2 = (f32[16,2,4,4,128]{4,3,2,1,0:T(4,128)}, f32[16,2,4,4,128]{4,3,2,1,0:T(4,128)S(1)}, u32[]{:S(2)}) copy-start(f32[16,2,4,4,128]{4,3,2,1,0:T(4,128)S(1)} %collective-permute-done.ya_far.ya) | copy-start | bytes 786436
  19.8 7.8 %copy-start.3 = (f32[16,2,4,4,128]{4,3,2,1,0:T(4,128)}, f32[16,2,4,4,128]{4,3,2,1,0:T(4,128)S(1)}, u32[]{:S(2)}) copy-start(f32[16,2,4,4,128]{4,3,2,1,0:T(4,128)S(1)} %collective-permute-done.1.yb_far.yb) | copy-start | bytes 786436
  19.9 5.8 %collective-permute-start.7 = (f32[2,8,8,128]{3,2,1,0:T(8,128)S(1)}, f32[2,8,8,128]{3,2,1,0:T(8,128)S(1)}, u32[]{:S(2)}, u32[]{:S(2)}) collective-permute-start(f32[2,8,8,128]{3,2,1,0:T(8,128)S(1)} %pad_maximum_fusion.6), channel_id=1, source_target_pairs={{0,4},{1,5},{2,6},{3,7},{4,0},{5,1},{6,2},{7,3},{8,12},{9,13},{10,... | collective-permute-start | bytes 196616 | tf_op jit(solution)/shard_map/ppermute | solution.py:651
  23.4 8.5 %collective-permute-start.5 = (f32[8,4,16,128]{3,2,1,0:T(8,128)}, f32[8,4,16,128]{3,2,1,0:T(8,128)S(1)}, u32[]{:S(2)}, u32[]{:S(2)}) collective-permute-start(f32[8,4,16,128]{3,2,1,0:T(8,128)} %get-tuple-element.51), channel_id=1, source_target_pairs={{0,8},{16,24},{8,0},{24,16},{1,9},{17,25},{9,1},{25,17},{2,10},{18... | collective-permute-start | bytes 786440 | tf_op jit(solution)/shard_map/ppermute | solution.py:802
  23.4 8.5 %collective-permute-start.6 = (f32[8,4,16,128]{3,2,1,0:T(8,128)}, f32[8,4,16,128]{3,2,1,0:T(8,128)S(1)}, u32[]{:S(2)}, u32[]{:S(2)}) collective-permute-start(f32[8,4,16,128]{3,2,1,0:T(8,128)} %get-tuple-element.52), channel_id=1, source_target_pairs={{8,16},{16,8},{9,17},{17,9},{10,18},{18,10},{11,19},{19,11},{12,20... | collective-permute-start | bytes 786440 | tf_op jit(solution)/shard_map/ppermute | solution.py:802
  25.7 6.1 %collective-permute-start.8 = (f32[4,8,8,128]{3,2,1,0:T(8,128)S(1)}, f32[4,8,8,128]{3,2,1,0:T(8,128)S(1)}, u32[]{:S(2)}, u32[]{:S(2)}) collective-permute-start(f32[4,8,8,128]{3,2,1,0:T(8,128)S(1)} %pad_maximum_fusion.4), channel_id=1, source_target_pairs={{0,2},{1,3},{2,0},{3,1},{4,6},{5,7},{6,4},{7,5},{8,10},{9,11},{10,... | collective-permute-start | bytes 393224 | tf_op jit(solution)/shard_map/ppermute | solution.py:651
  29.5 2.4 %collective-permute-start.3 = (f32[224,128]{1,0:T(8,128)}, f32[224,128]{1,0:T(8,128)S(1)}, u32[]{:S(2)}, u32[]{:S(2)}) collective-permute-start(f32[224,128]{1,0:T(8,128)} %get-tuple-element.49), channel_id=1, source_target_pairs={{0,8},{16,24},{8,0},{24,16},{1,9},{17,25},{9,1},{25,17},{2,10},{18... | collective-permute-start | bytes 344072 | tf_op jit(solution)/shard_map/ppermute | solution.py:802
  30.3 1.6 %collective-permute-start.4 = (f32[224,128]{1,0:T(8,128)}, f32[224,128]{1,0:T(8,128)S(1)}, u32[]{:S(2)}, u32[]{:S(2)}) collective-permute-start(f32[224,128]{1,0:T(8,128)} %get-tuple-element.50), channel_id=1, source_target_pairs={{8,16},{16,8},{9,17},{17,9},{10,18},{18,10},{11,19},{19,11},{12,20... | collective-permute-start | bytes 344072 | tf_op jit(solution)/shard_map/ppermute | solution.py:802
  31.9 5.6 %copy-start.8 = (f32[8,4,16,128]{3,2,1,0:T(8,128)}, f32[8,4,16,128]{3,2,1,0:T(8,128)S(1)}, u32[]{:S(2)}) copy-start(f32[8,4,16,128]{3,2,1,0:T(8,128)S(1)} %collective-permute-done.5.za) | copy-start | bytes 786436
  31.9 5.6 %copy-start.9 = (f32[8,4,16,128]{3,2,1,0:T(8,128)}, f32[8,4,16,128]{3,2,1,0:T(8,128)S(1)}, u32[]{:S(2)}) copy-start(f32[8,4,16,128]{3,2,1,0:T(8,128)S(1)} %collective-permute-done.6.zb) | copy-start | bytes 786436
  31.9 5.6 %copy-start.13 = (f32[224,128]{1,0:T(8,128)}, f32[224,128]{1,0:T(8,128)S(1)}, u32[]{:S(2)}) copy-start(f32[224,128]{1,0:T(8,128)S(1)} %collective-permute-done.3.ca) | copy-start | bytes 344068
  31.9 5.5 %copy-start.14 = (f32[224,128]{1,0:T(8,128)}, f32[224,128]{1,0:T(8,128)S(1)}, u32[]{:S(2)}) copy-start(f32[224,128]{1,0:T(8,128)S(1)} %collective-permute-done.4.cb) | copy-start | bytes 344068
  31.9 12.4 %collective-permute-start.9 = (f32[8,8,8,128]{3,2,1,0:T(8,128)S(1)}, f32[8,8,8,128]{3,2,1,0:T(8,128)S(1)}, u32[]{:S(2)}, u32[]{:S(2)}) collective-permute-start(f32[8,8,8,128]{3,2,1,0:T(8,128)S(1)} %pad_maximum_fusion.2), channel_id=1, source_target_pairs={{0,16},{1,17},{2,18},{3,19},{4,20},{5,21},{6,22},{7,23},{8,24},{9,... | collective-permute-start | bytes 786440 | tf_op jit(solution)/shard_map/ppermute | solution.py:651
  43.2 7.7 %copy-start.16 = (f32[160,128]{1,0:T(8,128)S(1)}, f32[160,128]{1,0:T(8,128)}, u32[]{:S(2)}) copy-start(f32[160,128]{1,0:T(8,128)} %get-tuple-element.66) | copy-start | bytes 245764
  43.2 7.8 %copy-start.15 = (f32[160,128]{1,0:T(8,128)S(1)}, f32[160,128]{1,0:T(8,128)}, u32[]{:S(2)}) copy-start(f32[160,128]{1,0:T(8,128)} %get-tuple-element.67) | copy-start | bytes 245764
  43.2 12.0 %copy-start.12 = (f32[8,8,128]{2,1,0:T(8,128)S(1)}, f32[8,8,128]{2,1,0:T(8,128)}, u32[]{:S(2)}) copy-start(f32[8,8,128]{2,1,0:T(8,128)} %get-tuple-element.63) | copy-start | bytes 98308
  44.4 25.4 %copy-start = (f32[16,8,8,128]{3,2,1,0:T(8,128)}, f32[16,8,8,128]{3,2,1,0:T(8,128)S(1)}, u32[]{:S(2)}) copy-start(f32[16,8,8,128]{3,2,1,0:T(8,128)S(1)} %pad_maximum_fusion.kmine) | copy-start | bytes 1572868
  44.4 5.7 %collective-permute-start.10 = (f32[1,8,8,128]{3,2,1,0:T(8,128)}, f32[1,8,8,128]{3,2,1,0:T(8,128)S(1)}, u32[]{:S(2)}, u32[]{:S(2)}) collective-permute-start(f32[1,8,8,128]{3,2,1,0:T(8,128)} %bitcast.2), channel_id=1, source_target_pairs={{0,4},{1,5},{2,6},{3,7},{4,0},{5,1},{6,2},{7,3},{8,12},{9,13},{10,... | collective-permute-start | bytes 98312 | tf_op jit(solution)/shard_map/ppermute | solution.py:651
  50.9 4.3 %collective-permute-start.11 = (f32[2,8,8,128]{3,2,1,0:T(8,128)S(1)}, f32[2,8,8,128]{3,2,1,0:T(8,128)S(1)}, u32[]{:S(2)}, u32[]{:S(2)}) collective-permute-start(f32[2,8,8,128]{3,2,1,0:T(8,128)S(1)} %pad_maximum_fusion.7), channel_id=1, source_target_pairs={{0,2},{1,3},{2,0},{3,1},{4,6},{5,7},{6,4},{7,5},{8,10},{9,11},{10,... | collective-permute-start | bytes 196616 | tf_op jit(solution)/shard_map/ppermute | solution.py:651
  50.9 4.3 %collective-permute-start.12 = (f32[160,128]{1,0:T(8,128)S(1)}, f32[160,128]{1,0:T(8,128)S(1)}, u32[]{:S(2)}, u32[]{:S(2)}) collective-permute-start(f32[160,128]{1,0:T(8,128)S(1)} %copy-done.16), channel_id=1, source_target_pairs={{0,8},{16,24},{8,0},{24,16},{1,9},{17,25},{9,1},{25,17},{2,10},{18... | collective-permute-start | bytes 245768 | tf_op jit(solution)/shard_map/ppermute | solution.py:802
  51.0 4.2 %collective-permute-start.13 = (f32[160,128]{1,0:T(8,128)S(1)}, f32[160,128]{1,0:T(8,128)S(1)}, u32[]{:S(2)}, u32[]{:S(2)}) collective-permute-start(f32[160,128]{1,0:T(8,128)S(1)} %copy-done.15), channel_id=1, source_target_pairs={{8,16},{16,8},{9,17},{17,9},{10,18},{18,10},{11,19},{19,11},{12,20... | collective-permute-start | bytes 245768 | tf_op jit(solution)/shard_map/ppermute | solution.py:802
  55.2 5.5 %collective-permute-start.14 = (f32[4,8,8,128]{3,2,1,0:T(8,128)S(1)}, f32[4,8,8,128]{3,2,1,0:T(8,128)S(1)}, u32[]{:S(2)}, u32[]{:S(2)}) collective-permute-start(f32[4,8,8,128]{3,2,1,0:T(8,128)S(1)} %pad_maximum_fusion.5), channel_id=1, source_target_pairs={{0,1},{1,0},{2,3},{3,2},{4,5},{5,4},{6,7},{7,6},{8,9},{9,8},{10,11... | collective-permute-start | bytes 393224 | tf_op jit(solution)/shard_map/ppermute | solution.py:651
  60.7 9.1 %collective-permute-start.15 = (f32[8,8,8,128]{3,2,1,0:T(8,128)S(1)}, f32[8,8,8,128]{3,2,1,0:T(8,128)S(1)}, u32[]{:S(2)}, u32[]{:S(2)}) collective-permute-start(f32[8,8,8,128]{3,2,1,0:T(8,128)S(1)} %pad_maximum_fusion.3), channel_id=1, source_target_pairs={{0,16},{1,17},{2,18},{3,19},{4,20},{5,21},{6,22},{7,23},{8,24},{9,... | collective-permute-start | bytes 786440 | tf_op jit(solution)/shard_map/ppermute | solution.py:651
  62.3 8.3 %collective-permute-start.16 = (f32[5,2,4,8,128]{4,3,2,1,0:T(8,128)}, f32[5,2,4,8,128]{4,3,2,1,0:T(8,128)S(1)}, u32[]{:S(2)}, u32[]{:S(2)}) collective-permute-start(f32[5,2,4,8,128]{4,3,2,1,0:T(8,128)} %get-tuple-element.76), channel_id=1, source_target_pairs={{0,1},{2,3},{4,5},{6,7},{1,0},{3,2},{5,4},{7,6},{8,9},{10,11},{12,... | collective-permute-start | bytes 491528 | tf_op jit(solution)/shard_map/ppermute | solution.py:802
  63.9 6.7 %collective-permute-start.17 = (f32[5,2,4,8,128]{4,3,2,1,0:T(8,128)}, f32[5,2,4,8,128]{4,3,2,1,0:T(8,128)S(1)}, u32[]{:S(2)}, u32[]{:S(2)}) collective-permute-start(f32[5,2,4,8,128]{4,3,2,1,0:T(8,128)} %get-tuple-element.77), channel_id=1, source_target_pairs={{1,2},{3,4},{5,6},{2,1},{4,3},{6,5},{9,10},{11,12},{13,14},{10,9},... | collective-permute-start | bytes 491528 | tf_op jit(solution)/shard_map/ppermute | solution.py:802
  64.6 6.0 %collective-permute-start.19 = (f32[16,8,8,128]{3,2,1,0:T(8,128)S(1)}, f32[16,8,8,128]{3,2,1,0:T(8,128)S(1)}, u32[]{:S(2)}, u32[]{:S(2)}) collective-permute-start(f32[16,8,8,128]{3,2,1,0:T(8,128)S(1)} %pad_maximum_fusion.kmine), channel_id=1, source_target_pairs={{0,8},{1,9},{2,10},{3,11},{4,12},{5,13},{6,14},{7,15},{8,0},{9,1},... | collective-permute-start | bytes 1572872 | tf_op jit(solution)/shard_map/ppermute | solution.py:651
  70.6 14.2 %copy-start.10 = (f32[5,2,4,8,128]{4,3,2,1,0:T(8,128)}, f32[5,2,4,8,128]{4,3,2,1,0:T(8,128)S(1)}, u32[]{:S(2)}) copy-start(f32[5,2,4,8,128]{4,3,2,1,0:T(8,128)S(1)} %collective-permute-done.16.yc) | copy-start | bytes 491524
  70.6 14.2 %copy-start.11 = (f32[5,2,4,8,128]{4,3,2,1,0:T(8,128)}, f32[5,2,4,8,128]{4,3,2,1,0:T(8,128)S(1)}, u32[]{:S(2)}) copy-start(f32[5,2,4,8,128]{4,3,2,1,0:T(8,128)S(1)} %collective-permute-done.17.yd) | copy-start | bytes 491524
  70.6 1.9 %collective-permute-start.18 = (f32[16,8,8,128]{3,2,1,0:T(8,128)S(1)}, f32[16,8,8,128]{3,2,1,0:T(8,128)S(1)}, u32[]{:S(2)}, u32[]{:S(2)}) collective-permute-start(f32[16,8,8,128]{3,2,1,0:T(8,128)S(1)} %pad_maximum_fusion.1.fmine), channel_id=1, source_target_pairs={{0,8},{1,9},{2,10},{3,11},{4,12},{5,13},{6,14},{7,15},{8,0},{9,1},... | collective-permute-start | bytes 1572872 | tf_op jit(solution)/shard_map/ppermute | solution.py:651
  (5 other events, 7.9 us)

commit v4 on v3

--- a/solution.py
+++ b/solution.py
@@ -10,16 +10,17 @@
 LEVELS = 4
 PAD = 5
 F32 = jnp.float32
+VMEM = pl.BlockSpec(memory_space=pltpu.VMEM)
+FAR = pl.BlockSpec(memory_space=pl.ANY)
 WHOLE_COARSE_CELLS = 1 << 19
 
 
 def call(body, micros, outs, scratch, *args, specs=None):
-    vmem = pl.BlockSpec(memory_space=pltpu.VMEM)
     return pl.pallas_call(
         body,
         out_shape=[jax.ShapeDtypeStruct(s, F32) for s in outs],
-        in_specs=specs or [vmem] * len(args),
-        out_specs=[vmem] * len(outs),
+        in_specs=specs or [VMEM] * len(args),
+        out_specs=[VMEM] * len(outs),
         scratch_shapes=[pltpu.VMEM(s, F32) if isinstance(s, tuple) else s for s in scratch],
         cost_estimate=pl.CostEstimate(flops=0, transcendentals=0, bytes_accessed=micros * 3_000_000),
         compiler_params=pltpu.CompilerParams(vmem_limit_bytes=56 << 20),
@@ -57,10 +58,13 @@
     return [lane_gather(mixed[-t % 8], 16 * ((lane % 8 + t) % 8) + lane // 8) for t in range(8)]
 
 
-def put_coarse(message, row, s, value):
+def put_coarse(message, row, s, value, tail=None):
     for z in range(4):
         e, c = z % 2, (s + z + row) % 2
-        message[(c * 2 + e) * 2 + s // 2, 2 * row + z // 2, :] = value[z]
+        m, at = (c * 2 + e) * 2 + s // 2, 2 * row + z // 2
+        message[m, at, :] = value[z]
+        if tail is not None:
+            tail[FACE_ROWS + 8 * m + at, :] = value[z]
 
 
 REACH = ((0, 0, 4), (0, 1, 3), (1, 0, 4), (1, 1, 5))
@@ -68,6 +72,10 @@
 ZFACE = sorted(((a, c, d) for a, c, n in REACH for d in range(1, n + 1)), key=lambda r: r[2] - REACH[2 * r[0] + r[1]][2])
 CORNER = {1: (12, 0, 12), 2: (8, 16, 8), 3: (4, 12, 4), 4: (1, 24, 4)}
 CORNER_ROWS = 28
+FACE_ROWS = 5 * 2 * 4 * 4
+DEPTHS = [min(i, 5, LINES - 1 - i) for i in range(LINES)]
+ZSTARTS = [4 * sum(DEPTHS[:i]) for i in range(LINES)]
+ZROWS = 4 * sum(DEPTHS)
 
 
 def own_sides():
@@ -188,12 +196,15 @@
 
 
 def down_kernel(
-    local, ya, yb, za, zb, ca, cb,
-    k, g, fs, half, ub, kx, zc, zd, coarse,
-    f, ur, vr, vb,
+    local, ya, yb, za, zb, ca_far, cb_far,
+    k, g, fs, half, ub, kx, yc, yd, coarse,
+    f, ur, vr, vb, ca, cb, sem,
 ):
     zabove, yabove = own_sides()
-    zup = zabove
+    yup = yabove
+    copies = [pltpu.make_async_copy(*pair, sem.at[i]) for i, pair in enumerate(((ca_far, ca), (cb_far, cb)))]
+    for copy in copies:
+        copy.start()
     blank = jnp.zeros((8, LANES), F32)
     for c in range(2):
         for line in (*range(PAD), *range(PAD + 8, LINES)):
@@ -227,6 +238,8 @@
             for s in range(4):
                 both[a][c, first, e, s, 0:4] = ya[i, e, s]
                 both[a][c, second, e, s, 0:4] = yb[i, e, s]
+    for copy in copies:
+        copy.wait()
     for yside in range(2):
         for s in range(4):
             for d, (count, at, _) in CORNER.items():
@@ -278,32 +291,41 @@
                     line = PAD + y
                     value = red_residual(line, y % 2, e, s, k, g, fs, half, ur, ub, vb)
                     total = value if total is None else total + value
-            put_coarse(coarse, row, s, total * 0.125)
-
-    for y in range(8):
-        for s in range(4):
-            for d in range(1, 6):
-                at, high, low = (4 * y + s) * 5 + d - 1, 8 - d, d - 1
-                up = ub[PAD + y, high % 2, s, high // 2 : high // 2 + 1]
-                down = ub[PAD + y, low % 2, s, low // 2 : low // 2 + 1]
-                zc[at : at + 1, :], zd[at : at + 1, :] = pick(zup, up, down)
-
-
-def widen_kernel(ub, zc, zd, wide, yc, yd):
-    zabove, yup = own_sides()
-    for y in range(8):
-        for s in range(4):
-            at = (4 * y + s) * 5
-            for e in range(2):
-                wide[y, e, s, 0:4] = ub[PAD + y, e, s, 0:4]
-            for side, part in enumerate(pick(zabove, zc[at : at + 4, :], zd[at : at + 4, :])):
-                for d in range(1, 5):
-                    e, row = halo_cell(side, d)
-                    wide[y, e, s, row : row + 1] = part[d - 1 : d]
-    first, second = pick(yup, 3, 0)
+            put_coarse(coarse, row, s, total * 0.125, yc)
+
+    first, second = pick(yup, PAD + 3, PAD)
     for i in range(5):
-        yc[i] = wide[first + i]
-        yd[i] = wide[second + i]
+        for e in range(2):
+            for s in range(4):
+                at = ((i * 2 + e) * 4 + s) * 4
+                yc[at : at + 4, :] = ub[first + i, e, s, 0:4]
+                yd[at : at + 4, :] = ub[second + i, e, s, 0:4]
+
+
+def widen_kernel(ub, yc_far, yd_far, zc, zd, faces, sem):
+    zup, yabove = own_sides()
+    slots, face = pick(yabove, 0, 1), pl.ds(0, FACE_ROWS)
+    copies = [
+        pltpu.make_async_copy(f.at[face], faces.at[t], sem.at[i]) for i, (f, t) in enumerate(zip((yc_far, yd_far), slots))
+    ]
+    for copy in copies:
+        copy.start()
+
+    def put(line, fetch):
+        for target, up in ((zc, zup), (zd, jnp.logical_not(zup))):
+            for d in range(1, DEPTHS[line] + 1):
+                z = jnp.where(up, 8 - d, d - 1)
+                for s in range(4):
+                    at = ZSTARTS[line] + s * DEPTHS[line] + d - 1
+                    target[at : at + 1, :] = fetch(lax.rem(z, 2), s, z // 2)
+
+    for line in range(PAD, PAD + 8):
+        put(line, lambda e, s, t: ub[line, e, s, pl.ds(t, 1)])
+    for copy in copies:
+        copy.wait()
+    for i in range(5):
+        for side, line in enumerate((PAD + 8 + i, i)):
+            put(line, lambda e, s, t: faces[side, pl.ds(((i * 2 + e) * 4 + s) * 4 + t, 1), :])
 
 
 def sweep(c, low, high, k, g, fs, u, v, edges=(None, None)):
@@ -330,25 +352,42 @@
 
 
 def up_kernel(
-    k, g, fs, half, wide, kx, yc, yd, zc, zd, error, errorx,
+    k, g, fs, half, old, kx, yc, yd, zc, zd, error, errorx,
     correction, residual,
     ub, ur, vb, vr, ux, vx, natural,
 ):
     zabove, yabove = own_sides()
-    ub[PAD : PAD + 8] = wide[...]
+    for y in range(8):
+        for e in range(2):
+            for s in range(4):
+                ub[PAD + y, e, s, 0:4] = old[PAD + y, e, s, 0:4]
     first, second = pick(yabove, PAD + 8, 0)
     for i in range(5):
-        ub[first + i] = yc[i]
-        ub[second + i] = yd[i]
-    for y in range(8):
+        for e in range(2):
+            for s in range(4):
+                at = ((i * 2 + e) * 4 + s) * 4
+                ub[first + i, e, s, 0:4] = yc[at : at + 4, :]
+                ub[second + i, e, s, 0:4] = yd[at : at + 4, :]
+    quiet = jnp.zeros((4, LANES), F32)
+    for line, depth in enumerate(DEPTHS):
         for s in range(4):
-            at = (4 * y + s) * 5 + 4
-            for side, part in enumerate(pick(zabove, zc[at : at + 1, :], zd[at : at + 1, :])):
-                beyond = kx[side, y, s : s + 1]
-                value = part + errorx[side, y // 2, s : s + 1]
-                value = jnp.where(beyond != 0.0, value, 0.0)
-                ux[side, y, s : s + 1] = value
-                vx[side, y, s : s + 1] = beyond * value
+            if depth < 4:
+                for e in range(2):
+                    ub[line, e, s, 4:8] = quiet
+            if not depth:
+                continue
+            at = ZSTARTS[line] + s * depth
+            for side, part in enumerate(pick(zabove, zc[at : at + depth, :], zd[at : at + depth, :])):
+                for d in range(1, min(depth, 4) + 1):
+                    e, row = halo_cell(side, d)
+                    ub[line, e, s, row : row + 1] = part[d - 1 : d]
+                if depth == 5:
+                    y = line - PAD
+                    beyond = kx[side, y, s : s + 1]
+                    value = part[4:5] + errorx[side, y // 2, s : s + 1]
+                    value = jnp.where(beyond != 0.0, value, 0.0)
+                    ux[side, y, s : s + 1] = value
+                    vx[side, y, s : s + 1] = beyond * value
 
     def add(line, parity):
         for e in range(2):
@@ -408,8 +447,8 @@
     height2, height3 = height // 2, height // 4
 
     def body(
-        fmine, ftheirs, kmine, ktheirs, error, errorx,
-        f, k, g, fs, half, ur, ub, vr, vb, f2, k2, fc, kc, gc, sc, uc, vc, hc, w3, f3,
+        fmine, ftheirs_far, kmine, ktheirs, error, errorx,
+        f, k, g, fs, half, ur, ub, vr, vb, f2, k2, fc, kc, gc, sc, uc, vc, hc, w3, f3, ftheirs, sem,
     ):
         u, v = (ur, ub), (vr, vb)
         zplace, yplace = lax.axis_index("gz"), lax.axis_index("gy")
@@ -418,24 +457,27 @@
             apart = (zplace * ny + yplace) ^ (i * ny + j)
             return sum(((apart >> step) & 1) << bit for bit, step in enumerate(swaps[:-1]))
 
-        def spread(odd):
+        def spread(odd, sources, target, swaps):
             def visit(j, carry):
-                for sources, target, swaps in (
-                    ((fmine, ftheirs), f, swap_steps(nz, ny)),
-                    ((kmine, ktheirs), k, swap_steps(nz, ny, 0)),
-                ):
-                    order = [slot(i, j, swaps) for i in range(nz)]
-                    for m in range(8):
-                        pieces = [sources[(i + odd) % 2][order[i], m] for i in range(nz)]
-                        for row in range(4):
-                            whole = jnp.concatenate([p[2 * row : 2 * row + 2] for p in pieces], axis=0)
-                            target[m // 4, 1 + 4 * j + row, m // 2 % 2, m % 2] = whole
+                order = [slot(i, j, swaps) for i in range(nz)]
+                for m in range(8):
+                    pieces = [sources[(i + odd) % 2][order[i], m] for i in range(nz)]
+                    for row in range(4):
+                        whole = jnp.concatenate([p[2 * row : 2 * row + 2] for p in pieces], axis=0)
+                        target[m // 4, 1 + 4 * j + row, m // 2 % 2, m % 2] = whole
                 return carry
 
             lax.fori_loop(0, ny, visit, 0)
 
-        for odd in range(2):
-            pl.when(lax.rem(zplace, 2) == odd)(lambda odd=odd: spread(odd))
+        def spread_either(*args):
+            for odd in range(2):
+                pl.when(lax.rem(zplace, 2) == odd)(lambda odd=odd: spread(odd, *args))
+
+        copy = pltpu.make_async_copy(ftheirs_far, ftheirs, sem)
+        copy.start()
+        spread_either((kmine, ktheirs), k, swap_steps(nz, ny))
+        copy.wait()
+        spread_either((fmine, ftheirs), f, swap_steps(nz, ny, 0))
         blank = jnp.zeros((depth, LANES), F32)
         for line in (0, height + 1):
             for e in range(2):
@@ -636,6 +678,7 @@
     flat2 = (2, height2, depth, LANES)
     scratch = [(2, *lines)] * 4 + [lines] * 5 + [flat2, flat2, flat2, (2, *lines2), flat2, flat2]
     scratch += [(2, *lines2), (2, *lines2), flat2[1:], (height3, 6, depth, LANES), (height3, depth, LANES)]
+    scratch += [(nz * ny // 2, 8, 8, LANES), pltpu.SemaphoreType.DMA(())]
     return body, scratch
 
 
@@ -658,7 +701,7 @@
 def solve_coarse(fmine, ftheirs, kmine, ktheirs, nz, ny):
     body, scratch = coarse_kernel(nz, ny)
     outs = ((10, 4, 8, LANES), (2, 4, 4, LANES))
-    return call(body, 11, outs, scratch, fmine, ftheirs, kmine, ktheirs)
+    return call(body, 11, outs, scratch, fmine, ftheirs, kmine, ktheirs, specs=[VMEM, FAR, VMEM, VMEM])
 
 
 def extended(array, sides, width):
@@ -816,50 +859,52 @@
     za, zb = exchange(za, zb, "gz")
     coarse_cells = 8 * 8 * LANES
     whole = nz * ny * coarse_cells <= WHOLE_COARSE_CELLS and nz & (nz - 1) == 0 and ny & (ny - 1) == 0
-    swaps, kswaps = swap_steps(nz, ny), swap_steps(nz, ny, 0)
+    swaps, kswaps = swap_steps(nz, ny, 0), swap_steps(nz, ny)
     kall = kmessage[None]
     if whole:
         kall = swapped(kall, kswaps[0], nz, ny)
-        ya, yb, kall = lax.optimization_barrier((ya, yb, kall))
-    relayed = (8 * CORNER_ROWS, LANES)
-    scratch = [(2, *yface), pltpu.SemaphoreType.DMA((2,))]
-    far = [pl.BlockSpec(memory_space=pl.ANY)] * 2
-    ca, cb = exchange(*call(relay_kernel, 2, (relayed, relayed), scratch, ya, yb, specs=far), "gz")
+        ya, yb, za, zb, kall = lax.optimization_barrier((ya, yb, za, zb, kall))
+    relayed, sems = (8 * CORNER_ROWS, LANES), pltpu.SemaphoreType.DMA((2,))
+    corners = call(relay_kernel, 2, (relayed, relayed), [(2, *yface), sems], ya, yb, specs=[FAR] * 2)
+    ca, cb = exchange(*corners, "gz")
     if whole:
-        for step in kswaps[1:-2]:
+        for step in kswaps[1:-3]:
             kall = swapped(kall, step, nz, ny)
-        ca, cb, za, zb, kall = lax.optimization_barrier((ca, cb, za, zb, kall))
+        ca, cb, kall = lax.optimization_barrier((ca, cb, kall))
+        kall = swapped(kall, kswaps[-3], nz, ny)
+    lines, face = (LINES, 2, 4, 8, LANES), (FACE_ROWS, LANES)
+    outs = ((2, *lines), (2, *lines), (2, *lines), (8, *lines[1:]), lines, (2, 8, 4, LANES))
+    outs += ((FACE_ROWS + 64, LANES), face, coarse)
+    scratch = [(2, *lines), lines, lines, lines, relayed, relayed, sems]
+    k, g, fs, half, ub, kx, yc, yd, message = call(
+        down_kernel, 6, outs, scratch, local, ya, yb, za, zb, ca, cb, specs=[VMEM] * 5 + [FAR] * 2
+    )
+    if whole:
+        yc, kall = lax.optimization_barrier((yc, kall))
+    yc, yd = exchange(yc, yd, "gy")
+    if whole:
+        fall = jnp.stack([message, yc[FACE_ROWS:].reshape(message.shape)])
+        fall = swapped(fall, swaps[1], nz, ny)
         kall = swapped(kall, kswaps[-2], nz, ny)
-    lines, zface = (LINES, 2, 4, 8, LANES), (160, LANES)
-    outs = ((2, *lines), (2, *lines), (2, *lines), (8, *lines[1:]), lines, (2, 8, 4, LANES), zface, zface, coarse)
-    scratch = [(2, *lines), lines, lines, lines]
-    k, g, fs, half, ub, kx, zc, zd, message = call(down_kernel, 6, outs, scratch, local, ya, yb, za, zb, ca, cb)
-    fall, half_way = message[None], len(swaps) // 2
+        fall, yc, yd = lax.optimization_barrier((fall, yc, yd))
+        for step in swaps[2:-2]:
+            fall = swapped(fall, step, nz, ny)
+    zface = (ZROWS, LANES)
+    zc, zd = call(widen_kernel, 2, (zface, zface), [(2, *face), sems], ub, yc, yd, specs=[VMEM, FAR, FAR])
     if whole:
-        fall, kall = lax.optimization_barrier((fall, kall))
-        ktheirs = swap(kall, kswaps[-1], nz, ny)
+        fall, zc, zd = lax.optimization_barrier((fall, zc, zd))
     zc, zd = exchange(zc, zd, "gz")
     if whole:
-        for step in swaps[:half_way]:
-            fall = swapped(fall, step, nz, ny)
-        fall, zc, zd = lax.optimization_barrier((fall, zc, zd))
-    yface = (5, *lines[1:])
-    wide, yc, yd = call(widen_kernel, 2, ((8, *lines[1:]), yface, yface), [], ub, zc, zd)
-    if whole:
-        fall = swapped(fall, swaps[half_way], nz, ny)
-        fall, yc, yd = lax.optimization_barrier((fall, yc, yd))
-    yc, yd = exchange(yc, yd, "gy")
-    if whole:
-        for step in swaps[half_way + 1 : -1]:
-            fall = swapped(fall, step, nz, ny)
-        fall, yc, yd = lax.optimization_barrier((fall, yc, yd))
+        fall = swapped(fall, swaps[-2], nz, ny)
+        ktheirs = swap(kall, kswaps[-1], nz, ny)
+        fall, kall, ktheirs, zc, zd = lax.optimization_barrier((fall, kall, ktheirs, zc, zd))
         ftheirs = swap(fall, swaps[-1], nz, ny)
         error, errorx = solve_coarse(fall, ftheirs, kall, ktheirs, nz, ny)
     else:
         error, errorx = solve_coarse_spread(message, kmessage, nz, ny)
     block = (8, 8, 8 * LANES)
     scratch = [lines] * 4 + [(2, 8, 4, LANES)] * 2 + [(2, 8, 64, LANES)]
-    return call(up_kernel, 6, (block, block), scratch, k, g, fs, half, wide, kx, yc, yd, zc, zd, error, errorx)
+    return call(up_kernel, 6, (block, block), scratch, k, g, fs, half, ub, kx, yc, yd, zc, zd, error, errorx)
 
 
 def solution(mesh):

time: 91.7 us -> 85.8 us (0.936)
  waiting for transfers between devices: 24.4 us -> 13.5 us
  starting transfers between devices: 30.3 us -> 33.6 us
  Pallas kernels: 32.5 us -> 34.5 us
    ppermute x10 -> x9, waiting for transfers between devices: 23.6 us -> 12.9 us  [swap(): lax.ppermute(block, ('gz', 'gy'), [(i, i ^ 1 << step) for i in range(nz *...]
    ppermute x10 -> x9, starting transfers between devices: 21.7 us -> 26.3 us  [swap(): lax.ppermute(block, ('gz', 'gy'), [(i, i ^ 1 << step) for i in range(nz *...]
    pallas_call x7, Pallas kernels: 32.5 us -> 34.5 us  [call(): pl.pallas_call(body, out_shape=[jax.ShapeDtypeStruct(s, F32) for s in out...]
    ppermute x10, starting transfers between devices: 8.65 us -> 7.25 us  [exchange(): lax.ppermute(message, axis, pairs + [(j, i) for i, j in pairs])]
  transfers between devices with their start and end apart: 20 -> 19, of which waited for: 10 -> 6; matrix products, arithmetic and copies ran while one was open for 1% -> 2% of each run, Pallas kernels for 13% -> 15%
where the time goes in v4:
time: 85.8 us; the launch traced here: 85.1 us
  Pallas kernels  34.5 us (40%)
  starting transfers between devices  33.6 us (39%)
  waiting for transfers between devices  13.5 us (16%)
  other arithmetic  1.65 us (2%)
  between operations  0.96 us (1%)
  local copies, waits for them, and re-layouts  0.88 us (1%)
    pallas_call x7, Pallas kernels, call(): pl.pallas_call(body, out_shape=[jax.ShapeDtypeStruct(s, F32) for s in out...  34.5 us
    ppermute x9, starting transfers between devices, swap(): lax.ppermute(block, ('gz', 'gy'), [(i, i ^ 1 << step) for i in range(nz *...  26.3 us
    ppermute x9, waiting for transfers between devices, swap(): lax.ppermute(block, ('gz', 'gy'), [(i, i ^ 1 << step) for i in range(nz *...  12.9 us
    ppermute x10, starting transfers between devices, exchange(): lax.ppermute(message, axis, pairs + [(j, i) for i, j in pairs])  7.25 us
  transfers between devices with their start and end apart: 19, of which 6 were waited for; matrix products, arithmetic and copies ran while one was open for 2% of the time, Pallas kernels for 15%

profile of v4, /device:TPU:0, one launch (start us, length us, event | category | flops | bytes accessed | tf_op | source)
XLA Modules:
  0.0 85.1 jit_solution(3095121864908501281)
XLA Ops:
  0.6 3.3 %shard_map.41 = (f32[2,2,8,2,4,4,128]{6,5,4,3,2,1,0:T(4,128)}, f32[16,2,4,4,128]{4,3,2,1,0:T(4,128)}, f32[16,2,4,4,128]{4,3,2,1,0:T(4,128)}) custom-call(f32[8,8,1024]{2,1,0:T(8,128)} %f_ref.1, f32[8,8,1024]{2,1,0:T(8,128)} %k_ref.1), custom_call_target="tpu_custom_call" | custom-call | bytes 9000000 | tf_op jit(solution)/shard_map/pallas_call | solution.py:19
  3.9 2.9 %collective-permute-start = (f32[16,2,4,4,128]{4,3,2,1,0:T(4,128)}, f32[16,2,4,4,128]{4,3,2,1,0:T(4,128)S(1)}, u32[]{:S(2)}, u32[]{:S(2)}) collective-permute-start(f32[16,2,4,4,128]{4,3,2,1,0:T(4,128)} %get-tuple-element.45), channel_id=1, source_target_pairs={{0,1},{2,3},{4,5},{6,7},{1,0},{3,2},{5,4},{7,6},{8,9},{10,11},{12,... | collective-permute-start | bytes 786440 | tf_op jit(solution)/shard_map/ppermute | solution.py:845
  6.9 0.7 collective-permute-start.1
  7.5 2.3 %shard_map.42 = (f32[8,4,16,128]{3,2,1,0:T(8,128)}, f32[8,4,16,128]{3,2,1,0:T(8,128)}, f32[8,8,128]{2,1,0:T(8,128)}) custom-call(f32[2,2,8,2,4,4,128]{6,5,4,3,2,1,0:T(4,128)} %get-tuple-element.44.local), custom_call_target="tpu_custom_call" | custom-call | bytes 6000000 | tf_op jit(solution)/shard_map/pallas_call | solution.py:19
  9.8 0.7 collective-permute-start.3
  10.5 4.3 %collective-permute-start.4 = (f32[1,8,8,128]{3,2,1,0:T(8,128)}, f32[1,8,8,128]{3,2,1,0:T(8,128)S(1)}, u32[]{:S(2)}, u32[]{:S(2)}) collective-permute-start(f32[1,8,8,128]{3,2,1,0:T(8,128)} %bitcast.6), channel_id=1, source_target_pairs={{0,4},{1,5},{2,6},{3,7},{4,0},{5,1},{6,2},{7,3},{8,12},{9,13},{10,... | collective-permute-start | bytes 98312 | tf_op jit(solution)/shard_map/ppermute | solution.py:694
  14.8 3.3 %collective-permute-done.4 = f32[1,8,8,128]{3,2,1,0:T(8,128)S(1)} collective-permute-done((f32[1,8,8,128]{3,2,1,0:T(8,128)}, f32[1,8,8,128]{3,2,1,0:T(8,128)S(1)}, u32[]{:S(2)}, u32[]{:S(2)}) %collective-permute-start.4) | collective-permute-done | bytes 32800 | tf_op jit(solution)/shard_map/ppermute | solution.py:694
  18.1 0.8 pad_maximum_fusion.5
  18.9 2.0 %collective-permute-start.7 = (f32[2,8,8,128]{3,2,1,0:T(8,128)S(1)}, f32[2,8,8,128]{3,2,1,0:T(8,128)S(1)}, u32[]{:S(2)}, u32[]{:S(2)}) collective-permute-start(f32[2,8,8,128]{3,2,1,0:T(8,128)S(1)} %pad_maximum_fusion.5), channel_id=1, source_target_pairs={{0,2},{1,3},{2,0},{3,1},{4,6},{5,7},{6,4},{7,5},{8,10},{9,11},{10,... | collective-permute-start | bytes 196616 | tf_op jit(solution)/shard_map/ppermute | solution.py:694
  20.9 1.9 %shard_map.43 = (f32[224,128]{1,0:T(8,128)}, f32[224,128]{1,0:T(8,128)}) custom-call(f32[16,2,4,4,128]{4,3,2,1,0:T(4,128)} %copy-done.2, f32[16,2,4,4,128]{4,3,2,1,0:T(4,128)} %copy-done.3), custom_call_target="tpu_custom_call" | custom-call | bytes 6000000 | tf_op jit(solution)/shard_map/pallas_call | solution.py:19
  22.8 0.3 collective-permute-start.5
  23.1 0.7 collective-permute-start.6
  23.8 0.6 collective-permute-done.5.ca_far
  24.4 2.5 %collective-permute-start.8 = (f32[4,8,8,128]{3,2,1,0:T(8,128)S(1)}, f32[4,8,8,128]{3,2,1,0:T(8,128)S(1)}, u32[]{:S(2)}, u32[]{:S(2)}) collective-permute-start(f32[4,8,8,128]{3,2,1,0:T(8,128)S(1)} %pad_maximum_fusion.3), channel_id=1, source_target_pairs={{0,1},{1,0},{2,3},{3,2},{4,5},{5,4},{6,7},{7,6},{8,9},{9,8},{10,11... | collective-permute-start | bytes 393224 | tf_op jit(solution)/shard_map/ppermute | solution.py:694
  26.9 6.0 %shard_map.44 = (f32[2,18,2,4,8,128]{5,4,3,2,1,0:T(8,128)}, f32[2,18,2,4,8,128]{5,4,3,2,1,0:T(8,128)}, f32[2,18,2,4,8,128]{5,4,3,2,1,0:T(8,128)}, f32[8,2,4,8,12...) custom-call(f32[2,2,8,2,4,4,128]{6,5,4,3,2,1,0:T(4,128)} %get-tuple-, ...), custom_call_target="tpu_custom_call" | custom-call | bytes 18000000 | tf_op jit(solution)/shard_map/pallas_call | solution.py:19
  32.9 0.7 collective-permute-start.9
  33.7 0.7 collective-permute-start.11
  34.3 7.1 %collective-permute-start.14 = (f32[8,8,8,128]{3,2,1,0:T(8,128)S(1)}, f32[8,8,8,128]{3,2,1,0:T(8,128)S(1)}, u32[]{:S(2)}, u32[]{:S(2)}) collective-permute-start(f32[8,8,8,128]{3,2,1,0:T(8,128)S(1)} %pad_maximum_fusion.1), channel_id=1, source_target_pairs={{0,16},{1,17},{2,18},{3,19},{4,20},{5,21},{6,22},{7,23},{8,24},{9,... | collective-permute-start | bytes 786440 | tf_op jit(solution)/shard_map/ppermute | solution.py:694
  41.4 0.8 pad_maximum_fusion.6
  42.2 4.2 %collective-permute-start.10 = (f32[2,8,8,128]{3,2,1,0:T(8,128)S(1)}, f32[2,8,8,128]{3,2,1,0:T(8,128)S(1)}, u32[]{:S(2)}, u32[]{:S(2)}) collective-permute-start(f32[2,8,8,128]{3,2,1,0:T(8,128)S(1)} %pad_maximum_fusion.6), channel_id=1, source_target_pairs={{0,4},{1,5},{2,6},{3,7},{4,0},{5,1},{6,2},{7,3},{8,12},{9,13},{10,... | collective-permute-start | bytes 196616 | tf_op jit(solution)/shard_map/ppermute | solution.py:694
  46.4 2.2 %collective-permute-done.10 = f32[2,8,8,128]{3,2,1,0:T(8,128)S(1)} collective-permute-done((f32[2,8,8,128]{3,2,1,0:T(8,128)S(1)}, f32[2,8,8,128]{3,2,1,0:T(8,128)S(1)}, u32[]{:S(2)}, u32[]{:S(2)}) %collective-permute-start.10) | collective-permute-done | bytes 65568 | tf_op jit(solution)/shard_map/ppermute | solution.py:694
  48.7 2.9 %collective-permute-start.12 = (f32[4,8,8,128]{3,2,1,0:T(8,128)S(1)}, f32[4,8,8,128]{3,2,1,0:T(8,128)S(1)}, u32[]{:S(2)}, u32[]{:S(2)}) collective-permute-start(f32[4,8,8,128]{3,2,1,0:T(8,128)S(1)} %pad_maximum_fusion.4), channel_id=1, source_target_pairs={{0,2},{1,3},{2,0},{3,1},{4,6},{5,7},{6,4},{7,5},{8,10},{9,11},{10,... | collective-permute-start | bytes 393224 | tf_op jit(solution)/shard_map/ppermute | solution.py:694
  51.6 0.1 collective-permute-start.15
  51.7 2.9 %shard_map.45 = (f32[240,128]{1,0:T(8,128)}, f32[240,128]{1,0:T(8,128)}) custom-call(f32[18,2,4,8,128]{4,3,2,1,0:T(8,128)} %get-tuple-element.63.ub.old, f32[224,128]{1,0:T(8,128)} %copy-done.4, f32[160,128]{1,0:T(8,128)} %copy-done.7), custom_call_target="tpu_custom_call" | custom-call | bytes 6000000 | tf_op jit(solution)/shard_map/pallas_call | solution.py:19
  54.7 2.2 %collective-permute-start.13 = (f32[8,8,8,128]{3,2,1,0:T(8,128)S(1)}, f32[8,8,8,128]{3,2,1,0:T(8,128)S(1)}, u32[]{:S(2)}, u32[]{:S(2)}) collective-permute-start(f32[8,8,8,128]{3,2,1,0:T(8,128)S(1)} %pad_maximum_fusion.2), channel_id=1, source_target_pairs={{0,16},{1,17},{2,18},{3,19},{4,20},{5,21},{6,22},{7,23},{8,24},{9,... | collective-permute-start | bytes 786440 | tf_op jit(solution)/shard_map/ppermute | solution.py:694
  56.9 0.7 collective-permute-start.17
  57.6 5.8 %collective-permute-done.13 = f32[8,8,8,128]{3,2,1,0:T(8,128)S(1)} collective-permute-done((f32[8,8,8,128]{3,2,1,0:T(8,128)S(1)}, f32[8,8,8,128]{3,2,1,0:T(8,128)S(1)}, u32[]{:S(2)}, u32[]{:S(2)}) %collective-permute-start.13) | collective-permute-done | bytes 262176 | tf_op jit(solution)/shard_map/ppermute | solution.py:694
  63.5 1.1 %collective-permute-start.18 = (f32[16,8,8,128]{3,2,1,0:T(8,128)S(1)}, f32[16,8,8,128]{3,2,1,0:T(8,128)S(1)}, u32[]{:S(2)}, u32[]{:S(2)}) collective-permute-start(f32[16,8,8,128]{3,2,1,0:T(8,128)S(1)} %pad_maximum_fusion.fmine), channel_id=1, source_target_pairs={{0,8},{1,9},{2,10},{3,11},{4,12},{5,13},{6,14},{7,15},{8,0},{9,1},... | collective-permute-start | bytes 1572872 | tf_op jit(solution)/shard_map/ppermute | solution.py:694
  64.6 1.5 %collective-permute-done.18.ftheirs_far = f32[16,8,8,128]{3,2,1,0:T(8,128)S(1)} collective-permute-done((f32[16,8,8,128]{3,2,1,0:T(8,128)S(1)}, f32[16,8,8,128]{3,2,1,0:T(8,128)S(1)}, u32[]{:S(2)}, u32[]{:S(2)}) %collective-permute-start.18) | collective-permute-done | bytes 524320 | tf_op jit(solution)/shard_map/ppermute | solution.py:694
  66.1 0.8 copy-done.6
  66.9 12.2 %shard_map.46 = (f32[10,4,8,128]{3,2,1,0:T(8,128)}, f32[2,4,4,128]{3,2,1,0:T(4,128)}) custom-call(f32[16,8,8,128]{3,2,1,0:T(8,128)} %copy-done, f32[16,8,8,128]{3,2,1,0:T(8,128)} %copy-done.6, f32[16,8,8,128]{3,2,1,0:T(8,128)} %copy-done.1, f32[16,8,8,128]{3,2,1,0:T(8,128)} %copy-done.5), custom_call_target="tpu_custom_call" | custom-call | bytes 33000000 | tf_op jit(solution)/shard_map/pallas_call | solution.py:19
  79.1 6.0 %shard_map.47 = (f32[8,8,1024]{2,1,0:T(8,128)}, f32[8,8,1024]{2,1,0:T(8,128)}) custom-call(f32[2,18,2,4,8,128]{5,4,3,2,1,0:T(8,128)} %get-tuple-element.59.k, f32[2,18,2,4,8,128]{5,4,3,2,1,0:T(8,128)} %get-tuple-element.60.g, f32[2,18,2,4,8,128]{5,4,3,2,1,0:T(8,128)} %get-tuple-element.61.fs, f32[8,2,4,8,128]{4,3,2,1,0:T(8,128)} %get-tuple-element.62.half, ...), custom_call_target="tpu_custom_call" | custom-call | bytes 18000000 | tf_op jit(solution)/shard_map/pallas_call | solution.py:19
  (53 shorter events, 0.3 us)
Async XLA Ops:
  3.9 14.9 %collective-permute-start = (f32[16,2,4,4,128]{4,3,2,1,0:T(4,128)}, f32[16,2,4,4,128]{4,3,2,1,0:T(4,128)S(1)}, u32[]{:S(2)}, u32[]{:S(2)}) collective-permute-start(f32[16,2,4,4,128]{4,3,2,1,0:T(4,128)} %get-tuple-element.45), channel_id=1, source_target_pairs={{0,1},{2,3},{4,5},{6,7},{1,0},{3,2},{5,4},{7,6},{8,9},{10,11},{12,... | collective-permute-start | bytes 786440 | tf_op jit(solution)/shard_map/ppermute | solution.py:845
  6.9 12.0 %collective-permute-start.1 = (f32[16,2,4,4,128]{4,3,2,1,0:T(4,128)}, f32[16,2,4,4,128]{4,3,2,1,0:T(4,128)S(1)}, u32[]{:S(2)}, u32[]{:S(2)}) collective-permute-start(f32[16,2,4,4,128]{4,3,2,1,0:T(4,128)} %get-tuple-element.46), channel_id=1, source_target_pairs={{1,2},{3,4},{5,6},{2,1},{4,3},{6,5},{9,10},{11,12},{13,14},{10,9},... | collective-permute-start | bytes 786440 | tf_op jit(solution)/shard_map/ppermute | solution.py:845
  9.8 9.1 %collective-permute-start.2 = (f32[8,4,16,128]{3,2,1,0:T(8,128)}, f32[8,4,16,128]{3,2,1,0:T(8,128)S(1)}, u32[]{:S(2)}, u32[]{:S(2)}) collective-permute-start(f32[8,4,16,128]{3,2,1,0:T(8,128)} %get-tuple-element.47), channel_id=1, source_target_pairs={{0,8},{16,24},{8,0},{24,16},{1,9},{17,25},{9,1},{25,17},{2,10},{18... | collective-permute-start | bytes 786440 | tf_op jit(solution)/shard_map/ppermute | solution.py:845
  9.8 9.1 %collective-permute-start.3 = (f32[8,4,16,128]{3,2,1,0:T(8,128)}, f32[8,4,16,128]{3,2,1,0:T(8,128)S(1)}, u32[]{:S(2)}, u32[]{:S(2)}) collective-permute-start(f32[8,4,16,128]{3,2,1,0:T(8,128)} %get-tuple-element.48), channel_id=1, source_target_pairs={{8,16},{16,8},{9,17},{17,9},{10,18},{18,10},{11,19},{19,11},{12,20... | collective-permute-start | bytes 786440 | tf_op jit(solution)/shard_map/ppermute | solution.py:845
  10.5 7.6 %collective-permute-start.4 = (f32[1,8,8,128]{3,2,1,0:T(8,128)}, f32[1,8,8,128]{3,2,1,0:T(8,128)S(1)}, u32[]{:S(2)}, u32[]{:S(2)}) collective-permute-start(f32[1,8,8,128]{3,2,1,0:T(8,128)} %bitcast.6), channel_id=1, source_target_pairs={{0,4},{1,5},{2,6},{3,7},{4,0},{5,1},{6,2},{7,3},{8,12},{9,13},{10,... | collective-permute-start | bytes 98312 | tf_op jit(solution)/shard_map/ppermute | solution.py:694
  18.9 2.1 %copy-start.2 = (f32[16,2,4,4,128]{4,3,2,1,0:T(4,128)}, f32[16,2,4,4,128]{4,3,2,1,0:T(4,128)S(1)}, u32[]{:S(2)}) copy-start(f32[16,2,4,4,128]{4,3,2,1,0:T(4,128)S(1)} %collective-permute-done.ya_far.ya) | copy-start | bytes 786436
  18.9 8.0 %copy-start.8 = (f32[8,4,16,128]{3,2,1,0:T(8,128)}, f32[8,4,16,128]{3,2,1,0:T(8,128)S(1)}, u32[]{:S(2)}) copy-start(f32[8,4,16,128]{3,2,1,0:T(8,128)S(1)} %collective-permute-done.2.za) | copy-start | bytes 786436
  18.9 8.0 %copy-start.9 = (f32[8,4,16,128]{3,2,1,0:T(8,128)}, f32[8,4,16,128]{3,2,1,0:T(8,128)S(1)}, u32[]{:S(2)}) copy-start(f32[8,4,16,128]{3,2,1,0:T(8,128)S(1)} %collective-permute-done.3.zb) | copy-start | bytes 786436
  18.9 4.9 %collective-permute-start.7 = (f32[2,8,8,128]{3,2,1,0:T(8,128)S(1)}, f32[2,8,8,128]{3,2,1,0:T(8,128)S(1)}, u32[]{:S(2)}, u32[]{:S(2)}) collective-permute-start(f32[2,8,8,128]{3,2,1,0:T(8,128)S(1)} %pad_maximum_fusion.5), channel_id=1, source_target_pairs={{0,2},{1,3},{2,0},{3,1},{4,6},{5,7},{6,4},{7,5},{8,10},{9,11},{10,... | collective-permute-start | bytes 196616 | tf_op jit(solution)/shard_map/ppermute | solution.py:694
  22.8 1.6 %collective-permute-start.5 = (f32[224,128]{1,0:T(8,128)}, f32[224,128]{1,0:T(8,128)S(1)}, u32[]{:S(2)}, u32[]{:S(2)}) collective-permute-start(f32[224,128]{1,0:T(8,128)} %get-tuple-element.54), channel_id=1, source_target_pairs={{0,8},{16,24},{8,0},{24,16},{1,9},{17,25},{9,1},{25,17},{2,10},{18... | collective-permute-start | bytes 344072 | tf_op jit(solution)/shard_map/ppermute | solution.py:845
  23.1 1.3 %collective-permute-start.6 = (f32[224,128]{1,0:T(8,128)}, f32[224,128]{1,0:T(8,128)S(1)}, u32[]{:S(2)}, u32[]{:S(2)}) collective-permute-start(f32[224,128]{1,0:T(8,128)} %get-tuple-element.55), channel_id=1, source_target_pairs={{8,16},{16,8},{9,17},{17,9},{10,18},{18,10},{11,19},{19,11},{12,20... | collective-permute-start | bytes 344072 | tf_op jit(solution)/shard_map/ppermute | solution.py:845
  24.4 2.5 %copy-start.13 = (f32[224,128]{1,0:T(8,128)}, f32[224,128]{1,0:T(8,128)S(1)}, u32[]{:S(2)}) copy-start(f32[224,128]{1,0:T(8,128)S(1)} %collective-permute-done.5.ca_far) | copy-start | bytes 344068
  24.4 2.5 %copy-start.14 = (f32[224,128]{1,0:T(8,128)}, f32[224,128]{1,0:T(8,128)S(1)}, u32[]{:S(2)}) copy-start(f32[224,128]{1,0:T(8,128)S(1)} %collective-permute-done.6.cb_far) | copy-start | bytes 344068
  24.4 8.5 %collective-permute-start.8 = (f32[4,8,8,128]{3,2,1,0:T(8,128)S(1)}, f32[4,8,8,128]{3,2,1,0:T(8,128)S(1)}, u32[]{:S(2)}, u32[]{:S(2)}) collective-permute-start(f32[4,8,8,128]{3,2,1,0:T(8,128)S(1)} %pad_maximum_fusion.3), channel_id=1, source_target_pairs={{0,1},{1,0},{2,3},{3,2},{4,5},{5,4},{6,7},{7,6},{8,9},{9,8},{10,11... | collective-permute-start | bytes 393224 | tf_op jit(solution)/shard_map/ppermute | solution.py:694
  32.9 15.8 %copy-start.10 = (f32[8,8,128]{2,1,0:T(8,128)S(1)}, f32[8,8,128]{2,1,0:T(8,128)}, u32[]{:S(2)}) copy-start(f32[8,8,128]{2,1,0:T(8,128)} %get-tuple-element.65) | copy-start | bytes 98308
  32.9 8.5 %collective-permute-start.9 = (f32[224,128]{1,0:T(8,128)}, f32[224,128]{1,0:T(8,128)S(1)}, u32[]{:S(2)}, u32[]{:S(2)}) collective-permute-start(f32[224,128]{1,0:T(8,128)} %get-tuple-element.68), channel_id=1, source_target_pairs={{0,1},{2,3},{4,5},{6,7},{1,0},{3,2},{5,4},{7,6},{8,9},{10,11},{12,... | collective-permute-start | bytes 344072 | tf_op jit(solution)/shard_map/ppermute | solution.py:845
  33.7 15.0 %collective-permute-start.11 = (f32[160,128]{1,0:T(8,128)}, f32[160,128]{1,0:T(8,128)S(1)}, u32[]{:S(2)}, u32[]{:S(2)}) collective-permute-start(f32[160,128]{1,0:T(8,128)} %get-tuple-element.69), channel_id=1, source_target_pairs={{1,2},{3,4},{5,6},{2,1},{4,3},{6,5},{9,10},{11,12},{13,14},{10,9},... | collective-permute-start | bytes 245768 | tf_op jit(solution)/shard_map/ppermute | solution.py:845
  34.3 17.3 %collective-permute-start.14 = (f32[8,8,8,128]{3,2,1,0:T(8,128)S(1)}, f32[8,8,8,128]{3,2,1,0:T(8,128)S(1)}, u32[]{:S(2)}, u32[]{:S(2)}) collective-permute-start(f32[8,8,8,128]{3,2,1,0:T(8,128)S(1)} %pad_maximum_fusion.1), channel_id=1, source_target_pairs={{0,16},{1,17},{2,18},{3,19},{4,20},{5,21},{6,22},{7,23},{8,24},{9,... | collective-permute-start | bytes 786440 | tf_op jit(solution)/shard_map/ppermute | solution.py:694
  41.4 10.3 %copy-start.4 = (f32[224,128]{1,0:T(8,128)}, f32[224,128]{1,0:T(8,128)S(1)}, u32[]{:S(2)}) copy-start(f32[224,128]{1,0:T(8,128)S(1)} %collective-permute-done.9.yc_far.yc) | copy-start | bytes 344068
  42.2 6.4 %collective-permute-start.10 = (f32[2,8,8,128]{3,2,1,0:T(8,128)S(1)}, f32[2,8,8,128]{3,2,1,0:T(8,128)S(1)}, u32[]{:S(2)}, u32[]{:S(2)}) collective-permute-start(f32[2,8,8,128]{3,2,1,0:T(8,128)S(1)} %pad_maximum_fusion.6), channel_id=1, source_target_pairs={{0,4},{1,5},{2,6},{3,7},{4,0},{5,1},{6,2},{7,3},{8,12},{9,13},{10,... | collective-permute-start | bytes 196616 | tf_op jit(solution)/shard_map/ppermute | solution.py:694
  48.7 3.0 %copy-start.7 = (f32[160,128]{1,0:T(8,128)}, f32[160,128]{1,0:T(8,128)S(1)}, u32[]{:S(2)}) copy-start(f32[160,128]{1,0:T(8,128)S(1)} %collective-permute-done.11.yd_far.yd) | copy-start | bytes 245764
  48.7 5.9 %collective-permute-start.12 = (f32[4,8,8,128]{3,2,1,0:T(8,128)S(1)}, f32[4,8,8,128]{3,2,1,0:T(8,128)S(1)}, u32[]{:S(2)}, u32[]{:S(2)}) collective-permute-start(f32[4,8,8,128]{3,2,1,0:T(8,128)S(1)} %pad_maximum_fusion.4), channel_id=1, source_target_pairs={{0,2},{1,3},{2,0},{3,1},{4,6},{5,7},{6,4},{7,5},{8,10},{9,11},{10,... | collective-permute-start | bytes 393224 | tf_op jit(solution)/shard_map/ppermute | solution.py:694
  51.6 11.8 %copy-start.1 = (f32[16,8,8,128]{3,2,1,0:T(8,128)}, f32[16,8,8,128]{3,2,1,0:T(8,128)S(1)}, u32[]{:S(2)}) copy-start(f32[16,8,8,128]{3,2,1,0:T(8,128)S(1)} %constant_dynamic-update-slice_fusion.kmine) | copy-start | bytes 1572868
  51.6 11.8 %collective-permute-start.15 = (f32[16,8,8,128]{3,2,1,0:T(8,128)S(1)}, f32[16,8,8,128]{3,2,1,0:T(8,128)S(1)}, u32[]{:S(2)}, u32[]{:S(2)}) collective-permute-start(f32[16,8,8,128]{3,2,1,0:T(8,128)S(1)} %constant_dynamic-update-slice_fusion.kmine), channel_id=1, source_target_pairs={{0,8},{1,9},{2,10},{3,11},{4,12},{5,13},{6,14},{7,15},{8,0},{9,1},... | collective-permute-start | bytes 1572872 | tf_op jit(solution)/shard_map/ppermute | solution.py:694
  54.7 8.7 %collective-permute-start.13 = (f32[8,8,8,128]{3,2,1,0:T(8,128)S(1)}, f32[8,8,8,128]{3,2,1,0:T(8,128)S(1)}, u32[]{:S(2)}, u32[]{:S(2)}) collective-permute-start(f32[8,8,8,128]{3,2,1,0:T(8,128)S(1)} %pad_maximum_fusion.2), channel_id=1, source_target_pairs={{0,16},{1,17},{2,18},{3,19},{4,20},{5,21},{6,22},{7,23},{8,24},{9,... | collective-permute-start | bytes 786440 | tf_op jit(solution)/shard_map/ppermute | solution.py:694
  56.9 6.5 %collective-permute-start.16 = (f32[240,128]{1,0:T(8,128)}, f32[240,128]{1,0:T(8,128)S(1)}, u32[]{:S(2)}, u32[]{:S(2)}) collective-permute-start(f32[240,128]{1,0:T(8,128)} %get-tuple-element.77), channel_id=1, source_target_pairs={{0,8},{16,24},{8,0},{24,16},{1,9},{17,25},{9,1},{25,17},{2,10},{18... | collective-permute-start | bytes 368648 | tf_op jit(solution)/shard_map/ppermute | solution.py:845
  56.9 6.5 %collective-permute-start.17 = (f32[240,128]{1,0:T(8,128)}, f32[240,128]{1,0:T(8,128)S(1)}, u32[]{:S(2)}, u32[]{:S(2)}) collective-permute-start(f32[240,128]{1,0:T(8,128)} %get-tuple-element.78), channel_id=1, source_target_pairs={{8,16},{16,8},{9,17},{17,9},{10,18},{18,10},{11,19},{19,11},{12,20... | collective-permute-start | bytes 368648 | tf_op jit(solution)/shard_map/ppermute | solution.py:845
  63.4 2.7 %copy-start = (f32[16,8,8,128]{3,2,1,0:T(8,128)}, f32[16,8,8,128]{3,2,1,0:T(8,128)S(1)}, u32[]{:S(2)}) copy-start(f32[16,8,8,128]{3,2,1,0:T(8,128)S(1)} %pad_maximum_fusion.fmine) | copy-start | bytes 1572868
  63.4 15.6 %copy-start.11 = (f32[240,128]{1,0:T(8,128)}, f32[240,128]{1,0:T(8,128)S(1)}, u32[]{:S(2)}) copy-start(f32[240,128]{1,0:T(8,128)S(1)} %collective-permute-done.16.zc) | copy-start | bytes 368644
  63.4 15.6 %copy-start.12 = (f32[240,128]{1,0:T(8,128)}, f32[240,128]{1,0:T(8,128)S(1)}, u32[]{:S(2)}) copy-start(f32[240,128]{1,0:T(8,128)S(1)} %collective-permute-done.17.zd) | copy-start | bytes 368644
  63.5 2.6 %copy-start.5 = (f32[16,8,8,128]{3,2,1,0:T(8,128)}, f32[16,8,8,128]{3,2,1,0:T(8,128)S(1)}, u32[]{:S(2)}) copy-start(f32[16,8,8,128]{3,2,1,0:T(8,128)S(1)} %collective-permute-done.15.ktheirs) | copy-start | bytes 1572868
  63.5 2.6 %collective-permute-start.18 = (f32[16,8,8,128]{3,2,1,0:T(8,128)S(1)}, f32[16,8,8,128]{3,2,1,0:T(8,128)S(1)}, u32[]{:S(2)}, u32[]{:S(2)}) collective-permute-start(f32[16,8,8,128]{3,2,1,0:T(8,128)S(1)} %pad_maximum_fusion.fmine), channel_id=1, source_target_pairs={{0,8},{1,9},{2,10},{3,11},{4,12},{5,13},{6,14},{7,15},{8,0},{9,1},... | collective-permute-start | bytes 1572872 | tf_op jit(solution)/shard_map/ppermute | solution.py:694
  (2 other events, 2.8 us)

commit v5 on v4

--- a/solution.py
+++ b/solution.py
@@ -23,7 +23,7 @@
         out_specs=[VMEM] * len(outs),
         scratch_shapes=[pltpu.VMEM(s, F32) if isinstance(s, tuple) else s for s in scratch],
         cost_estimate=pl.CostEstimate(flops=0, transcendentals=0, bytes_accessed=micros * 3_000_000),
-        compiler_params=pltpu.CompilerParams(vmem_limit_bytes=56 << 20),
+        compiler_params=pltpu.CompilerParams(vmem_limit_bytes=18 << 20),
     )(*args)
 
 

time: 85.8 us -> 71.4 us (0.83)
  Pallas kernels: 34.5 us -> 18.3 us
  waiting for transfers between devices: 13.5 us -> 18.2 us
  starting transfers between devices: 33.6 us -> 31.7 us
  other arithmetic: 1.65 us -> 0.11 us
  local copies, waits for them, and re-layouts: 0.88 us -> 1.93 us
    pallas_call x7, Pallas kernels: 34.5 us -> 18.3 us  [call(): pl.pallas_call(body, out_shape=[jax.ShapeDtypeStruct(s, F32) for s in out...]
    ppermute x9, waiting for transfers between devices: 12.9 us -> 18.2 us  [swap(): lax.ppermute(block, ('gz', 'gy'), [(i, i ^ 1 << step) for i in range(nz *...]
    ppermute x9, starting transfers between devices: 26.3 us -> 23.2 us  [swap(): lax.ppermute(block, ('gz', 'gy'), [(i, i ^ 1 << step) for i in range(nz *...]
    ppermute x10, starting transfers between devices: 7.25 us -> 8.45 us  [exchange(): lax.ppermute(message, axis, pairs + [(j, i) for i, j in pairs])]
    unnamed x31 -> x5, local copies, waits for them, and re-layouts: 0.86 us -> 1.91 us
  transfers between devices with their start and end apart: 19 -> 19, of which waited for: 6 -> 7; matrix products, arithmetic and copies ran while one was open for 2% -> 0% of each run, Pallas kernels for 15% -> 5%
where the time goes in v5:
time: 71.4 us; the launch traced here: 71.1 us
  starting transfers between devices  31.7 us (44%)
  Pallas kernels  18.3 us (26%)
  waiting for transfers between devices  18.2 us (25%)
  local copies, waits for them, and re-layouts  1.93 us (3%)
  between operations  0.87 us (1%)
    ppermute x9, starting transfers between devices, swap(): lax.ppermute(block, ('gz', 'gy'), [(i, i ^ 1 << step) for i in range(nz *...  23.2 us
    pallas_call x7, Pallas kernels, call(): pl.pallas_call(body, out_shape=[jax.ShapeDtypeStruct(s, F32) for s in out...  18.3 us
    ppermute x9, waiting for transfers between devices, swap(): lax.ppermute(block, ('gz', 'gy'), [(i, i ^ 1 << step) for i in range(nz *...  18.2 us
    ppermute x10, starting transfers between devices, exchange(): lax.ppermute(message, axis, pairs + [(j, i) for i, j in pairs])  8.45 us
    unnamed x5, local copies, waits for them, and re-layouts  1.91 us
  transfers between devices with their start and end apart: 19, of which 7 were waited for; matrix products, arithmetic and copies ran while one was open for 0% of the time, Pallas kernels for 5%

profile of v5, /device:TPU:0, one launch (start us, length us, event | category | flops | bytes accessed | tf_op | source)
XLA Modules:
  0.0 71.1 jit_solution(11153151567441280392)
XLA Ops:
  0.6 0.9 %copy-done = f32[8,8,1024]{2,1,0:T(8,128)S(1)} copy-done((f32[8,8,1024]{2,1,0:T(8,128)S(1)}, f32[8,8,1024]{2,1,0:T(8,128)}, u32[]{:S(2)}) %copy-start) | copy-done | bytes 262168
  1.6 0.9 %copy-done.1 = f32[8,8,1024]{2,1,0:T(8,128)S(1)} copy-done((f32[8,8,1024]{2,1,0:T(8,128)S(1)}, f32[8,8,1024]{2,1,0:T(8,128)}, u32[]{:S(2)}) %copy-start.1) | copy-done | bytes 262168
  2.5 1.4 %shard_map.41 = (f32[2,2,8,2,4,4,128]{6,5,4,3,2,1,0:T(4,128)S(1)}, f32[16,2,4,4,128]{4,3,2,1,0:T(4,128)S(1)}, f32[16,2,4,4,128]{4,3,2,1,0:T(4,128)S(1)}) custom-call(f32[8,8,1024]{2,1,0:T(8,128)S(1)} %copy-done, f32[8,8,1024]{2,1,0:T(8,128)S(1)} %copy-done.1), custom_call_target="tpu_custom_call" | custom-call | bytes 9000000 | tf_op jit(solution)/shard_map/pallas_call | solution.py:19
  3.9 3.0 %collective-permute-start = (f32[16,2,4,4,128]{4,3,2,1,0:T(4,128)S(1)}, f32[16,2,4,4,128]{4,3,2,1,0:T(4,128)S(1)}, u32[]{:S(2)}, u32[]{:S(2)}) collective-permute-start(f32[16,2,4,4,128]{4,3,2,1,0:T(4,128)S(1)} %get-tuple-element.45), channel_id=1, source_target_pairs={{0,1},{2,3},{4,5},{6,7},{1,0},{3,2},{5,4},{7,6},{8,9},{10,11},{12,... | collective-permute-start | bytes 786440 | tf_op jit(solution)/shard_map/ppermute | solution.py:845
  6.9 0.7 collective-permute-start.1
  7.6 0.4 shard_map.42
  8.0 0.1 collective-permute-start.2
  8.1 0.7 collective-permute-start.3
  8.8 4.3 %collective-permute-start.4 = (f32[1,8,8,128]{3,2,1,0:T(8,128)S(1)}, f32[1,8,8,128]{3,2,1,0:T(8,128)S(1)}, u32[]{:S(2)}, u32[]{:S(2)}) collective-permute-start(f32[1,8,8,128]{3,2,1,0:T(8,128)S(1)} %bitcast.6), channel_id=1, source_target_pairs={{0,4},{1,5},{2,6},{3,7},{4,0},{5,1},{6,2},{7,3},{8,12},{9,13},{10,... | collective-permute-start | bytes 98312 | tf_op jit(solution)/shard_map/ppermute | solution.py:694
  13.1 5.5 %collective-permute-done.4 = f32[1,8,8,128]{3,2,1,0:T(8,128)S(1)} collective-permute-done((f32[1,8,8,128]{3,2,1,0:T(8,128)S(1)}, f32[1,8,8,128]{3,2,1,0:T(8,128)S(1)}, u32[]{:S(2)}, u32[]{:S(2)}) %collective-permute-start.4) | collective-permute-done | bytes 32800 | tf_op jit(solution)/shard_map/ppermute | solution.py:694
  18.7 2.1 %collective-permute-start.7 = (f32[2,8,8,128]{3,2,1,0:T(8,128)S(1)}, f32[2,8,8,128]{3,2,1,0:T(8,128)S(1)}, u32[]{:S(2)}, u32[]{:S(2)}) collective-permute-start(f32[2,8,8,128]{3,2,1,0:T(8,128)S(1)} %pad_maximum_fusion.5), channel_id=1, source_target_pairs={{0,2},{1,3},{2,0},{3,1},{4,6},{5,7},{6,4},{7,5},{8,10},{9,11},{10,... | collective-permute-start | bytes 196616 | tf_op jit(solution)/shard_map/ppermute | solution.py:694
  20.7 0.2 shard_map.43
  21.0 0.7 collective-permute-start.6
  21.7 1.3 %collective-permute-done.7 = f32[2,8,8,128]{3,2,1,0:T(8,128)S(1)} collective-permute-done((f32[2,8,8,128]{3,2,1,0:T(8,128)S(1)}, f32[2,8,8,128]{3,2,1,0:T(8,128)S(1)}, u32[]{:S(2)}, u32[]{:S(2)}) %collective-permute-start.7) | collective-permute-done | bytes 65568 | tf_op jit(solution)/shard_map/ppermute | solution.py:694
  23.0 2.0 %collective-permute-start.8 = (f32[4,8,8,128]{3,2,1,0:T(8,128)S(1)}, f32[4,8,8,128]{3,2,1,0:T(8,128)S(1)}, u32[]{:S(2)}, u32[]{:S(2)}) collective-permute-start(f32[4,8,8,128]{3,2,1,0:T(8,128)S(1)} %pad_maximum_fusion.3), channel_id=1, source_target_pairs={{0,1},{1,0},{2,3},{3,2},{4,5},{5,4},{6,7},{7,6},{8,9},{9,8},{10,11... | collective-permute-start | bytes 393224 | tf_op jit(solution)/shard_map/ppermute | solution.py:694
  25.0 2.7 %shard_map.44 = (f32[2,18,2,4,8,128]{5,4,3,2,1,0:T(8,128)S(1)}, f32[2,18,2,4,8,128]{5,4,3,2,1,0:T(8,128)S(1)}, f32[2,18,2,4,8,128]{5,4,3,2,1,0:T(8,128)S(1)}, f3...) custom-call(f32[2,2,8,2,4,4,128]{6,5,4,3,2,1,0:T(4,128)S(1)} %get-tu, ...), custom_call_target="tpu_custom_call" | custom-call | bytes 18000000 | tf_op jit(solution)/shard_map/pallas_call | solution.py:19
  27.7 0.3 collective-permute-done.8
  28.1 2.0 %collective-permute-start.9 = (f32[224,128]{1,0:T(8,128)S(1)}, f32[224,128]{1,0:T(8,128)S(1)}, u32[]{:S(2)}, u32[]{:S(2)}) collective-permute-start(f32[224,128]{1,0:T(8,128)S(1)} %get-tuple-element.68), channel_id=1, source_target_pairs={{0,1},{2,3},{4,5},{6,7},{1,0},{3,2},{5,4},{7,6},{8,9},{10,11},{12,... | collective-permute-start | bytes 344072 | tf_op jit(solution)/shard_map/ppermute | solution.py:845
  30.1 0.7 collective-permute-start.11
  30.7 5.2 %collective-permute-start.14 = (f32[8,8,8,128]{3,2,1,0:T(8,128)S(1)}, f32[8,8,8,128]{3,2,1,0:T(8,128)S(1)}, u32[]{:S(2)}, u32[]{:S(2)}) collective-permute-start(f32[8,8,8,128]{3,2,1,0:T(8,128)S(1)} %pad_maximum_fusion.1), channel_id=1, source_target_pairs={{0,16},{1,17},{2,18},{3,19},{4,20},{5,21},{6,22},{7,23},{8,24},{9,... | collective-permute-start | bytes 786440 | tf_op jit(solution)/shard_map/ppermute | solution.py:694
  35.9 3.0 %collective-permute-start.10 = (f32[2,8,8,128]{3,2,1,0:T(8,128)S(1)}, f32[2,8,8,128]{3,2,1,0:T(8,128)S(1)}, u32[]{:S(2)}, u32[]{:S(2)}) collective-permute-start(f32[2,8,8,128]{3,2,1,0:T(8,128)S(1)} %pad_maximum_fusion.6), channel_id=1, source_target_pairs={{0,4},{1,5},{2,6},{3,7},{4,0},{5,1},{6,2},{7,3},{8,12},{9,13},{10,... | collective-permute-start | bytes 196616 | tf_op jit(solution)/shard_map/ppermute | solution.py:694
  38.9 2.8 %collective-permute-done.10 = f32[2,8,8,128]{3,2,1,0:T(8,128)S(1)} collective-permute-done((f32[2,8,8,128]{3,2,1,0:T(8,128)S(1)}, f32[2,8,8,128]{3,2,1,0:T(8,128)S(1)}, u32[]{:S(2)}, u32[]{:S(2)}) %collective-permute-start.10) | collective-permute-done | bytes 65568 | tf_op jit(solution)/shard_map/ppermute | solution.py:694
  41.8 2.7 %collective-permute-start.12 = (f32[4,8,8,128]{3,2,1,0:T(8,128)S(1)}, f32[4,8,8,128]{3,2,1,0:T(8,128)S(1)}, u32[]{:S(2)}, u32[]{:S(2)}) collective-permute-start(f32[4,8,8,128]{3,2,1,0:T(8,128)S(1)} %pad_maximum_fusion.4), channel_id=1, source_target_pairs={{0,2},{1,3},{2,0},{3,1},{4,6},{5,7},{6,4},{7,5},{8,10},{9,11},{10,... | collective-permute-start | bytes 393224 | tf_op jit(solution)/shard_map/ppermute | solution.py:694
  44.6 0.4 shard_map.45
  45.0 2.4 %collective-permute-done.12 = f32[4,8,8,128]{3,2,1,0:T(8,128)S(1)} collective-permute-done((f32[4,8,8,128]{3,2,1,0:T(8,128)S(1)}, f32[4,8,8,128]{3,2,1,0:T(8,128)S(1)}, u32[]{:S(2)}, u32[]{:S(2)}) %collective-permute-start.12) | collective-permute-done | bytes 131104 | tf_op jit(solution)/shard_map/ppermute | solution.py:694
  47.5 2.2 %collective-permute-start.13 = (f32[8,8,8,128]{3,2,1,0:T(8,128)S(1)}, f32[8,8,8,128]{3,2,1,0:T(8,128)S(1)}, u32[]{:S(2)}, u32[]{:S(2)}) collective-permute-start(f32[8,8,8,128]{3,2,1,0:T(8,128)S(1)} %pad_maximum_fusion.2), channel_id=1, source_target_pairs={{0,16},{1,17},{2,18},{3,19},{4,20},{5,21},{6,22},{7,23},{8,24},{9,... | collective-permute-start | bytes 786440 | tf_op jit(solution)/shard_map/ppermute | solution.py:694
  49.7 0.7 collective-permute-start.17
  50.4 4.2 %collective-permute-done.13 = f32[8,8,8,128]{3,2,1,0:T(8,128)S(1)} collective-permute-done((f32[8,8,8,128]{3,2,1,0:T(8,128)S(1)}, f32[8,8,8,128]{3,2,1,0:T(8,128)S(1)}, u32[]{:S(2)}, u32[]{:S(2)}) %collective-permute-start.13) | collective-permute-done | bytes 262176 | tf_op jit(solution)/shard_map/ppermute | solution.py:694
  54.7 1.7 %collective-permute-start.18 = (f32[16,8,8,128]{3,2,1,0:T(8,128)S(1)}, f32[16,8,8,128]{3,2,1,0:T(8,128)S(1)}, u32[]{:S(2)}, u32[]{:S(2)}) collective-permute-start(f32[16,8,8,128]{3,2,1,0:T(8,128)S(1)} %pad_maximum_fusion.fmine), channel_id=1, source_target_pairs={{0,8},{1,9},{2,10},{3,11},{4,12},{5,13},{6,14},{7,15},{8,0},{9,1},... | collective-permute-start | bytes 1572872 | tf_op jit(solution)/shard_map/ppermute | solution.py:694
  56.4 1.5 %collective-permute-done.18.ftheirs_far = f32[16,8,8,128]{3,2,1,0:T(8,128)S(1)} collective-permute-done((f32[16,8,8,128]{3,2,1,0:T(8,128)S(1)}, f32[16,8,8,128]{3,2,1,0:T(8,128)S(1)}, u32[]{:S(2)}, u32[]{:S(2)}) %collective-permute-start.18) | collective-permute-done | bytes 524320 | tf_op jit(solution)/shard_map/ppermute | solution.py:694
  57.9 9.5 %shard_map.46 = (f32[10,4,8,128]{3,2,1,0:T(8,128)S(1)}, f32[2,4,4,128]{3,2,1,0:T(4,128)S(1)}) custom-call(f32[16,8,8,128]{3,2,1,0:T(8,128)S(1)} %pad_maximum_fusion.fmine, f32[16,8,8,128]{3,2,1,0:T(8,128)S(1)} %collective-permute-done.18.ftheirs_far, f32[16,8,8,128]{3,2,1,0:T(8,128)S(1)} %constant_dynamic-update-slice_fusion.kmine, ...), custom_call_target="tpu_custom_call" | custom-call | bytes 33000000 | tf_op jit(solution)/shard_map/pallas_call | solution.py:19
  67.5 3.6 %shard_map.47 = (f32[8,8,1024]{2,1,0:T(8,128)}, f32[8,8,1024]{2,1,0:T(8,128)}) custom-call(f32[2,18,2,4,8,128]{5,4,3,2,1,0:T(8,128)S(1)} %get-tuple-element.59.k, f32[2,18,2,4,8,128]{5,4,3,2,1,0:T(8,128)S(1)} %get-tuple-element.60.g, f32[2,18,2,4,8,128]{5,4,3,2,1,0:T(8,128)S(1)} %get-tuple-element.61.fs, f32[8,2,4,8,128]{4,3,2,1,0:T(8,128)S(1)} %get-tuple-element.62.half, ...), custom_call_target="tpu_custom_call" | custom-call | bytes 18000000 | tf_op jit(solution)/shard_map/pallas_call | solution.py:19
  (27 shorter events, 0.3 us)
Async XLA Ops:
  0.6 1.0 %copy-start = (f32[8,8,1024]{2,1,0:T(8,128)S(1)}, f32[8,8,1024]{2,1,0:T(8,128)}, u32[]{:S(2)}) copy-start(f32[8,8,1024]{2,1,0:T(8,128)} %f_ref.1) | copy-start | bytes 786436
  1.6 0.9 %copy-start.1 = (f32[8,8,1024]{2,1,0:T(8,128)S(1)}, f32[8,8,1024]{2,1,0:T(8,128)}, u32[]{:S(2)}) copy-start(f32[8,8,1024]{2,1,0:T(8,128)} %k_ref.1) | copy-start | bytes 786436
  3.9 14.7 %collective-permute-start = (f32[16,2,4,4,128]{4,3,2,1,0:T(4,128)S(1)}, f32[16,2,4,4,128]{4,3,2,1,0:T(4,128)S(1)}, u32[]{:S(2)}, u32[]{:S(2)}) collective-permute-start(f32[16,2,4,4,128]{4,3,2,1,0:T(4,128)S(1)} %get-tuple-element.45), channel_id=1, source_target_pairs={{0,1},{2,3},{4,5},{6,7},{1,0},{3,2},{5,4},{7,6},{8,9},{10,11},{12,... | collective-permute-start | bytes 786440 | tf_op jit(solution)/shard_map/ppermute | solution.py:845
  6.9 11.7 %collective-permute-start.1 = (f32[16,2,4,4,128]{4,3,2,1,0:T(4,128)S(1)}, f32[16,2,4,4,128]{4,3,2,1,0:T(4,128)S(1)}, u32[]{:S(2)}, u32[]{:S(2)}) collective-permute-start(f32[16,2,4,4,128]{4,3,2,1,0:T(4,128)S(1)} %get-tuple-element.46), channel_id=1, source_target_pairs={{1,2},{3,4},{5,6},{2,1},{4,3},{6,5},{9,10},{11,12},{13,14},{10,9},... | collective-permute-start | bytes 786440 | tf_op jit(solution)/shard_map/ppermute | solution.py:845
  8.0 10.6 %collective-permute-start.2 = (f32[8,4,16,128]{3,2,1,0:T(8,128)S(1)}, f32[8,4,16,128]{3,2,1,0:T(8,128)S(1)}, u32[]{:S(2)}, u32[]{:S(2)}) collective-permute-start(f32[8,4,16,128]{3,2,1,0:T(8,128)S(1)} %get-tuple-element.47), channel_id=1, source_target_pairs={{0,8},{16,24},{8,0},{24,16},{1,9},{17,25},{9,1},{25,17},{2,10},{18... | collective-permute-start | bytes 786440 | tf_op jit(solution)/shard_map/ppermute | solution.py:845
  8.1 10.6 %collective-permute-start.3 = (f32[8,4,16,128]{3,2,1,0:T(8,128)S(1)}, f32[8,4,16,128]{3,2,1,0:T(8,128)S(1)}, u32[]{:S(2)}, u32[]{:S(2)}) collective-permute-start(f32[8,4,16,128]{3,2,1,0:T(8,128)S(1)} %get-tuple-element.48), channel_id=1, source_target_pairs={{8,16},{16,8},{9,17},{17,9},{10,18},{18,10},{11,19},{19,11},{12,20... | collective-permute-start | bytes 786440 | tf_op jit(solution)/shard_map/ppermute | solution.py:845
  8.8 9.8 %collective-permute-start.4 = (f32[1,8,8,128]{3,2,1,0:T(8,128)S(1)}, f32[1,8,8,128]{3,2,1,0:T(8,128)S(1)}, u32[]{:S(2)}, u32[]{:S(2)}) collective-permute-start(f32[1,8,8,128]{3,2,1,0:T(8,128)S(1)} %bitcast.6), channel_id=1, source_target_pairs={{0,4},{1,5},{2,6},{3,7},{4,0},{5,1},{6,2},{7,3},{8,12},{9,13},{10,... | collective-permute-start | bytes 98312 | tf_op jit(solution)/shard_map/ppermute | solution.py:694
  18.7 4.3 %collective-permute-start.7 = (f32[2,8,8,128]{3,2,1,0:T(8,128)S(1)}, f32[2,8,8,128]{3,2,1,0:T(8,128)S(1)}, u32[]{:S(2)}, u32[]{:S(2)}) collective-permute-start(f32[2,8,8,128]{3,2,1,0:T(8,128)S(1)} %pad_maximum_fusion.5), channel_id=1, source_target_pairs={{0,2},{1,3},{2,0},{3,1},{4,6},{5,7},{6,4},{7,5},{8,10},{9,11},{10,... | collective-permute-start | bytes 196616 | tf_op jit(solution)/shard_map/ppermute | solution.py:694
  20.9 2.1 %collective-permute-start.5 = (f32[224,128]{1,0:T(8,128)S(1)}, f32[224,128]{1,0:T(8,128)S(1)}, u32[]{:S(2)}, u32[]{:S(2)}) collective-permute-start(f32[224,128]{1,0:T(8,128)S(1)} %get-tuple-element.54), channel_id=1, source_target_pairs={{0,8},{16,24},{8,0},{24,16},{1,9},{17,25},{9,1},{25,17},{2,10},{18... | collective-permute-start | bytes 344072 | tf_op jit(solution)/shard_map/ppermute | solution.py:845
  21.0 2.0 %collective-permute-start.6 = (f32[224,128]{1,0:T(8,128)S(1)}, f32[224,128]{1,0:T(8,128)S(1)}, u32[]{:S(2)}, u32[]{:S(2)}) collective-permute-start(f32[224,128]{1,0:T(8,128)S(1)} %get-tuple-element.55), channel_id=1, source_target_pairs={{8,16},{16,8},{9,17},{17,9},{10,18},{18,10},{11,19},{19,11},{12,20... | collective-permute-start | bytes 344072 | tf_op jit(solution)/shard_map/ppermute | solution.py:845
  23.0 5.0 %collective-permute-start.8 = (f32[4,8,8,128]{3,2,1,0:T(8,128)S(1)}, f32[4,8,8,128]{3,2,1,0:T(8,128)S(1)}, u32[]{:S(2)}, u32[]{:S(2)}) collective-permute-start(f32[4,8,8,128]{3,2,1,0:T(8,128)S(1)} %pad_maximum_fusion.3), channel_id=1, source_target_pairs={{0,1},{1,0},{2,3},{3,2},{4,5},{5,4},{6,7},{7,6},{8,9},{9,8},{10,11... | collective-permute-start | bytes 393224 | tf_op jit(solution)/shard_map/ppermute | solution.py:694
  28.1 7.8 %collective-permute-start.9 = (f32[224,128]{1,0:T(8,128)S(1)}, f32[224,128]{1,0:T(8,128)S(1)}, u32[]{:S(2)}, u32[]{:S(2)}) collective-permute-start(f32[224,128]{1,0:T(8,128)S(1)} %get-tuple-element.68), channel_id=1, source_target_pairs={{0,1},{2,3},{4,5},{6,7},{1,0},{3,2},{5,4},{7,6},{8,9},{10,11},{12,... | collective-permute-start | bytes 344072 | tf_op jit(solution)/shard_map/ppermute | solution.py:845
  30.1 11.7 %collective-permute-start.11 = (f32[160,128]{1,0:T(8,128)S(1)}, f32[160,128]{1,0:T(8,128)S(1)}, u32[]{:S(2)}, u32[]{:S(2)}) collective-permute-start(f32[160,128]{1,0:T(8,128)S(1)} %get-tuple-element.69), channel_id=1, source_target_pairs={{1,2},{3,4},{5,6},{2,1},{4,3},{6,5},{9,10},{11,12},{13,14},{10,9},... | collective-permute-start | bytes 245768 | tf_op jit(solution)/shard_map/ppermute | solution.py:845
  30.7 13.8 %collective-permute-start.14 = (f32[8,8,8,128]{3,2,1,0:T(8,128)S(1)}, f32[8,8,8,128]{3,2,1,0:T(8,128)S(1)}, u32[]{:S(2)}, u32[]{:S(2)}) collective-permute-start(f32[8,8,8,128]{3,2,1,0:T(8,128)S(1)} %pad_maximum_fusion.1), channel_id=1, source_target_pairs={{0,16},{1,17},{2,18},{3,19},{4,20},{5,21},{6,22},{7,23},{8,24},{9,... | collective-permute-start | bytes 786440 | tf_op jit(solution)/shard_map/ppermute | solution.py:694
  35.9 5.8 %collective-permute-start.10 = (f32[2,8,8,128]{3,2,1,0:T(8,128)S(1)}, f32[2,8,8,128]{3,2,1,0:T(8,128)S(1)}, u32[]{:S(2)}, u32[]{:S(2)}) collective-permute-start(f32[2,8,8,128]{3,2,1,0:T(8,128)S(1)} %pad_maximum_fusion.6), channel_id=1, source_target_pairs={{0,4},{1,5},{2,6},{3,7},{4,0},{5,1},{6,2},{7,3},{8,12},{9,13},{10,... | collective-permute-start | bytes 196616 | tf_op jit(solution)/shard_map/ppermute | solution.py:694
  41.8 5.6 %collective-permute-start.12 = (f32[4,8,8,128]{3,2,1,0:T(8,128)S(1)}, f32[4,8,8,128]{3,2,1,0:T(8,128)S(1)}, u32[]{:S(2)}, u32[]{:S(2)}) collective-permute-start(f32[4,8,8,128]{3,2,1,0:T(8,128)S(1)} %pad_maximum_fusion.4), channel_id=1, source_target_pairs={{0,2},{1,3},{2,0},{3,1},{4,6},{5,7},{6,4},{7,5},{8,10},{9,11},{10,... | collective-permute-start | bytes 393224 | tf_op jit(solution)/shard_map/ppermute | solution.py:694
  44.5 10.2 %collective-permute-start.15 = (f32[16,8,8,128]{3,2,1,0:T(8,128)S(1)}, f32[16,8,8,128]{3,2,1,0:T(8,128)S(1)}, u32[]{:S(2)}, u32[]{:S(2)}) collective-permute-start(f32[16,8,8,128]{3,2,1,0:T(8,128)S(1)} %constant_dynamic-update-slice_fusion.kmine), channel_id=1, source_target_pairs={{0,8},{1,9},{2,10},{3,11},{4,12},{5,13},{6,14},{7,15},{8,0},{9,1},... | collective-permute-start | bytes 1572872 | tf_op jit(solution)/shard_map/ppermute | solution.py:694
  47.5 7.1 %collective-permute-start.13 = (f32[8,8,8,128]{3,2,1,0:T(8,128)S(1)}, f32[8,8,8,128]{3,2,1,0:T(8,128)S(1)}, u32[]{:S(2)}, u32[]{:S(2)}) collective-permute-start(f32[8,8,8,128]{3,2,1,0:T(8,128)S(1)} %pad_maximum_fusion.2), channel_id=1, source_target_pairs={{0,16},{1,17},{2,18},{3,19},{4,20},{5,21},{6,22},{7,23},{8,24},{9,... | collective-permute-start | bytes 786440 | tf_op jit(solution)/shard_map/ppermute | solution.py:694
  49.7 5.0 %collective-permute-start.16 = (f32[240,128]{1,0:T(8,128)S(1)}, f32[240,128]{1,0:T(8,128)S(1)}, u32[]{:S(2)}, u32[]{:S(2)}) collective-permute-start(f32[240,128]{1,0:T(8,128)S(1)} %get-tuple-element.77), channel_id=1, source_target_pairs={{0,8},{16,24},{8,0},{24,16},{1,9},{17,25},{9,1},{25,17},{2,10},{18... | collective-permute-start | bytes 368648 | tf_op jit(solution)/shard_map/ppermute | solution.py:845
  49.7 5.0 %collective-permute-start.17 = (f32[240,128]{1,0:T(8,128)S(1)}, f32[240,128]{1,0:T(8,128)S(1)}, u32[]{:S(2)}, u32[]{:S(2)}) collective-permute-start(f32[240,128]{1,0:T(8,128)S(1)} %get-tuple-element.78), channel_id=1, source_target_pairs={{8,16},{16,8},{9,17},{17,9},{10,18},{18,10},{11,19},{19,11},{12,20... | collective-permute-start | bytes 368648 | tf_op jit(solution)/shard_map/ppermute | solution.py:845
  54.7 3.2 %collective-permute-start.18 = (f32[16,8,8,128]{3,2,1,0:T(8,128)S(1)}, f32[16,8,8,128]{3,2,1,0:T(8,128)S(1)}, u32[]{:S(2)}, u32[]{:S(2)}) collective-permute-start(f32[16,8,8,128]{3,2,1,0:T(8,128)S(1)} %pad_maximum_fusion.fmine), channel_id=1, source_target_pairs={{0,8},{1,9},{2,10},{3,11},{4,12},{5,13},{6,14},{7,15},{8,0},{9,1},... | collective-permute-start | bytes 1572872 | tf_op jit(solution)/shard_map/ppermute | solution.py:694

commit v6 on v5

--- a/solution.py
+++ b/solution.py
@@ -870,8 +870,6 @@
     if whole:
         for step in kswaps[1:-3]:
             kall = swapped(kall, step, nz, ny)
-        ca, cb, kall = lax.optimization_barrier((ca, cb, kall))
-        kall = swapped(kall, kswaps[-3], nz, ny)
     lines, face = (LINES, 2, 4, 8, LANES), (FACE_ROWS, LANES)
     outs = ((2, *lines), (2, *lines), (2, *lines), (8, *lines[1:]), lines, (2, 8, 4, LANES))
     outs += ((FACE_ROWS + 64, LANES), face, coarse)
@@ -884,15 +882,16 @@
     yc, yd = exchange(yc, yd, "gy")
     if whole:
         fall = jnp.stack([message, yc[FACE_ROWS:].reshape(message.shape)])
+        kall = swapped(kall, kswaps[-3], nz, ny)
         fall = swapped(fall, swaps[1], nz, ny)
+        fall, kall = lax.optimization_barrier((fall, kall))
         kall = swapped(kall, kswaps[-2], nz, ny)
-        fall, yc, yd = lax.optimization_barrier((fall, yc, yd))
         for step in swaps[2:-2]:
             fall = swapped(fall, step, nz, ny)
     zface = (ZROWS, LANES)
-    zc, zd = call(widen_kernel, 2, (zface, zface), [(2, *face), sems], ub, yc, yd, specs=[VMEM, FAR, FAR])
+    zc, zd = call(widen_kernel, 1, (zface, zface), [(2, *face), sems], ub, yc, yd, specs=[VMEM, FAR, FAR])
     if whole:
-        fall, zc, zd = lax.optimization_barrier((fall, zc, zd))
+        fall, kall, zc, zd = lax.optimization_barrier((fall, kall, zc, zd))
     zc, zd = exchange(zc, zd, "gz")
     if whole:
         fall = swapped(fall, swaps[-2], nz, ny)

time: 71.4 us -> 74.3 us (1.041)
  the two profiles are of different devices: /device:TPU:0 before, /device:TPU:11 now
where the time goes in v6:
time: 74.3 us; the launch traced here: 74.1 us
  starting transfers between devices  30.3 us (41%)
  waiting for transfers between devices  22.6 us (30%)
  Pallas kernels  18.3 us (25%)
  local copies, waits for them, and re-layouts  1.9 us (3%)
  between operations  0.86 us (1%)
    ppermute x10, starting transfers between devices, exchange(): lax.ppermute(message, axis, pairs + [(j, i) for i, j in pairs])  20.3 us
    pallas_call x7, Pallas kernels, call(): pl.pallas_call(body, out_shape=[jax.ShapeDtypeStruct(s, F32) for s in out...  18.3 us
    ppermute x9, waiting for transfers between devices, swap(): lax.ppermute(block, ('gz', 'gy'), [(i, i ^ 1 << step) for i in range(nz *...  12.1 us
    ppermute x10, waiting for transfers between devices, exchange(): lax.ppermute(message, axis, pairs + [(j, i) for i, j in pairs])  10.5 us
    ppermute x9, starting transfers between devices, swap(): lax.ppermute(block, ('gz', 'gy'), [(i, i ^ 1 << step) for i in range(nz *...  10 us
    unnamed x4, local copies, waits for them, and re-layouts  1.89 us
  transfers between devices with their start and end apart: 19, of which 9 were waited for; matrix products, arithmetic and copies ran while one was open for 0% of the time, Pallas kernels for 1%

profile of v6, /device:TPU:11, one launch (start us, length us, event | category | flops | bytes accessed | tf_op | source)
XLA Modules:
  0.0 74.1 jit_solution(9316298395757432439)
XLA Ops:
  0.6 0.9 %copy-done = f32[8,8,1024]{2,1,0:T(8,128)S(1)} copy-done((f32[8,8,1024]{2,1,0:T(8,128)S(1)}, f32[8,8,1024]{2,1,0:T(8,128)}, u32[]{:S(2)}) %copy-start) | copy-done | bytes 262168
  1.6 0.9 %copy-done.1 = f32[8,8,1024]{2,1,0:T(8,128)S(1)} copy-done((f32[8,8,1024]{2,1,0:T(8,128)S(1)}, f32[8,8,1024]{2,1,0:T(8,128)}, u32[]{:S(2)}) %copy-start.1) | copy-done | bytes 262168
  2.5 1.4 %shard_map.41 = (f32[2,2,8,2,4,4,128]{6,5,4,3,2,1,0:T(4,128)S(1)}, f32[16,2,4,4,128]{4,3,2,1,0:T(4,128)S(1)}, f32[16,2,4,4,128]{4,3,2,1,0:T(4,128)S(1)}) custom-call(f32[8,8,1024]{2,1,0:T(8,128)S(1)} %copy-done, f32[8,8,1024]{2,1,0:T(8,128)S(1)} %copy-done.1), custom_call_target="tpu_custom_call" | custom-call | bytes 9000000 | tf_op jit(solution)/shard_map/pallas_call | solution.py:19
  3.9 0.3 collective-permute-start
  4.2 4.1 %collective-permute-start.1 = (f32[16,2,4,4,128]{4,3,2,1,0:T(4,128)S(1)}, f32[16,2,4,4,128]{4,3,2,1,0:T(4,128)S(1)}, u32[]{:S(2)}, u32[]{:S(2)}) collective-permute-start(f32[16,2,4,4,128]{4,3,2,1,0:T(4,128)S(1)} %get-tuple-element.43), channel_id=1, source_target_pairs={{1,2},{3,4},{5,6},{2,1},{4,3},{6,5},{9,10},{11,12},{13,14},{10,9},... | collective-permute-start | bytes 786440 | tf_op jit(solution)/shard_map/ppermute | solution.py:845
  8.3 0.4 shard_map.42
  8.8 1.3 %collective-permute-start.2 = (f32[8,4,16,128]{3,2,1,0:T(8,128)S(1)}, f32[8,4,16,128]{3,2,1,0:T(8,128)S(1)}, u32[]{:S(2)}, u32[]{:S(2)}) collective-permute-start(f32[8,4,16,128]{3,2,1,0:T(8,128)S(1)} %get-tuple-element.44), channel_id=1, source_target_pairs={{0,8},{16,24},{8,0},{24,16},{1,9},{17,25},{9,1},{25,17},{2,10},{18... | collective-permute-start | bytes 786440 | tf_op jit(solution)/shard_map/ppermute | solution.py:845
  10.1 3.0 %collective-permute-start.3 = (f32[8,4,16,128]{3,2,1,0:T(8,128)S(1)}, f32[8,4,16,128]{3,2,1,0:T(8,128)S(1)}, u32[]{:S(2)}, u32[]{:S(2)}) collective-permute-start(f32[8,4,16,128]{3,2,1,0:T(8,128)S(1)} %get-tuple-element.45), channel_id=1, source_target_pairs={{8,16},{16,8},{9,17},{17,9},{10,18},{18,10},{11,19},{19,11},{12,20... | collective-permute-start | bytes 786440 | tf_op jit(solution)/shard_map/ppermute | solution.py:845
  13.2 3.7 %collective-permute-done.4 = f32[1,8,8,128]{3,2,1,0:T(8,128)S(1)} collective-permute-done((f32[1,8,8,128]{3,2,1,0:T(8,128)S(1)}, f32[1,8,8,128]{3,2,1,0:T(8,128)S(1)}, u32[]{:S(2)}, u32[]{:S(2)}) %collective-permute-start.4) | collective-permute-done | bytes 32800 | tf_op jit(solution)/shard_map/ppermute | solution.py:694
  16.9 1.0 %collective-permute-done.3.zb = f32[8,4,16,128]{3,2,1,0:T(8,128)S(1)} collective-permute-done((f32[8,4,16,128]{3,2,1,0:T(8,128)S(1)}, f32[8,4,16,128]{3,2,1,0:T(8,128)S(1)}, u32[]{:S(2)}, u32[]{:S(2)}) %collective-permute-start.3) | collective-permute-done | bytes 262176 | tf_op jit(solution)/shard_map/ppermute | solution.py:845
  17.9 0.2 collective-permute-start.7
  18.1 0.2 shard_map.43
  18.3 0.8 %collective-permute-start.5 = (f32[224,128]{1,0:T(8,128)S(1)}, f32[224,128]{1,0:T(8,128)S(1)}, u32[]{:S(2)}, u32[]{:S(2)}) collective-permute-start(f32[224,128]{1,0:T(8,128)S(1)} %get-tuple-element.51), channel_id=1, source_target_pairs={{0,8},{16,24},{8,0},{24,16},{1,9},{17,25},{9,1},{25,17},{2,10},{18... | collective-permute-start | bytes 344072 | tf_op jit(solution)/shard_map/ppermute | solution.py:845
  19.1 3.0 %collective-permute-start.6 = (f32[224,128]{1,0:T(8,128)S(1)}, f32[224,128]{1,0:T(8,128)S(1)}, u32[]{:S(2)}, u32[]{:S(2)}) collective-permute-start(f32[224,128]{1,0:T(8,128)S(1)} %get-tuple-element.52), channel_id=1, source_target_pairs={{8,16},{16,8},{9,17},{17,9},{10,18},{18,10},{11,19},{19,11},{12,20... | collective-permute-start | bytes 344072 | tf_op jit(solution)/shard_map/ppermute | solution.py:845
  22.2 3.0 %collective-permute-done.6.cb_far = f32[224,128]{1,0:T(8,128)S(1)} collective-permute-done((f32[224,128]{1,0:T(8,128)S(1)}, f32[224,128]{1,0:T(8,128)S(1)}, u32[]{:S(2)}, u32[]{:S(2)}) %collective-permute-start.6) | collective-permute-done | bytes 114720 | tf_op jit(solution)/shard_map/ppermute | solution.py:845
  25.2 2.7 %shard_map.44 = (f32[2,18,2,4,8,128]{5,4,3,2,1,0:T(8,128)S(1)}, f32[2,18,2,4,8,128]{5,4,3,2,1,0:T(8,128)S(1)}, f32[2,18,2,4,8,128]{5,4,3,2,1,0:T(8,128)S(1)}, f3...) custom-call(f32[2,2,8,2,4,4,128]{6,5,4,3,2,1,0:T(4,128)S(1)} %get-tu, ...), custom_call_target="tpu_custom_call" | custom-call | bytes 18000000 | tf_op jit(solution)/shard_map/pallas_call | solution.py:19
  28.0 1.5 %collective-permute-start.11 = (f32[4,8,8,128]{3,2,1,0:T(8,128)S(1)}, f32[4,8,8,128]{3,2,1,0:T(8,128)S(1)}, u32[]{:S(2)}, u32[]{:S(2)}) collective-permute-start(f32[4,8,8,128]{3,2,1,0:T(8,128)S(1)} %pad_maximum_fusion.4), channel_id=1, source_target_pairs={{0,1},{1,0},{2,3},{3,2},{4,5},{5,4},{6,7},{7,6},{8,9},{9,8},{10,11... | collective-permute-start | bytes 393224 | tf_op jit(solution)/shard_map/ppermute | solution.py:694
  29.5 2.8 %collective-permute-done.8.yc_far.yc = f32[224,128]{1,0:T(8,128)S(1)} collective-permute-done((f32[224,128]{1,0:T(8,128)S(1)}, f32[224,128]{1,0:T(8,128)S(1)}, u32[]{:S(2)}, u32[]{:S(2)}) %collective-permute-start.8) | collective-permute-done | bytes 114720 | tf_op jit(solution)/shard_map/ppermute | solution.py:845
  32.3 1.8 %collective-permute-start.10 = (f32[2,8,8,128]{3,2,1,0:T(8,128)S(1)}, f32[2,8,8,128]{3,2,1,0:T(8,128)S(1)}, u32[]{:S(2)}, u32[]{:S(2)}) collective-permute-start(f32[2,8,8,128]{3,2,1,0:T(8,128)S(1)} %pad_maximum_fusion.7), channel_id=1, source_target_pairs={{0,4},{1,5},{2,6},{3,7},{4,0},{5,1},{6,2},{7,3},{8,12},{9,13},{10,... | collective-permute-start | bytes 196616 | tf_op jit(solution)/shard_map/ppermute | solution.py:694
  34.1 2.4 %collective-permute-done.10 = f32[2,8,8,128]{3,2,1,0:T(8,128)S(1)} collective-permute-done((f32[2,8,8,128]{3,2,1,0:T(8,128)S(1)}, f32[2,8,8,128]{3,2,1,0:T(8,128)S(1)}, u32[]{:S(2)}, u32[]{:S(2)}) %collective-permute-start.10) | collective-permute-done | bytes 65568 | tf_op jit(solution)/shard_map/ppermute | solution.py:694
  36.5 1.4 %collective-permute-start.12 = (f32[4,8,8,128]{3,2,1,0:T(8,128)S(1)}, f32[4,8,8,128]{3,2,1,0:T(8,128)S(1)}, u32[]{:S(2)}, u32[]{:S(2)}) collective-permute-start(f32[4,8,8,128]{3,2,1,0:T(8,128)S(1)} %pad_maximum_fusion.5), channel_id=1, source_target_pairs={{0,2},{1,3},{2,0},{3,1},{4,6},{5,7},{6,4},{7,5},{8,10},{9,11},{10,... | collective-permute-start | bytes 393224 | tf_op jit(solution)/shard_map/ppermute | solution.py:694
  37.9 3.8 %collective-permute-start.9 = (f32[160,128]{1,0:T(8,128)S(1)}, f32[160,128]{1,0:T(8,128)S(1)}, u32[]{:S(2)}, u32[]{:S(2)}) collective-permute-start(f32[160,128]{1,0:T(8,128)S(1)} %get-tuple-element.62), channel_id=1, source_target_pairs={{1,2},{3,4},{5,6},{2,1},{4,3},{6,5},{9,10},{11,12},{13,14},{10,9},... | collective-permute-start | bytes 245768 | tf_op jit(solution)/shard_map/ppermute | solution.py:845
  41.7 2.3 %collective-permute-done.9.yd_far.yd = f32[160,128]{1,0:T(8,128)S(1)} collective-permute-done((f32[160,128]{1,0:T(8,128)S(1)}, f32[160,128]{1,0:T(8,128)S(1)}, u32[]{:S(2)}, u32[]{:S(2)}) %collective-permute-start.9) | collective-permute-done | bytes 81952 | tf_op jit(solution)/shard_map/ppermute | solution.py:845
  44.0 0.4 shard_map.45
  44.4 5.1 %collective-permute-start.15 = (f32[16,8,8,128]{3,2,1,0:T(8,128)S(1)}, f32[16,8,8,128]{3,2,1,0:T(8,128)S(1)}, u32[]{:S(2)}, u32[]{:S(2)}) collective-permute-start(f32[16,8,8,128]{3,2,1,0:T(8,128)S(1)} %pad_maximum_fusion.kmine), channel_id=1, source_target_pairs={{0,8},{1,9},{2,10},{3,11},{4,12},{5,13},{6,14},{7,15},{8,0},{9,1},... | collective-permute-start | bytes 1572872 | tf_op jit(solution)/shard_map/ppermute | solution.py:694
  49.6 0.2 collective-permute-start.16
  49.8 3.6 %collective-permute-start.17 = (f32[240,128]{1,0:T(8,128)S(1)}, f32[240,128]{1,0:T(8,128)S(1)}, u32[]{:S(2)}, u32[]{:S(2)}) collective-permute-start(f32[240,128]{1,0:T(8,128)S(1)} %get-tuple-element.72), channel_id=1, source_target_pairs={{8,16},{16,8},{9,17},{17,9},{10,18},{18,10},{11,19},{19,11},{12,20... | collective-permute-start | bytes 368648 | tf_op jit(solution)/shard_map/ppermute | solution.py:845
  53.4 4.1 %collective-permute-done.14 = f32[8,8,8,128]{3,2,1,0:T(8,128)S(1)} collective-permute-done((f32[8,8,8,128]{3,2,1,0:T(8,128)S(1)}, f32[8,8,8,128]{3,2,1,0:T(8,128)S(1)}, u32[]{:S(2)}, u32[]{:S(2)}) %collective-permute-start.14) | collective-permute-done | bytes 262176 | tf_op jit(solution)/shard_map/ppermute | solution.py:694
  57.5 1.4 %collective-permute-done.17.zd = f32[240,128]{1,0:T(8,128)S(1)} collective-permute-done((f32[240,128]{1,0:T(8,128)S(1)}, f32[240,128]{1,0:T(8,128)S(1)}, u32[]{:S(2)}, u32[]{:S(2)}) %collective-permute-start.17) | collective-permute-done | bytes 122912 | tf_op jit(solution)/shard_map/ppermute | solution.py:845
  59.0 1.9 %collective-permute-done.18.ftheirs_far = f32[16,8,8,128]{3,2,1,0:T(8,128)S(1)} collective-permute-done((f32[16,8,8,128]{3,2,1,0:T(8,128)S(1)}, f32[16,8,8,128]{3,2,1,0:T(8,128)S(1)}, u32[]{:S(2)}, u32[]{:S(2)}) %collective-permute-start.18) | collective-permute-done | bytes 524320 | tf_op jit(solution)/shard_map/ppermute | solution.py:694
  60.9 9.6 %shard_map.46 = (f32[10,4,8,128]{3,2,1,0:T(8,128)S(1)}, f32[2,4,4,128]{3,2,1,0:T(4,128)S(1)}) custom-call(f32[16,8,8,128]{3,2,1,0:T(8,128)S(1)} %pad_maximum_fusion.1.fmine, f32[16,8,8,128]{3,2,1,0:T(8,128)S(1)} %collective-permute-done.18.ftheirs_far, f32[16,8,8,128]{3,2,1,0:T(8,128)S(1)} %pad_maximum_fusion.kmine, ...), custom_call_target="tpu_custom_call" | custom-call | bytes 33000000 | tf_op jit(solution)/shard_map/pallas_call | solution.py:19
  70.4 3.6 %shard_map.47 = (f32[8,8,1024]{2,1,0:T(8,128)}, f32[8,8,1024]{2,1,0:T(8,128)}) custom-call(f32[2,18,2,4,8,128]{5,4,3,2,1,0:T(8,128)S(1)} %get-tuple-element.53.k, f32[2,18,2,4,8,128]{5,4,3,2,1,0:T(8,128)S(1)} %get-tuple-element.54.g, f32[2,18,2,4,8,128]{5,4,3,2,1,0:T(8,128)S(1)} %get-tuple-element.55.fs, f32[8,2,4,8,128]{4,3,2,1,0:T(8,128)S(1)} %get-tuple-element.56.half, ...), custom_call_target="tpu_custom_call" | custom-call | bytes 18000000 | tf_op jit(solution)/shard_map/pallas_call | solution.py:19
  (26 shorter events, 0.4 us)
Async XLA Ops:
  0.6 1.0 %copy-start = (f32[8,8,1024]{2,1,0:T(8,128)S(1)}, f32[8,8,1024]{2,1,0:T(8,128)}, u32[]{:S(2)}) copy-start(f32[8,8,1024]{2,1,0:T(8,128)} %f_ref.1) | copy-start | bytes 786436
  1.6 0.9 %copy-start.1 = (f32[8,8,1024]{2,1,0:T(8,128)S(1)}, f32[8,8,1024]{2,1,0:T(8,128)}, u32[]{:S(2)}) copy-start(f32[8,8,1024]{2,1,0:T(8,128)} %k_ref.1) | copy-start | bytes 786436
  3.9 13.0 %collective-permute-start = (f32[16,2,4,4,128]{4,3,2,1,0:T(4,128)S(1)}, f32[16,2,4,4,128]{4,3,2,1,0:T(4,128)S(1)}, u32[]{:S(2)}, u32[]{:S(2)}) collective-permute-start(f32[16,2,4,4,128]{4,3,2,1,0:T(4,128)S(1)} %get-tuple-element.42), channel_id=1, source_target_pairs={{0,1},{2,3},{4,5},{6,7},{1,0},{3,2},{5,4},{7,6},{8,9},{10,11},{12,... | collective-permute-start | bytes 786440 | tf_op jit(solution)/shard_map/ppermute | solution.py:845
  4.2 12.7 %collective-permute-start.1 = (f32[16,2,4,4,128]{4,3,2,1,0:T(4,128)S(1)}, f32[16,2,4,4,128]{4,3,2,1,0:T(4,128)S(1)}, u32[]{:S(2)}, u32[]{:S(2)}) collective-permute-start(f32[16,2,4,4,128]{4,3,2,1,0:T(4,128)S(1)} %get-tuple-element.43), channel_id=1, source_target_pairs={{1,2},{3,4},{5,6},{2,1},{4,3},{6,5},{9,10},{11,12},{13,14},{10,9},... | collective-permute-start | bytes 786440 | tf_op jit(solution)/shard_map/ppermute | solution.py:845
  8.8 8.1 %collective-permute-start.2 = (f32[8,4,16,128]{3,2,1,0:T(8,128)S(1)}, f32[8,4,16,128]{3,2,1,0:T(8,128)S(1)}, u32[]{:S(2)}, u32[]{:S(2)}) collective-permute-start(f32[8,4,16,128]{3,2,1,0:T(8,128)S(1)} %get-tuple-element.44), channel_id=1, source_target_pairs={{0,8},{16,24},{8,0},{24,16},{1,9},{17,25},{9,1},{25,17},{2,10},{18... | collective-permute-start | bytes 786440 | tf_op jit(solution)/shard_map/ppermute | solution.py:845
  10.1 7.8 %collective-permute-start.3 = (f32[8,4,16,128]{3,2,1,0:T(8,128)S(1)}, f32[8,4,16,128]{3,2,1,0:T(8,128)S(1)}, u32[]{:S(2)}, u32[]{:S(2)}) collective-permute-start(f32[8,4,16,128]{3,2,1,0:T(8,128)S(1)} %get-tuple-element.45), channel_id=1, source_target_pairs={{8,16},{16,8},{9,17},{17,9},{10,18},{18,10},{11,19},{19,11},{12,20... | collective-permute-start | bytes 786440 | tf_op jit(solution)/shard_map/ppermute | solution.py:845
  13.1 3.7 %collective-permute-start.4 = (f32[1,8,8,128]{3,2,1,0:T(8,128)S(1)}, f32[1,8,8,128]{3,2,1,0:T(8,128)S(1)}, u32[]{:S(2)}, u32[]{:S(2)}) collective-permute-start(f32[1,8,8,128]{3,2,1,0:T(8,128)S(1)} %bitcast.6), channel_id=1, source_target_pairs={{0,4},{1,5},{2,6},{3,7},{4,0},{5,1},{6,2},{7,3},{8,12},{9,13},{10,... | collective-permute-start | bytes 98312 | tf_op jit(solution)/shard_map/ppermute | solution.py:694
  17.9 4.3 %collective-permute-start.7 = (f32[2,8,8,128]{3,2,1,0:T(8,128)S(1)}, f32[2,8,8,128]{3,2,1,0:T(8,128)S(1)}, u32[]{:S(2)}, u32[]{:S(2)}) collective-permute-start(f32[2,8,8,128]{3,2,1,0:T(8,128)S(1)} %pad_maximum_fusion.6), channel_id=1, source_target_pairs={{0,2},{1,3},{2,0},{3,1},{4,6},{5,7},{6,4},{7,5},{8,10},{9,11},{10,... | collective-permute-start | bytes 196616 | tf_op jit(solution)/shard_map/ppermute | solution.py:694
  18.3 3.9 %collective-permute-start.5 = (f32[224,128]{1,0:T(8,128)S(1)}, f32[224,128]{1,0:T(8,128)S(1)}, u32[]{:S(2)}, u32[]{:S(2)}) collective-permute-start(f32[224,128]{1,0:T(8,128)S(1)} %get-tuple-element.51), channel_id=1, source_target_pairs={{0,8},{16,24},{8,0},{24,16},{1,9},{17,25},{9,1},{25,17},{2,10},{18... | collective-permute-start | bytes 344072 | tf_op jit(solution)/shard_map/ppermute | solution.py:845
  19.1 6.1 %collective-permute-start.6 = (f32[224,128]{1,0:T(8,128)S(1)}, f32[224,128]{1,0:T(8,128)S(1)}, u32[]{:S(2)}, u32[]{:S(2)}) collective-permute-start(f32[224,128]{1,0:T(8,128)S(1)} %get-tuple-element.52), channel_id=1, source_target_pairs={{8,16},{16,8},{9,17},{17,9},{10,18},{18,10},{11,19},{19,11},{12,20... | collective-permute-start | bytes 344072 | tf_op jit(solution)/shard_map/ppermute | solution.py:845
  27.9 4.3 %collective-permute-start.8 = (f32[224,128]{1,0:T(8,128)S(1)}, f32[224,128]{1,0:T(8,128)S(1)}, u32[]{:S(2)}, u32[]{:S(2)}) collective-permute-start(f32[224,128]{1,0:T(8,128)S(1)} %get-tuple-element.61), channel_id=1, source_target_pairs={{0,1},{2,3},{4,5},{6,7},{1,0},{3,2},{5,4},{7,6},{8,9},{10,11},{12,... | collective-permute-start | bytes 344072 | tf_op jit(solution)/shard_map/ppermute | solution.py:845
  28.0 6.0 %collective-permute-start.11 = (f32[4,8,8,128]{3,2,1,0:T(8,128)S(1)}, f32[4,8,8,128]{3,2,1,0:T(8,128)S(1)}, u32[]{:S(2)}, u32[]{:S(2)}) collective-permute-start(f32[4,8,8,128]{3,2,1,0:T(8,128)S(1)} %pad_maximum_fusion.4), channel_id=1, source_target_pairs={{0,1},{1,0},{2,3},{3,2},{4,5},{5,4},{6,7},{7,6},{8,9},{9,8},{10,11... | collective-permute-start | bytes 393224 | tf_op jit(solution)/shard_map/ppermute | solution.py:694
  32.3 4.2 %collective-permute-start.10 = (f32[2,8,8,128]{3,2,1,0:T(8,128)S(1)}, f32[2,8,8,128]{3,2,1,0:T(8,128)S(1)}, u32[]{:S(2)}, u32[]{:S(2)}) collective-permute-start(f32[2,8,8,128]{3,2,1,0:T(8,128)S(1)} %pad_maximum_fusion.7), channel_id=1, source_target_pairs={{0,4},{1,5},{2,6},{3,7},{4,0},{5,1},{6,2},{7,3},{8,12},{9,13},{10,... | collective-permute-start | bytes 196616 | tf_op jit(solution)/shard_map/ppermute | solution.py:694
  36.5 7.9 %collective-permute-start.13 = (f32[8,8,8,128]{3,2,1,0:T(8,128)S(1)}, f32[8,8,8,128]{3,2,1,0:T(8,128)S(1)}, u32[]{:S(2)}, u32[]{:S(2)}) collective-permute-start(f32[8,8,8,128]{3,2,1,0:T(8,128)S(1)} %pad_maximum_fusion.2), channel_id=1, source_target_pairs={{0,16},{1,17},{2,18},{3,19},{4,20},{5,21},{6,22},{7,23},{8,24},{9,... | collective-permute-start | bytes 786440 | tf_op jit(solution)/shard_map/ppermute | solution.py:694
  36.5 7.8 %collective-permute-start.12 = (f32[4,8,8,128]{3,2,1,0:T(8,128)S(1)}, f32[4,8,8,128]{3,2,1,0:T(8,128)S(1)}, u32[]{:S(2)}, u32[]{:S(2)}) collective-permute-start(f32[4,8,8,128]{3,2,1,0:T(8,128)S(1)} %pad_maximum_fusion.5), channel_id=1, source_target_pairs={{0,2},{1,3},{2,0},{3,1},{4,6},{5,7},{6,4},{7,5},{8,10},{9,11},{10,... | collective-permute-start | bytes 393224 | tf_op jit(solution)/shard_map/ppermute | solution.py:694
  37.9 6.1 %collective-permute-start.9 = (f32[160,128]{1,0:T(8,128)S(1)}, f32[160,128]{1,0:T(8,128)S(1)}, u32[]{:S(2)}, u32[]{:S(2)}) collective-permute-start(f32[160,128]{1,0:T(8,128)S(1)} %get-tuple-element.62), channel_id=1, source_target_pairs={{1,2},{3,4},{5,6},{2,1},{4,3},{6,5},{9,10},{11,12},{13,14},{10,9},... | collective-permute-start | bytes 245768 | tf_op jit(solution)/shard_map/ppermute | solution.py:845
  44.4 14.5 %collective-permute-start.15 = (f32[16,8,8,128]{3,2,1,0:T(8,128)S(1)}, f32[16,8,8,128]{3,2,1,0:T(8,128)S(1)}, u32[]{:S(2)}, u32[]{:S(2)}) collective-permute-start(f32[16,8,8,128]{3,2,1,0:T(8,128)S(1)} %pad_maximum_fusion.kmine), channel_id=1, source_target_pairs={{0,8},{1,9},{2,10},{3,11},{4,12},{5,13},{6,14},{7,15},{8,0},{9,1},... | collective-permute-start | bytes 1572872 | tf_op jit(solution)/shard_map/ppermute | solution.py:694
  49.6 7.9 %collective-permute-start.14 = (f32[8,8,8,128]{3,2,1,0:T(8,128)S(1)}, f32[8,8,8,128]{3,2,1,0:T(8,128)S(1)}, u32[]{:S(2)}, u32[]{:S(2)}) collective-permute-start(f32[8,8,8,128]{3,2,1,0:T(8,128)S(1)} %pad_maximum_fusion.3), channel_id=1, source_target_pairs={{0,16},{1,17},{2,18},{3,19},{4,20},{5,21},{6,22},{7,23},{8,24},{9,... | collective-permute-start | bytes 786440 | tf_op jit(solution)/shard_map/ppermute | solution.py:694
  49.6 7.9 %collective-permute-start.16 = (f32[240,128]{1,0:T(8,128)S(1)}, f32[240,128]{1,0:T(8,128)S(1)}, u32[]{:S(2)}, u32[]{:S(2)}) collective-permute-start(f32[240,128]{1,0:T(8,128)S(1)} %get-tuple-element.71), channel_id=1, source_target_pairs={{0,8},{16,24},{8,0},{24,16},{1,9},{17,25},{9,1},{25,17},{2,10},{18... | collective-permute-start | bytes 368648 | tf_op jit(solution)/shard_map/ppermute | solution.py:845
  49.8 9.2 %collective-permute-start.17 = (f32[240,128]{1,0:T(8,128)S(1)}, f32[240,128]{1,0:T(8,128)S(1)}, u32[]{:S(2)}, u32[]{:S(2)}) collective-permute-start(f32[240,128]{1,0:T(8,128)S(1)} %get-tuple-element.72), channel_id=1, source_target_pairs={{8,16},{16,8},{9,17},{17,9},{10,18},{18,10},{11,19},{19,11},{12,20... | collective-permute-start | bytes 368648 | tf_op jit(solution)/shard_map/ppermute | solution.py:845
  59.0 1.9 %collective-permute-start.18 = (f32[16,8,8,128]{3,2,1,0:T(8,128)S(1)}, f32[16,8,8,128]{3,2,1,0:T(8,128)S(1)}, u32[]{:S(2)}, u32[]{:S(2)}) collective-permute-start(f32[16,8,8,128]{3,2,1,0:T(8,128)S(1)} %pad_maximum_fusion.1.fmine), channel_id=1, source_target_pairs={{0,8},{1,9},{2,10},{3,11},{4,12},{5,13},{6,14},{7,15},{8,0},{9,1},... | collective-permute-start | bytes 1572872 | tf_op jit(solution)/shard_map/ppermute | solution.py:694

commit v7 on v6

--- a/solution.py
+++ b/solution.py
@@ -442,24 +442,29 @@
     return jnp.where((where >= size - step) if step > 0 else (where < -step), 0.0, moved)
 
 
-def coarse_kernel(nz, ny):
-    height, depth = 4 * ny, 2 * nz
-    height2, height3 = height // 2, height // 4
-
-    def body(
-        fmine, ftheirs_far, kmine, ktheirs, error, errorx,
-        f, k, g, fs, half, ur, ub, vr, vb, f2, k2, fc, kc, gc, sc, uc, vc, hc, w3, f3, ftheirs, sem,
-    ):
-        u, v = (ur, ub), (vr, vb)
+class Coarse:
+    def __init__(self, nz, ny):
+        self.nz, self.ny = nz, ny
+        self.height, self.depth = 4 * ny, 2 * nz
+        self.height2, self.height3 = self.height // 2, self.height // 4
+        tile = (self.depth, LANES)
+        self.lines, self.lines2 = (self.height + 2, 2, 2, *tile), (self.height2 + 2, *tile)
+        self.flat2 = (2, self.height2, *tile)
+        self.ready = ((2, *self.lines), (2, *self.lines), self.lines)
+        self.ready += ((2, *self.lines2), self.flat2, self.flat2[1:])
+        self.ready += ((self.height3, 6, *tile), (self.height3, *tile))
+
+    def spread(self, sources, target, swaps):
+        nz, ny = self.nz, self.ny
         zplace, yplace = lax.axis_index("gz"), lax.axis_index("gy")
 
-        def slot(i, j, swaps):
+        def slot(i, j):
             apart = (zplace * ny + yplace) ^ (i * ny + j)
             return sum(((apart >> step) & 1) << bit for bit, step in enumerate(swaps[:-1]))
 
-        def spread(odd, sources, target, swaps):
+        def run(odd):
             def visit(j, carry):
-                order = [slot(i, j, swaps) for i in range(nz)]
+                order = [slot(i, j) for i in range(nz)]
                 for m in range(8):
                     pieces = [sources[(i + odd) % 2][order[i], m] for i in range(nz)]
                     for row in range(4):
@@ -469,39 +474,125 @@
 
             lax.fori_loop(0, ny, visit, 0)
 
-        def spread_either(*args):
-            for odd in range(2):
-                pl.when(lax.rem(zplace, 2) == odd)(lambda odd=odd: spread(odd, *args))
-
-        copy = pltpu.make_async_copy(ftheirs_far, ftheirs, sem)
-        copy.start()
-        spread_either((kmine, ktheirs), k, swap_steps(nz, ny))
-        copy.wait()
-        spread_either((fmine, ftheirs), f, swap_steps(nz, ny, 0))
+        for odd in range(2):
+            pl.when(lax.rem(zplace, 2) == odd)(lambda odd=odd: run(odd))
+
+    def zero(self, c, y):
+        even = iota(0, self.depth) % 2 == 0
+        return even if (y + c) % 2 == 0 else jnp.logical_not(even)
+
+    def around(self, ref, c, y):
+        mid = ref[1 + y]
+        other = jnp.where(self.zero(c, y), shifted(mid, -1, 1), shifted(mid, 1, 1))
+        return (mid + other) + (shifted(mid, -1, 0) + shifted(mid, 1, 0)) + (ref[y] + ref[y + 2])
+
+    def paired(self, a, b):
+        total = (a + b) * 0.125
+        even = iota(0, self.depth) % 2 == 0
+        return jnp.where(even, total + pltpu.roll(total, self.depth - 1, axis=0), 0.0)
+
+
+MOVES = ((-2, 0), (2, 0), (-1, 1), (1, 1))
+
+
+def prepare_coarse(kmine, ktheirs, nz, ny):
+    grid = Coarse(nz, ny)
+    height, depth, height2, height3 = grid.height, grid.depth, grid.height2, grid.height3
+
+    def body(kmine, ktheirs, k, g, half, kc, gc, hc, w3, g3, k2):
+        grid.spread((kmine, ktheirs), k, swap_steps(nz, ny))
+        blank = jnp.zeros((depth, LANES), F32)
+        for c in range(2):
+            for line in (0, height + 1):
+                for e in range(2):
+                    for s in range(2):
+                        k[c, line, e, s] = blank
+            for line in (0, height2 + 1):
+                kc[c, line] = blank
+
+        def prepare(line, parity):
+            for c in range(2):
+                for e in range(2):
+                    for s in range(2):
+                        _, total = diagonal(k.at[c], k.at[1 - c], line, e, s, (e + parity + c) % 2, 2, closed)
+                        g[c, line, e, s] = 1.0 / total
+                        if c == 0:
+                            half[line, e, s] = 0.125 * total
+
+        over_lines(0, height - 1, 1, prepare, 4)
+
+        def restrict(i, carry):
+            for s in range(2):
+                total = None
+                for j in range(2):
+                    for e in range(2):
+                        part = k[0, 1 + 2 * i + j, e, s] + k[1, 1 + 2 * i + j, e, s]
+                        total = part if total is None else total + part
+                k2[s, i] = total * 0.125
+            return carry
+
+        lax.fori_loop(0, height2, restrict, 0)
+        for c in range(2):
+            for y in range(height2):
+                kc[c, 1 + y] = jnp.where(grid.zero(c, y), k2[0, y], k2[1, y])
+        for c in range(2):
+            for y in range(height2):
+                total = 6.0 * kc[c, 1 + y] + grid.around(kc.at[1 - c], c, y)
+                gc[c, y] = 1.0 / total
+                if c == 0:
+                    hc[y] = total * (0.5 / 16.0)
+        conduct = []
+        for y in range(height3):
+            conduct.append(grid.paired(*[kc[0, 1 + 2 * y + j] + kc[1, 1 + 2 * y + j] for j in range(2)]))
+        even = iota(0, depth) % 2 == 0
+        lane, row = iota(1, depth), iota(0, depth)
+        open_faces = (row >= 2, row < depth - 2, lane >= 1, lane < LANES - 1)
+        for y in range(height3):
+            centre = conduct[y]
+            beside = [shifted(centre, step, axis) for step, axis in MOVES]
+            beside.append(conduct[y - 1] if y else jnp.zeros_like(centre))
+            beside.append(conduct[y + 1] if y + 1 < height3 else jnp.zeros_like(centre))
+            total = 6.0 * centre
+            for part in beside:
+                total = total + part
+            scale = jnp.where(even, 1.0 / jnp.where(even, total, 1.0), 0.0)
+            g3[y] = scale
+            for i in range(6):
+                weight = (centre + beside[i]) * scale
+                w3[y, i] = jnp.where(open_faces[i], weight, 0.0) if i < 4 else weight
+
+    return call(body, 4, grid.ready, [grid.flat2], kmine, ktheirs)
+
+
+def coarse_kernel(nz, ny):
+    grid = Coarse(nz, ny)
+    height, depth, height2, height3 = grid.height, grid.depth, grid.height2, grid.height3
+
+    def body(
+        fmine, ftheirs, k, g, half, kc, gc, hc, w3, g3, error, errorx,
+        f, fs, ur, ub, vr, vb, f2, fc, sc, uc, vc, f3,
+    ):
+        u, v = (ur, ub), (vr, vb)
+        zplace, yplace = lax.axis_index("gz"), lax.axis_index("gy")
+        grid.spread((fmine, ftheirs), f, swap_steps(nz, ny, 0))
         blank = jnp.zeros((depth, LANES), F32)
         for line in (0, height + 1):
             for e in range(2):
                 for s in range(2):
                     for c in range(2):
-                        k[c, line, e, s] = blank
                         u[c][line, e, s] = blank
                         v[c][line, e, s] = blank
 
-        def prepare(c):
-            def visit(line, parity):
-                for e in range(2):
-                    for s in range(2):
-                        centre, total = diagonal(k.at[c], k.at[1 - c], line, e, s, (e + parity + c) % 2, 2, closed)
-                        scale = 1.0 / total
-                        start = 8.0 * f[c, line, e, s] * scale
-                        g[c, line, e, s] = scale
-                        fs[c, line, e, s] = start
-                        if c == 0:
-                            half[line, e, s] = 0.125 * total
-                            ur[line, e, s] = start
-                            vr[line, e, s] = centre * start
-
-            over_lines(0, height - 1, 1, visit, 8)
+        def begin(line, parity):
+            for e in range(2):
+                for s in range(2):
+                    start = 8.0 * f[0, line, e, s] * g[0, line, e, s]
+                    fs[0, line, e, s] = start
+                    ur[line, e, s] = start
+                    vr[line, e, s] = k[0, line, e, s] * start
+                    fs[1, line, e, s] = 8.0 * f[1, line, e, s] * g[1, line, e, s]
+
+        over_lines(0, height - 1, 1, begin, 8)
 
         def fresh(c, line, parity, e, s):
             q = (e + parity + c) % 2
@@ -519,64 +610,42 @@
 
             over_lines(0, height - 1, 1, visit, 8)
 
-        prepare(0)
-        prepare(1)
         relax(1)
         relax(0)
         relax(1)
 
-        def restrict(i, carry):
+        def restrict(line, parity):
+            i = (line - 1) // 2
             for s in range(2):
-                value, conduct = None, None
+                value = None
                 for j in range(2):
-                    line = 1 + 2 * i + j
                     for e in range(2):
-                        part = half[line, e, s] * (fresh(0, line, j, e, s) - ur[line, e, s])
+                        at = 1 + 2 * i + j
+                        part = half[at, e, s] * (fresh(0, at, j, e, s) - ur[at, e, s])
                         value = part if value is None else value + part
-                        part = k[0, line, e, s] + k[1, line, e, s]
-                        conduct = part if conduct is None else conduct + part
                 f2[s, i] = value * 0.125
-                k2[s, i] = conduct * 0.125
+
+        def restrict_pairs(i, carry):
+            for j in range(2):
+                restrict(1 + 2 * (2 * i + j), 0)
             return carry
 
-        lax.fori_loop(0, height2, restrict, 0)
-
-        even = iota(0, depth) % 2 == 0
-
-        def q_is_zero(c, y):
-            return even if (y + c) % 2 == 0 else jnp.logical_not(even)
-
-        def coloured(pair, c, y):
-            return jnp.where(q_is_zero(c, y), pair[0], pair[1])
-
-        def around(ref, c, y):
-            mid = ref[1 + y]
-            other = jnp.where(q_is_zero(c, y), shifted(mid, -1, 1), shifted(mid, 1, 1))
-            return (mid + other) + (shifted(mid, -1, 0) + shifted(mid, 1, 0)) + (ref[y] + ref[y + 2])
+        lax.fori_loop(0, height2 // 2, restrict_pairs, 0)
 
         for c in range(2):
             for line in (0, height2 + 1):
-                kc[c, line] = blank
                 uc[c, line] = blank
                 vc[c, line] = blank
             for y in range(height2):
-                kc[c, 1 + y] = coloured((k2[0, y], k2[1, y]), c, y)
-                fc[c, y] = coloured((f2[0, y], f2[1, y]), c, y)
-        for c in range(2):
-            for y in range(height2):
-                centre = kc[c, 1 + y]
-                total = 6.0 * centre + around(kc.at[1 - c], c, y)
-                scale = 1.0 / total
-                start = 32.0 * fc[c, y] * scale
-                gc[c, y] = scale
+                right = jnp.where(grid.zero(c, y), f2[0, y], f2[1, y])
+                start = 32.0 * right * gc[c, y]
                 sc[c, y] = start
                 if c == 0:
-                    hc[y] = total * (0.5 / 16.0)
                     uc[0, 1 + y] = start
-                    vc[0, 1 + y] = centre * start
+                    vc[0, 1 + y] = kc[0, 1 + y] * start
 
         def fresh2(c, y):
-            flow = kc[c, 1 + y] * around(uc.at[1 - c], c, y) + around(vc.at[1 - c], c, y)
+            flow = kc[c, 1 + y] * grid.around(uc.at[1 - c], c, y) + grid.around(vc.at[1 - c], c, y)
             return sc[c, y] + gc[c, y] * flow
 
         def relax2(c):
@@ -589,33 +658,9 @@
         relax2(0)
         relax2(1)
 
-        def paired(a, b):
-            total = (a + b) * 0.125
-            return jnp.where(even, total + pltpu.roll(total, depth - 1, axis=0), 0.0)
-
-        conduct = []
-        right = []
         for y in range(height3):
             parts = [hc[2 * y + j] * (fresh2(0, 2 * y + j) - uc[0, 1 + 2 * y + j]) for j in range(2)]
-            right.append(paired(*parts))
-            parts = [kc[0, 1 + 2 * y + j] + kc[1, 1 + 2 * y + j] for j in range(2)]
-            conduct.append(paired(*parts))
-        moves = ((-2, 0), (2, 0), (-1, 1), (1, 1))
-        for y in range(height3):
-            centre = conduct[y]
-            beside = [shifted(centre, step, axis) for step, axis in moves]
-            beside.append(conduct[y - 1] if y else jnp.zeros_like(centre))
-            beside.append(conduct[y + 1] if y + 1 < height3 else jnp.zeros_like(centre))
-            total = 6.0 * centre
-            for part in beside:
-                total = total + part
-            scale = jnp.where(even, 1.0 / jnp.where(even, total, 1.0), 0.0)
-            f3[y] = 128.0 * right[y] * scale
-            lane, row = iota(1, depth), iota(0, depth)
-            open_faces = (row >= 2, row < depth - 2, lane >= 1, lane < LANES - 1)
-            for i in range(6):
-                weight = (centre + beside[i]) * scale
-                w3[y, i] = jnp.where(open_faces[i], weight, 0.0) if i < 4 else weight
+            f3[y] = 128.0 * grid.paired(*parts) * g3[y]
         mixed = (iota(0, depth) // 2 + iota(1, depth)) % 2
 
         def relax3(c, field):
@@ -623,7 +668,7 @@
             for y in range(height3):
                 mid = field[y]
                 value = f3[y]
-                for i, (step, axis) in enumerate(moves):
+                for i, (step, axis) in enumerate(MOVES):
                     value = value + w3[y, i] * pltpu.roll(mid, -step % mid.shape[axis], axis=axis)
                 if y:
                     value = value + w3[y, 4] * field[y - 1]
@@ -646,7 +691,7 @@
             relax2(c)
 
         for y in range(height2):
-            zero = q_is_zero(0, y)
+            zero = grid.zero(0, y)
             red, black = uc[0, 1 + y], uc[1, 1 + y]
             f2[0, y] = jnp.where(zero, red, black)
             f2[1, y] = jnp.where(zero, black, red)
@@ -674,12 +719,9 @@
                     elif 0 <= j < 8 // 2:
                         errorx[1 if t < 0 else 0, j, s : s + 1, :] = row
 
-    lines, lines2 = (height + 2, 2, 2, depth, LANES), (height2 + 2, depth, LANES)
-    flat2 = (2, height2, depth, LANES)
-    scratch = [(2, *lines)] * 4 + [lines] * 5 + [flat2, flat2, flat2, (2, *lines2), flat2, flat2]
-    scratch += [(2, *lines2), (2, *lines2), flat2[1:], (height3, 6, depth, LANES), (height3, depth, LANES)]
-    scratch += [(nz * ny // 2, 8, 8, LANES), pltpu.SemaphoreType.DMA(())]
-    return body, scratch
+    lines, lines2, flat2 = grid.lines, grid.lines2, grid.flat2
+    scratch = [(2, *lines), (2, *lines), *[lines] * 4, flat2, flat2, flat2, (2, *lines2), (2, *lines2)]
+    return body, scratch + [(height3, depth, LANES)]
 
 
 def swap_steps(nz, ny, first=None):
@@ -698,10 +740,10 @@
     return jnp.concatenate([block, swap(block, step, nz, ny)])
 
 
-def solve_coarse(fmine, ftheirs, kmine, ktheirs, nz, ny):
+def solve_coarse(fmine, ftheirs, ready, nz, ny):
     body, scratch = coarse_kernel(nz, ny)
     outs = ((10, 4, 8, LANES), (2, 4, 4, LANES))
-    return call(body, 11, outs, scratch, fmine, ftheirs, kmine, ktheirs, specs=[VMEM, FAR, VMEM, VMEM])
+    return call(body, 8, outs, scratch, fmine, ftheirs, *ready)
 
 
 def extended(array, sides, width):
@@ -863,7 +905,7 @@
     kall = kmessage[None]
     if whole:
         kall = swapped(kall, kswaps[0], nz, ny)
-        ya, yb, za, zb, kall = lax.optimization_barrier((ya, yb, za, zb, kall))
+        ya, yb, kall = lax.optimization_barrier((ya, yb, kall))
     relayed, sems = (8 * CORNER_ROWS, LANES), pltpu.SemaphoreType.DMA((2,))
     corners = call(relay_kernel, 2, (relayed, relayed), [(2, *yface), sems], ya, yb, specs=[FAR] * 2)
     ca, cb = exchange(*corners, "gz")
@@ -884,21 +926,22 @@
         fall = jnp.stack([message, yc[FACE_ROWS:].reshape(message.shape)])
         kall = swapped(kall, kswaps[-3], nz, ny)
         fall = swapped(fall, swaps[1], nz, ny)
-        fall, kall = lax.optimization_barrier((fall, kall))
+        fall, kall, yc, yd = lax.optimization_barrier((fall, kall, yc, yd))
         kall = swapped(kall, kswaps[-2], nz, ny)
         for step in swaps[2:-2]:
             fall = swapped(fall, step, nz, ny)
     zface = (ZROWS, LANES)
     zc, zd = call(widen_kernel, 1, (zface, zface), [(2, *face), sems], ub, yc, yd, specs=[VMEM, FAR, FAR])
     if whole:
-        fall, kall, zc, zd = lax.optimization_barrier((fall, kall, zc, zd))
+        fall, zc, zd = lax.optimization_barrier((fall, zc, zd))
     zc, zd = exchange(zc, zd, "gz")
     if whole:
         fall = swapped(fall, swaps[-2], nz, ny)
         ktheirs = swap(kall, kswaps[-1], nz, ny)
-        fall, kall, ktheirs, zc, zd = lax.optimization_barrier((fall, kall, ktheirs, zc, zd))
+        ready = prepare_coarse(kall, ktheirs, nz, ny)
+        fall, zc, zd, *ready = lax.optimization_barrier((fall, zc, zd, *ready))
         ftheirs = swap(fall, swaps[-1], nz, ny)
-        error, errorx = solve_coarse(fall, ftheirs, kall, ktheirs, nz, ny)
+        error, errorx = solve_coarse(fall, ftheirs, ready, nz, ny)
     else:
         error, errorx = solve_coarse_spread(message, kmessage, nz, ny)
     block = (8, 8, 8 * LANES)

time: 74.3 us -> 72.1 us (0.970)
  the two profiles are of different devices: /device:TPU:11 before, /device:TPU:0 now
where the time goes in v7:
time: 72.1 us; the launch traced here: 71.9 us
  waiting for transfers between devices  25.5 us (35%)
  starting transfers between devices  25.4 us (35%)
  Pallas kernels  18.1 us (25%)
  local copies, waits for them, and re-layouts  1.93 us (3%)
  between operations  0.88 us (1%)
    ppermute x9, waiting for transfers between devices, swap(): lax.ppermute(block, ('gz', 'gy'), [(i, i ^ 1 << step) for i in range(nz *...  23.4 us
    pallas_call x8, Pallas kernels, call(): pl.pallas_call(body, out_shape=[jax.ShapeDtypeStruct(s, F32) for s in out...  18.1 us
    ppermute x9, starting transfers between devices, swap(): lax.ppermute(block, ('gz', 'gy'), [(i, i ^ 1 << step) for i in range(nz *...  16.9 us
    ppermute x10, starting transfers between devices, exchange(): lax.ppermute(message, axis, pairs + [(j, i) for i, j in pairs])  8.54 us
    ppermute x10, waiting for transfers between devices, exchange(): lax.ppermute(message, axis, pairs + [(j, i) for i, j in pairs])  2.13 us
    unnamed x5, local copies, waits for them, and re-layouts  1.91 us
  transfers between devices with their start and end apart: 19, of which 7 were waited for; matrix products, arithmetic and copies ran while one was open for 0% of the time, Pallas kernels for 4%

profile of v7, /device:TPU:0, one launch (start us, length us, event | category | flops | bytes accessed | tf_op | source)
XLA Modules:
  0.0 71.9 jit_solution(14796023668487700259)
XLA Ops:
  0.6 0.9 %copy-done = f32[8,8,1024]{2,1,0:T(8,128)S(1)} copy-done((f32[8,8,1024]{2,1,0:T(8,128)S(1)}, f32[8,8,1024]{2,1,0:T(8,128)}, u32[]{:S(2)}) %copy-start) | copy-done | bytes 262168
  1.6 0.9 %copy-done.1 = f32[8,8,1024]{2,1,0:T(8,128)S(1)} copy-done((f32[8,8,1024]{2,1,0:T(8,128)S(1)}, f32[8,8,1024]{2,1,0:T(8,128)}, u32[]{:S(2)}) %copy-start.1) | copy-done | bytes 262168
  2.5 1.4 %shard_map.41 = (f32[2,2,8,2,4,4,128]{6,5,4,3,2,1,0:T(4,128)S(1)}, f32[16,2,4,4,128]{4,3,2,1,0:T(4,128)S(1)}, f32[16,2,4,4,128]{4,3,2,1,0:T(4,128)S(1)}) custom-call(f32[8,8,1024]{2,1,0:T(8,128)S(1)} %copy-done, f32[8,8,1024]{2,1,0:T(8,128)S(1)} %copy-done.1), custom_call_target="tpu_custom_call" | custom-call | bytes 9000000 | tf_op jit(solution)/shard_map/pallas_call | solution.py:19
  3.9 3.0 %collective-permute-start = (f32[16,2,4,4,128]{4,3,2,1,0:T(4,128)S(1)}, f32[16,2,4,4,128]{4,3,2,1,0:T(4,128)S(1)}, u32[]{:S(2)}, u32[]{:S(2)}) collective-permute-start(f32[16,2,4,4,128]{4,3,2,1,0:T(4,128)S(1)} %get-tuple-element.55), channel_id=1, source_target_pairs={{0,1},{2,3},{4,5},{6,7},{1,0},{3,2},{5,4},{7,6},{8,9},{10,11},{12,... | collective-permute-start | bytes 786440 | tf_op jit(solution)/shard_map/ppermute | solution.py:887
  6.9 0.7 collective-permute-start.1
  7.6 0.4 shard_map.42
  8.0 4.3 %collective-permute-start.2 = (f32[1,8,8,128]{3,2,1,0:T(8,128)S(1)}, f32[1,8,8,128]{3,2,1,0:T(8,128)S(1)}, u32[]{:S(2)}, u32[]{:S(2)}) collective-permute-start(f32[1,8,8,128]{3,2,1,0:T(8,128)S(1)} %bitcast.6), channel_id=1, source_target_pairs={{0,4},{1,5},{2,6},{3,7},{4,0},{5,1},{6,2},{7,3},{8,12},{9,13},{10,... | collective-permute-start | bytes 98312 | tf_op jit(solution)/shard_map/ppermute | solution.py:736
  12.3 0.7 collective-permute-start.4
  13.0 5.6 %collective-permute-done.2 = f32[1,8,8,128]{3,2,1,0:T(8,128)S(1)} collective-permute-done((f32[1,8,8,128]{3,2,1,0:T(8,128)S(1)}, f32[1,8,8,128]{3,2,1,0:T(8,128)S(1)}, u32[]{:S(2)}, u32[]{:S(2)}) %collective-permute-start.2) | collective-permute-done | bytes 32800 | tf_op jit(solution)/shard_map/ppermute | solution.py:736
  18.7 2.0 %collective-permute-start.7 = (f32[2,8,8,128]{3,2,1,0:T(8,128)S(1)}, f32[2,8,8,128]{3,2,1,0:T(8,128)S(1)}, u32[]{:S(2)}, u32[]{:S(2)}) collective-permute-start(f32[2,8,8,128]{3,2,1,0:T(8,128)S(1)} %pad_maximum_fusion.5), channel_id=1, source_target_pairs={{0,2},{1,3},{2,0},{3,1},{4,6},{5,7},{6,4},{7,5},{8,10},{9,11},{10,... | collective-permute-start | bytes 196616 | tf_op jit(solution)/shard_map/ppermute | solution.py:736
  20.7 0.2 shard_map.43
  21.0 0.7 collective-permute-start.6
  21.6 1.4 %collective-permute-done.7 = f32[2,8,8,128]{3,2,1,0:T(8,128)S(1)} collective-permute-done((f32[2,8,8,128]{3,2,1,0:T(8,128)S(1)}, f32[2,8,8,128]{3,2,1,0:T(8,128)S(1)}, u32[]{:S(2)}, u32[]{:S(2)}) %collective-permute-start.7) | collective-permute-done | bytes 65568 | tf_op jit(solution)/shard_map/ppermute | solution.py:736
  23.0 2.8 %shard_map.44 = (f32[2,18,2,4,8,128]{5,4,3,2,1,0:T(8,128)S(1)}, f32[2,18,2,4,8,128]{5,4,3,2,1,0:T(8,128)S(1)}, f32[2,18,2,4,8,128]{5,4,3,2,1,0:T(8,128)S(1)}, f3...) custom-call(f32[2,2,8,2,4,4,128]{6,5,4,3,2,1,0:T(4,128)S(1)} %get-tu, ...), custom_call_target="tpu_custom_call" | custom-call | bytes 18000000 | tf_op jit(solution)/shard_map/pallas_call | solution.py:19
  25.8 1.9 %collective-permute-start.8 = (f32[224,128]{1,0:T(8,128)S(1)}, f32[224,128]{1,0:T(8,128)S(1)}, u32[]{:S(2)}, u32[]{:S(2)}) collective-permute-start(f32[224,128]{1,0:T(8,128)S(1)} %get-tuple-element.73), channel_id=1, source_target_pairs={{0,1},{2,3},{4,5},{6,7},{1,0},{3,2},{5,4},{7,6},{8,9},{10,11},{12,... | collective-permute-start | bytes 344072 | tf_op jit(solution)/shard_map/ppermute | solution.py:887
  27.7 0.2 collective-permute-start.10
  27.9 0.7 collective-permute-start.11
  28.6 2.1 %collective-permute-done.8.yc_far.yc = f32[224,128]{1,0:T(8,128)S(1)} collective-permute-done((f32[224,128]{1,0:T(8,128)S(1)}, f32[224,128]{1,0:T(8,128)S(1)}, u32[]{:S(2)}, u32[]{:S(2)}) %collective-permute-start.8) | collective-permute-done | bytes 114720 | tf_op jit(solution)/shard_map/ppermute | solution.py:887
  30.7 3.6 %collective-permute-start.9 = (f32[2,8,8,128]{3,2,1,0:T(8,128)S(1)}, f32[2,8,8,128]{3,2,1,0:T(8,128)S(1)}, u32[]{:S(2)}, u32[]{:S(2)}) collective-permute-start(f32[2,8,8,128]{3,2,1,0:T(8,128)S(1)} %pad_maximum_fusion.6), channel_id=1, source_target_pairs={{0,4},{1,5},{2,6},{3,7},{4,0},{5,1},{6,2},{7,3},{8,12},{9,13},{10,... | collective-permute-start | bytes 196616 | tf_op jit(solution)/shard_map/ppermute | solution.py:736
  34.3 3.0 %collective-permute-done.9 = f32[2,8,8,128]{3,2,1,0:T(8,128)S(1)} collective-permute-done((f32[2,8,8,128]{3,2,1,0:T(8,128)S(1)}, f32[2,8,8,128]{3,2,1,0:T(8,128)S(1)}, u32[]{:S(2)}, u32[]{:S(2)}) %collective-permute-start.9) | collective-permute-done | bytes 65568 | tf_op jit(solution)/shard_map/ppermute | solution.py:736
  37.3 4.2 %collective-permute-start.16 = (f32[8,8,8,128]{3,2,1,0:T(8,128)S(1)}, f32[8,8,8,128]{3,2,1,0:T(8,128)S(1)}, u32[]{:S(2)}, u32[]{:S(2)}) collective-permute-start(f32[8,8,8,128]{3,2,1,0:T(8,128)S(1)} %pad_maximum_fusion.1), channel_id=1, source_target_pairs={{0,16},{1,17},{2,18},{3,19},{4,20},{5,21},{6,22},{7,23},{8,24},{9,... | collective-permute-start | bytes 786440 | tf_op jit(solution)/shard_map/ppermute | solution.py:736
  41.5 2.1 %collective-permute-start.12 = (f32[4,8,8,128]{3,2,1,0:T(8,128)S(1)}, f32[4,8,8,128]{3,2,1,0:T(8,128)S(1)}, u32[]{:S(2)}, u32[]{:S(2)}) collective-permute-start(f32[4,8,8,128]{3,2,1,0:T(8,128)S(1)} %pad_maximum_fusion.4), channel_id=1, source_target_pairs={{0,2},{1,3},{2,0},{3,1},{4,6},{5,7},{6,4},{7,5},{8,10},{9,11},{10,... | collective-permute-start | bytes 393224 | tf_op jit(solution)/shard_map/ppermute | solution.py:736
  43.6 4.0 %collective-permute-done.16 = f32[8,8,8,128]{3,2,1,0:T(8,128)S(1)} collective-permute-done((f32[8,8,8,128]{3,2,1,0:T(8,128)S(1)}, f32[8,8,8,128]{3,2,1,0:T(8,128)S(1)}, u32[]{:S(2)}, u32[]{:S(2)}) %collective-permute-start.16) | collective-permute-done | bytes 262176 | tf_op jit(solution)/shard_map/ppermute | solution.py:736
  47.8 0.4 shard_map.45
  48.2 0.4 collective-permute-start.13
  48.6 0.2 collective-permute-start.14
  48.8 0.7 collective-permute-start.15
  49.5 7.5 %collective-permute-done.13 = f32[8,8,8,128]{3,2,1,0:T(8,128)S(1)} collective-permute-done((f32[8,8,8,128]{3,2,1,0:T(8,128)S(1)}, f32[8,8,8,128]{3,2,1,0:T(8,128)S(1)}, u32[]{:S(2)}, u32[]{:S(2)}) %collective-permute-start.13) | collective-permute-done | bytes 262176 | tf_op jit(solution)/shard_map/ppermute | solution.py:736
  57.0 1.5 %shard_map.46 = (f32[2,34,2,2,8,128]{5,4,3,2,1,0:T(8,128)S(1)}, f32[2,34,2,2,8,128]{5,4,3,2,1,0:T(8,128)S(1)}, f32[34,2,2,8,128]{4,3,2,1,0:T(8,128)S(1)}, f32[2,...) custom-call(f32[16,8,8,128]{3,2,1,0:T(8,128)S(1)} %constant_dynamic-, ...), custom_call_target="tpu_custom_call" | custom-call | bytes 12000000 | tf_op jit(solution)/shard_map/pallas_call | solution.py:19
  58.6 1.9 %collective-permute-done.18.ftheirs = f32[16,8,8,128]{3,2,1,0:T(8,128)S(1)} collective-permute-done((f32[16,8,8,128]{3,2,1,0:T(8,128)S(1)}, f32[16,8,8,128]{3,2,1,0:T(8,128)S(1)}, u32[]{:S(2)}, u32[]{:S(2)}) %collective-permute-start.18) | collective-permute-done | bytes 524320 | tf_op jit(solution)/shard_map/ppermute | solution.py:736
  60.5 7.7 %shard_map.47 = (f32[10,4,8,128]{3,2,1,0:T(8,128)S(1)}, f32[2,4,4,128]{3,2,1,0:T(4,128)S(1)}) custom-call(f32[16,8,8,128]{3,2,1,0:T(8,128)S(1)} %pad_maximum_fusion.fmine, f32[16,8,8,128]{3,2,1,0:T(8,128)S(1)} %collective-permute-done.18.ftheirs, f32[2,34,2,2,8,128]{5,4,3,2,1,0:T(8,128)S(1)} %get-tuple-element.96.k, ...), custom_call_target="tpu_custom_call" | custom-call | bytes 24000000 | tf_op jit(solution)/shard_map/pallas_call | solution.py:19
  68.2 3.6 %shard_map.48 = (f32[8,8,1024]{2,1,0:T(8,128)}, f32[8,8,1024]{2,1,0:T(8,128)}) custom-call(f32[2,18,2,4,8,128]{5,4,3,2,1,0:T(8,128)S(1)} %get-tuple-element.64.k, f32[2,18,2,4,8,128]{5,4,3,2,1,0:T(8,128)S(1)} %get-tuple-element.65.g, f32[2,18,2,4,8,128]{5,4,3,2,1,0:T(8,128)S(1)} %get-tuple-element.66.fs, f32[8,2,4,8,128]{4,3,2,1,0:T(8,128)S(1)} %get-tuple-element.67.half, ...), custom_call_target="tpu_custom_call" | custom-call | bytes 18000000 | tf_op jit(solution)/shard_map/pallas_call | solution.py:19
  (28 shorter events, 0.4 us)
Async XLA Ops:
  0.6 1.0 %copy-start = (f32[8,8,1024]{2,1,0:T(8,128)S(1)}, f32[8,8,1024]{2,1,0:T(8,128)}, u32[]{:S(2)}) copy-start(f32[8,8,1024]{2,1,0:T(8,128)} %f_ref.1) | copy-start | bytes 786436
  1.6 0.9 %copy-start.1 = (f32[8,8,1024]{2,1,0:T(8,128)S(1)}, f32[8,8,1024]{2,1,0:T(8,128)}, u32[]{:S(2)}) copy-start(f32[8,8,1024]{2,1,0:T(8,128)} %k_ref.1) | copy-start | bytes 786436
  3.9 14.7 %collective-permute-start = (f32[16,2,4,4,128]{4,3,2,1,0:T(4,128)S(1)}, f32[16,2,4,4,128]{4,3,2,1,0:T(4,128)S(1)}, u32[]{:S(2)}, u32[]{:S(2)}) collective-permute-start(f32[16,2,4,4,128]{4,3,2,1,0:T(4,128)S(1)} %get-tuple-element.55), channel_id=1, source_target_pairs={{0,1},{2,3},{4,5},{6,7},{1,0},{3,2},{5,4},{7,6},{8,9},{10,11},{12,... | collective-permute-start | bytes 786440 | tf_op jit(solution)/shard_map/ppermute | solution.py:887
  6.9 11.7 %collective-permute-start.1 = (f32[16,2,4,4,128]{4,3,2,1,0:T(4,128)S(1)}, f32[16,2,4,4,128]{4,3,2,1,0:T(4,128)S(1)}, u32[]{:S(2)}, u32[]{:S(2)}) collective-permute-start(f32[16,2,4,4,128]{4,3,2,1,0:T(4,128)S(1)} %get-tuple-element.56), channel_id=1, source_target_pairs={{1,2},{3,4},{5,6},{2,1},{4,3},{6,5},{9,10},{11,12},{13,14},{10,9},... | collective-permute-start | bytes 786440 | tf_op jit(solution)/shard_map/ppermute | solution.py:887
  8.0 10.6 %collective-permute-start.2 = (f32[1,8,8,128]{3,2,1,0:T(8,128)S(1)}, f32[1,8,8,128]{3,2,1,0:T(8,128)S(1)}, u32[]{:S(2)}, u32[]{:S(2)}) collective-permute-start(f32[1,8,8,128]{3,2,1,0:T(8,128)S(1)} %bitcast.6), channel_id=1, source_target_pairs={{0,4},{1,5},{2,6},{3,7},{4,0},{5,1},{6,2},{7,3},{8,12},{9,13},{10,... | collective-permute-start | bytes 98312 | tf_op jit(solution)/shard_map/ppermute | solution.py:736
  12.3 10.7 %collective-permute-start.3 = (f32[8,4,16,128]{3,2,1,0:T(8,128)S(1)}, f32[8,4,16,128]{3,2,1,0:T(8,128)S(1)}, u32[]{:S(2)}, u32[]{:S(2)}) collective-permute-start(f32[8,4,16,128]{3,2,1,0:T(8,128)S(1)} %get-tuple-element.60), channel_id=1, source_target_pairs={{0,8},{16,24},{8,0},{24,16},{1,9},{17,25},{9,1},{25,17},{2,10},{18... | collective-permute-start | bytes 786440 | tf_op jit(solution)/shard_map/ppermute | solution.py:887
  12.3 10.7 %collective-permute-start.4 = (f32[8,4,16,128]{3,2,1,0:T(8,128)S(1)}, f32[8,4,16,128]{3,2,1,0:T(8,128)S(1)}, u32[]{:S(2)}, u32[]{:S(2)}) collective-permute-start(f32[8,4,16,128]{3,2,1,0:T(8,128)S(1)} %get-tuple-element.61), channel_id=1, source_target_pairs={{8,16},{16,8},{9,17},{17,9},{10,18},{18,10},{11,19},{19,11},{12,20... | collective-permute-start | bytes 786440 | tf_op jit(solution)/shard_map/ppermute | solution.py:887
  18.7 4.3 %collective-permute-start.7 = (f32[2,8,8,128]{3,2,1,0:T(8,128)S(1)}, f32[2,8,8,128]{3,2,1,0:T(8,128)S(1)}, u32[]{:S(2)}, u32[]{:S(2)}) collective-permute-start(f32[2,8,8,128]{3,2,1,0:T(8,128)S(1)} %pad_maximum_fusion.5), channel_id=1, source_target_pairs={{0,2},{1,3},{2,0},{3,1},{4,6},{5,7},{6,4},{7,5},{8,10},{9,11},{10,... | collective-permute-start | bytes 196616 | tf_op jit(solution)/shard_map/ppermute | solution.py:736
  20.9 2.2 %collective-permute-start.5 = (f32[224,128]{1,0:T(8,128)S(1)}, f32[224,128]{1,0:T(8,128)S(1)}, u32[]{:S(2)}, u32[]{:S(2)}) collective-permute-start(f32[224,128]{1,0:T(8,128)S(1)} %get-tuple-element.62), channel_id=1, source_target_pairs={{0,8},{16,24},{8,0},{24,16},{1,9},{17,25},{9,1},{25,17},{2,10},{18... | collective-permute-start | bytes 344072 | tf_op jit(solution)/shard_map/ppermute | solution.py:887
  21.0 2.1 %collective-permute-start.6 = (f32[224,128]{1,0:T(8,128)S(1)}, f32[224,128]{1,0:T(8,128)S(1)}, u32[]{:S(2)}, u32[]{:S(2)}) collective-permute-start(f32[224,128]{1,0:T(8,128)S(1)} %get-tuple-element.63), channel_id=1, source_target_pairs={{8,16},{16,8},{9,17},{17,9},{10,18},{18,10},{11,19},{19,11},{12,20... | collective-permute-start | bytes 344072 | tf_op jit(solution)/shard_map/ppermute | solution.py:887
  25.8 4.9 %collective-permute-start.8 = (f32[224,128]{1,0:T(8,128)S(1)}, f32[224,128]{1,0:T(8,128)S(1)}, u32[]{:S(2)}, u32[]{:S(2)}) collective-permute-start(f32[224,128]{1,0:T(8,128)S(1)} %get-tuple-element.73), channel_id=1, source_target_pairs={{0,1},{2,3},{4,5},{6,7},{1,0},{3,2},{5,4},{7,6},{8,9},{10,11},{12,... | collective-permute-start | bytes 344072 | tf_op jit(solution)/shard_map/ppermute | solution.py:887
  27.7 6.5 %collective-permute-start.10 = (f32[4,8,8,128]{3,2,1,0:T(8,128)S(1)}, f32[4,8,8,128]{3,2,1,0:T(8,128)S(1)}, u32[]{:S(2)}, u32[]{:S(2)}) collective-permute-start(f32[4,8,8,128]{3,2,1,0:T(8,128)S(1)} %pad_maximum_fusion.3), channel_id=1, source_target_pairs={{0,1},{1,0},{2,3},{3,2},{4,5},{5,4},{6,7},{7,6},{8,9},{9,8},{10,11... | collective-permute-start | bytes 393224 | tf_op jit(solution)/shard_map/ppermute | solution.py:736
  27.9 9.4 %collective-permute-start.11 = (f32[160,128]{1,0:T(8,128)S(1)}, f32[160,128]{1,0:T(8,128)S(1)}, u32[]{:S(2)}, u32[]{:S(2)}) collective-permute-start(f32[160,128]{1,0:T(8,128)S(1)} %get-tuple-element.75), channel_id=1, source_target_pairs={{1,2},{3,4},{5,6},{2,1},{4,3},{6,5},{9,10},{11,12},{13,14},{10,9},... | collective-permute-start | bytes 245768 | tf_op jit(solution)/shard_map/ppermute | solution.py:887
  30.7 6.6 %collective-permute-start.9 = (f32[2,8,8,128]{3,2,1,0:T(8,128)S(1)}, f32[2,8,8,128]{3,2,1,0:T(8,128)S(1)}, u32[]{:S(2)}, u32[]{:S(2)}) collective-permute-start(f32[2,8,8,128]{3,2,1,0:T(8,128)S(1)} %pad_maximum_fusion.6), channel_id=1, source_target_pairs={{0,4},{1,5},{2,6},{3,7},{4,0},{5,1},{6,2},{7,3},{8,12},{9,13},{10,... | collective-permute-start | bytes 196616 | tf_op jit(solution)/shard_map/ppermute | solution.py:736
  37.3 10.4 %collective-permute-start.16 = (f32[8,8,8,128]{3,2,1,0:T(8,128)S(1)}, f32[8,8,8,128]{3,2,1,0:T(8,128)S(1)}, u32[]{:S(2)}, u32[]{:S(2)}) collective-permute-start(f32[8,8,8,128]{3,2,1,0:T(8,128)S(1)} %pad_maximum_fusion.1), channel_id=1, source_target_pairs={{0,16},{1,17},{2,18},{3,19},{4,20},{5,21},{6,22},{7,23},{8,24},{9,... | collective-permute-start | bytes 786440 | tf_op jit(solution)/shard_map/ppermute | solution.py:736
  41.5 6.7 %collective-permute-start.12 = (f32[4,8,8,128]{3,2,1,0:T(8,128)S(1)}, f32[4,8,8,128]{3,2,1,0:T(8,128)S(1)}, u32[]{:S(2)}, u32[]{:S(2)}) collective-permute-start(f32[4,8,8,128]{3,2,1,0:T(8,128)S(1)} %pad_maximum_fusion.4), channel_id=1, source_target_pairs={{0,2},{1,3},{2,0},{3,1},{4,6},{5,7},{6,4},{7,5},{8,10},{9,11},{10,... | collective-permute-start | bytes 393224 | tf_op jit(solution)/shard_map/ppermute | solution.py:736
  47.7 9.3 %collective-permute-start.17 = (f32[16,8,8,128]{3,2,1,0:T(8,128)S(1)}, f32[16,8,8,128]{3,2,1,0:T(8,128)S(1)}, u32[]{:S(2)}, u32[]{:S(2)}) collective-permute-start(f32[16,8,8,128]{3,2,1,0:T(8,128)S(1)} %constant_dynamic-update-slice_fusion.kmine), channel_id=1, source_target_pairs={{0,8},{1,9},{2,10},{3,11},{4,12},{5,13},{6,14},{7,15},{8,0},{9,1},... | collective-permute-start | bytes 1572872 | tf_op jit(solution)/shard_map/ppermute | solution.py:736
  48.2 8.7 %collective-permute-start.13 = (f32[8,8,8,128]{3,2,1,0:T(8,128)S(1)}, f32[8,8,8,128]{3,2,1,0:T(8,128)S(1)}, u32[]{:S(2)}, u32[]{:S(2)}) collective-permute-start(f32[8,8,8,128]{3,2,1,0:T(8,128)S(1)} %pad_maximum_fusion.2), channel_id=1, source_target_pairs={{0,16},{1,17},{2,18},{3,19},{4,20},{5,21},{6,22},{7,23},{8,24},{9,... | collective-permute-start | bytes 786440 | tf_op jit(solution)/shard_map/ppermute | solution.py:736
  48.6 9.9 %collective-permute-start.14 = (f32[240,128]{1,0:T(8,128)S(1)}, f32[240,128]{1,0:T(8,128)S(1)}, u32[]{:S(2)}, u32[]{:S(2)}) collective-permute-start(f32[240,128]{1,0:T(8,128)S(1)} %get-tuple-element.82), channel_id=1, source_target_pairs={{0,8},{16,24},{8,0},{24,16},{1,9},{17,25},{9,1},{25,17},{2,10},{18... | collective-permute-start | bytes 368648 | tf_op jit(solution)/shard_map/ppermute | solution.py:887
  48.8 9.7 %collective-permute-start.15 = (f32[240,128]{1,0:T(8,128)S(1)}, f32[240,128]{1,0:T(8,128)S(1)}, u32[]{:S(2)}, u32[]{:S(2)}) collective-permute-start(f32[240,128]{1,0:T(8,128)S(1)} %get-tuple-element.83), channel_id=1, source_target_pairs={{8,16},{16,8},{9,17},{17,9},{10,18},{18,10},{11,19},{19,11},{12,20... | collective-permute-start | bytes 368648 | tf_op jit(solution)/shard_map/ppermute | solution.py:887
  58.5 2.0 %collective-permute-start.18 = (f32[16,8,8,128]{3,2,1,0:T(8,128)S(1)}, f32[16,8,8,128]{3,2,1,0:T(8,128)S(1)}, u32[]{:S(2)}, u32[]{:S(2)}) collective-permute-start(f32[16,8,8,128]{3,2,1,0:T(8,128)S(1)} %pad_maximum_fusion.fmine), channel_id=1, source_target_pairs={{0,8},{1,9},{2,10},{3,11},{4,12},{5,13},{6,14},{7,15},{8,0},{9,1},... | collective-permute-start | bytes 1572872 | tf_op jit(solution)/shard_map/ppermute | solution.py:736
